TPU v7x, 256 devices: a whole 4x4x8 slice. The times are simulated.
256 devices in a mesh: slab: 16 (over z_lo, x, core), grp: 16 (over y, z_hi).
Axes of the slice: x: 4, y: 4, z: 8 (z_hi: 4, z_lo: 2; z = z_hi * 2 + z_lo), core: 2. Of those that a mesh axis runs over, the one named last changes fastest.
Arguments:
- vectors: bfloat16 [4096, 3072], P(('slab', 'grp')), may hold values from -6 to 6
- tiles: bfloat16 [32, 36864], replicated, may hold values from -0.09375 to 0.09375
- near_src: int32 [4096, 20], P(('slab', 'grp')), may hold values from 0 to 4095, as said below
- near_type: int32 [4096, 20], P(('slab', 'grp')), may hold values from 0 to 31, as said below
- near_count: int32 [4096], P(('slab', 'grp')), may hold values from 10 to 20
- bases: bfloat16 [4096, 6144], P(('slab', 'grp')), may hold values from -0.4375 to 0.4375
- far_src: int32 [4096, 32], P(('slab', 'grp')), may hold values from 0 to 4095, as said below
- coupling: bfloat16 [4096, 32, 1024], P(('slab', 'grp')), may hold values from -0.1875 to 0.1875
Outputs:
- first: bfloat16 [4096, 3072], P(('slab', 'grp'))
- second: bfloat16 [4096, 3072], P(('slab', 'grp'))
Inputs may be any that keep to these rules, and one draw needn't show every extreme that they name: `near_src`: each source block is one of the same device's blocks, one of the last 8 blocks of the device with the same grp index in the previous slab, or one of the first 8 blocks of that device in the next slab; slabs are cyclic. `near_type`: the tile types of one block's slots are all different. `far_src`: each partner block lies in the same slab as the block.
All inputs are finite; a program needn't handle non-finite values.
Results may differ from a plain program's by a relative error of at most 0.0065.
Values may be sent and summed in bfloat16 or wider, within the bound.
No kernel may reach another device: no remote copies, remote signals or barrier semaphores. Data moves between devices by JAX's collectives and lax.ppermute only.
A program may use at most 64 MiB of HBM per device.

v0:
```python
import jax
import jax.numpy as jnp
from jax import lax
from jax.sharding import PartitionSpec as P

TILE = 192
RHS = 16
RANK = 32


def padded(array, sides, width):
    for axis, dim in sides:
        peers, length = (lax.axis_size(axis), array.shape[dim])
        up = [(i, (i + 1) % peers) for i in range(peers)]
        down = [(j, i) for i, j in up]
        last = lax.slice_in_dim(array, length - width, length, axis=dim)
        initial = lax.slice_in_dim(array, 0, width, axis=dim)
        before = lax.ppermute(last, axis, up)
        after = lax.ppermute(initial, axis, down)
        array = jnp.concatenate([before, array, after], axis=dim)
    return array


def per_device(vectors, tiles, near_src, near_type, near_count, bases, far_src, coupling):
    block_count = vectors.shape[0]
    rhs_count = RHS
    tile_width = TILE
    rank_width = RANK
    type_count = tiles.shape[0]
    slot_count = near_src.shape[1]
    partner_count = far_src.shape[1]
    slab_index = lax.axis_index("slab")
    slab_count = lax.axis_size("slab")
    slab_blocks = block_count * lax.axis_size("grp")
    table = tiles.reshape(type_count, tile_width, tile_width)
    basis = bases.reshape(block_count, rank_width, tile_width)
    src_slab = near_src // slab_blocks
    src_local = near_src % block_count
    slab_step = (src_slab - slab_index) % slab_count
    positions = jnp.where(
        slab_step == 0,
        block_count + src_local,
        jnp.where(slab_step == 1, 2 * block_count + src_local, src_local),
    )
    slot_ids = jnp.arange(slot_count, dtype=jnp.int32)
    live_slot = slot_ids[None, :] < near_count[:, None]
    type_ids = jnp.arange(type_count, dtype=jnp.int32)
    selector = ((near_type[:, :, None] == type_ids[None, None, :]) & live_slot[:, :, None]).astype(
        jnp.bfloat16
    )
    far_local = far_src % slab_blocks
    couple = coupling.reshape(block_count, partner_count, rank_width, rank_width)

    def apply_operator(field):
        extended = padded(field, (("slab", 0),), block_count)
        sources = jnp.take(extended, positions, axis=0).reshape(
            block_count, slot_count, rhs_count, tile_width
        )
        placed = jnp.einsum(
            "ikt,ikhc->ithc", selector, sources, preferred_element_type=jnp.bfloat16
        )
        near_term = lax.dot_general(
            placed, table, (((1, 3), (0, 2)), ((), ())), preferred_element_type=jnp.float32
        )
        field_rows = field.reshape(block_count, rhs_count, tile_width)
        coefficients = jnp.einsum(
            "ipc,ihc->ihp", basis, field_rows, preferred_element_type=jnp.float32
        )
        coefficients = coefficients.astype(jnp.bfloat16).reshape(
            block_count, rhs_count * rank_width
        )
        every_coef = lax.all_gather(coefficients, "grp", axis=0, tiled=True)
        picked = jnp.take(every_coef, far_local, axis=0).reshape(
            block_count, partner_count, rhs_count, rank_width
        )
        far_mix = jnp.einsum("ikpq,ikhq->ihp", couple, picked, preferred_element_type=jnp.float32)
        far_term = jnp.einsum(
            "ihp,ipc->ihc", far_mix.astype(jnp.bfloat16), basis, preferred_element_type=jnp.float32
        )
        return (
            (near_term + far_term).astype(jnp.bfloat16).reshape(block_count, rhs_count * tile_width)
        )

    first = apply_operator(vectors)
    second = apply_operator(first)
    return (first, second)


def solution(mesh):
    in_specs = (
        P(("slab", "grp"), None),
        P(),
        P(("slab", "grp"), None),
        P(("slab", "grp"), None),
        P(("slab", "grp")),
        P(("slab", "grp"), None),
        P(("slab", "grp"), None),
        P(("slab", "grp"), None, None),
    )
    out_specs = (P(("slab", "grp"), None), P(("slab", "grp"), None))
    return jax.shard_map(
        per_device, mesh=mesh, in_specs=in_specs, out_specs=out_specs, check_vma=False
    )
```

profile of v0, /device:TPU:32, one launch (start us, length us, event | category | flops | bytes accessed | tf_op | source)
XLA Modules:
  0.0 168.1 jit_solution(6637559471706352046)
XLA Ops:
  0.7 3.8 %collective-permute-start.1 = (bf16[16,3072]{1,0:T(8,128)(2,1)}, bf16[16,3072]{1,0:T(8,128)(2,1)S(1)}, u32[]{:S(2)}, u32[]{:S(2)}) collective-permute-start(bf16[16,3072]{1,0:T(8,128)(2,1)} %param.12), channel_id=1, source_target_pairs={{16,0},{32,16},{48,32},{64,48},{80,64},{96,80},{112,96},{128,112},... | collective-permute-start | bytes 294920 | tf_op jit(solution)/shard_map/ppermute | solution.py:19
  7.3 47.2 %all_gather.6 = bf16[256,512]{1,0:T(8,128)(2,1)S(1)} all-gather(bf16[16,512]{1,0:T(8,128)(2,1)S(1)} %reshape.76), channel_id=1, replica_groups=mesh['slab'=16,'grp'=16] {'grp'}, dimensions={0}, use_global_device_ids=true | all-gather | bytes 278528 | tf_op jit(solution)/shard_map/all_gather | solution.py:72
  55.3 2.0 %gather_fusion.1 = bf16[512,512]{1,0:T(8,128)(2,1)S(1)} fusion(bf16[256,512]{1,0:T(8,128)(2,1)S(1)} %all_gather.6, s32[1024]{0:T(1024)S(1)} %pad_clamp_fusion), kind=kCustom, calls=%fused_computation.1.clone | custom fusion | bytes 1050624 | tf_op jit(solution)/shard_map/jit(_take)/gather | solution.py:73
  58.2 3.6 %reshape.77 = bf16[16,32,16,32]{3,2,1,0:T(8,128)(2,1)} reshape(bf16[16,32,512]{2,1,0:T(8,128)(2,1)} %broadcast_select_fusion.3) | data formatting | bytes 1048576 | tf_op jit(solution)/shard_map/reshape | solution.py:73
  62.0 4.5 %reshape.141 = bf16[32,192,192,1]{2,1,0,3:T(8,128)(2,1)} reshape(bf16[32,36864]{1,0:T(8,128)(2,1)S(1)} %copy-done.4) | data formatting | bytes 4718592 | tf_op jit(solution)/shard_map/reshape | solution.py:35
  66.5 6.3 %reshape.78 = bf16[16,32,32,32]{3,2,1,0:T(8,128)(2,1)} reshape(bf16[16,32,1024]{2,1,0:T(8,128)(2,1)} %param.19) | data formatting | bytes 2097152 | tf_op jit(solution)/shard_map/reshape | solution.py:52
  72.8 2.9 %gather_fusion = bf16[320,3072]{1,0:T(8,128)(2,1)S(1)} fusion(bf16[48,3072]{1,0:T(8,128)(2,1)S(1)} %pad_maximum_fusion, s32[1024]{0:T(1024)S(1)} %pad_clamp_fusion.1), kind=kCustom, calls=%fused_computation.clone | custom fusion | bytes 3933440 | tf_op jit(solution)/shard_map/jit(_take)/gather | solution.py:56
  75.7 2.1 %reshape.127 = bf16[16,20,3072]{2,1,0:T(8,128)(2,1)} reshape(bf16[320,3072]{1,0:T(8,128)(2,1)S(1)} %gather_fusion) | data formatting | bytes 3932160 | tf_op jit(solution)/shard_map/jit(_take)/gather | solution.py:56
  77.8 3.4 %broadcast_select_fusion.1 = bf16[16,20,3072]{2,1,0:T(8,128)(2,1)} fusion(bf16[16,20,3072]{2,1,0:T(8,128)(2,1)} %reshape.127, pred[16,20]{1,0:T(8,128)(4,1)S(1)} %get-tuple-element.6), kind=kLoop, calls=%fused_computation.13 | loop fusion | flops 983040 | bytes 3932480 | tf_op jit(solution)/shard_map/jit(_take)/select_n | solution.py:56
  81.2 4.7 %reshape.146 = bf16[16,20,16,192]{3,2,1,0:T(8,128)(2,1)S(1)} reshape(bf16[16,20,3072]{2,1,0:T(8,128)(2,1)} %broadcast_select_fusion.1) | data formatting | bytes 3932160 | tf_op jit(solution)/shard_map/reshape | solution.py:56
  86.0 1.7 %fusion.6 = bf16[16,32,16,192]{3,1,2,0:T(8,128)(2,1)S(1)} fusion(bf16[16,20,16,192]{3,2,1,0:T(8,128)(2,1)S(1)} %reshape.146, s32[16,20]{1,0:T(8,128)S(1)} %copy-done.7, pred[16,20]{1,0:T(8,128)(4,1)S(1)} %iota_compare_fusion.1), kind=kOutput, calls=%fused_computation.10 | convolution fusion | flops 62935040 | bytes 5113408 | tf_op jit(solution)/shard_map/ikt,ikhc->ithc/dot_general | solution.py:59
  87.8 4.6 %fusion.8 = f32[16,16,192]{2,1,0:T(8,128)S(1)} fusion(bf16[32,192,192,1]{2,1,0,3:T(8,128)(2,1)S(1)} %copy-done.2, bf16[16,32,16,192]{3,1,2,0:T(8,128)(2,1)S(1)} %fusion.6), kind=kOutput, calls=%fused_computation.16 | convolution fusion | flops 603979776 | bytes 5701632 | tf_op jit(solution)/shard_map/dot_general | solution.py:62
  92.5 3.5 %fusion.14 = bf16[16,16,192]{2,1,0:T(8,128)(2,1)S(1)} fusion(f32[16,16,192]{2,1,0:T(8,128)S(1)} %fusion.8, bf16[16,32,192]{2,1,0:T(8,128)(2,1)S(1)} %reshape.75, bf16[16,32,16,32]{3,2,1,0:T(8,128)(2,1)S(1)} %copy-done, bf16[16,32,32,32]{3,2,1,0:T(8,128)(2,1)} %reshape.78), kind=kOutput, calls=%fused_computation.18 | convolution fusion | flops 20029440 | bytes 2064384 | tf_op jit(solution)/shard_map/ihp,ipc->ihc/dot_general | solution.py:77
  96.3 3.8 %collective-permute-start.3 = (bf16[16,3072]{1,0:T(8,128)(2,1)S(1)}, bf16[16,3072]{1,0:T(8,128)(2,1)S(1)}, u32[]{:S(2)}, u32[]{:S(2)}) collective-permute-start(bf16[16,3072]{1,0:T(8,128)(2,1)S(1)} %reshape.79), channel_id=1, source_target_pairs={{16,0},{32,16},{48,32},{64,48},{80,64},{96,80},{112,96},{128,112},... | collective-permute-start | bytes 294920 | tf_op jit(solution)/shard_map/ppermute | solution.py:19
  100.4 39.6 %all_gather.7 = bf16[256,512]{1,0:T(8,128)(2,1)S(1)} all-gather(bf16[16,512]{1,0:T(8,128)(2,1)S(1)} %reshape.81), channel_id=1, replica_groups=mesh['slab'=16,'grp'=16] {'grp'}, dimensions={0}, use_global_device_ids=true | all-gather | bytes 278528 | tf_op jit(solution)/shard_map/all_gather | solution.py:72
  140.0 2.0 %gather_fusion.3 = bf16[512,512]{1,0:T(8,128)(2,1)S(1)} fusion(bf16[256,512]{1,0:T(8,128)(2,1)S(1)} %all_gather.7, s32[1024]{0:T(1024)S(1)} %pad_clamp_fusion), kind=kCustom, calls=%fused_computation.3.clone | custom fusion | bytes 1050624 | tf_op jit(solution)/shard_map/jit(_take)/gather | solution.py:73
  142.1 2.2 %reshape.82 = bf16[16,32,16,32]{3,2,1,0:T(8,128)(2,1)} reshape(bf16[16,32,512]{2,1,0:T(8,128)(2,1)S(1)} %broadcast_select_fusion.2) | data formatting | bytes 1048576 | tf_op jit(solution)/shard_map/reshape | solution.py:73
  144.3 2.9 %gather_fusion.2 = bf16[320,3072]{1,0:T(8,128)(2,1)S(1)} fusion(bf16[48,3072]{1,0:T(8,128)(2,1)S(1)} %pad_maximum_fusion.1, s32[1024]{0:T(1024)S(1)} %pad_clamp_fusion.1), kind=kCustom, calls=%fused_computation.2.clone | custom fusion | bytes 3933440 | tf_op jit(solution)/shard_map/jit(_take)/gather | solution.py:56
  147.2 2.1 %reshape.135 = bf16[16,20,3072]{2,1,0:T(8,128)(2,1)} reshape(bf16[320,3072]{1,0:T(8,128)(2,1)S(1)} %gather_fusion.2) | data formatting | bytes 3932160 | tf_op jit(solution)/shard_map/jit(_take)/gather | solution.py:56
  149.4 3.4 %broadcast_select_fusion = bf16[16,20,3072]{2,1,0:T(8,128)(2,1)} fusion(bf16[16,20,3072]{2,1,0:T(8,128)(2,1)} %reshape.135, pred[16,20]{1,0:T(8,128)(4,1)S(1)} %get-tuple-element.6), kind=kLoop, calls=%fused_computation.12 | loop fusion | flops 983040 | bytes 3932480 | tf_op jit(solution)/shard_map/jit(_take)/select_n | solution.py:56
  152.8 4.5 %reshape.148 = bf16[16,20,16,192]{3,2,1,0:T(8,128)(2,1)S(1)} reshape(bf16[16,20,3072]{2,1,0:T(8,128)(2,1)} %broadcast_select_fusion) | data formatting | bytes 3932160 | tf_op jit(solution)/shard_map/reshape | solution.py:56
  157.3 1.7 %fusion.4 = bf16[16,32,16,192]{3,1,2,0:T(8,128)(2,1)S(1)} fusion(bf16[16,20,16,192]{3,2,1,0:T(8,128)(2,1)S(1)} %reshape.148, s32[16,20]{1,0:T(8,128)S(1)} %copy-done.7, pred[16,20]{1,0:T(8,128)(4,1)S(1)} %iota_compare_fusion.1), kind=kOutput, calls=%fused_computation.8 | convolution fusion | flops 62935040 | bytes 5113408 | tf_op jit(solution)/shard_map/ikt,ikhc->ithc/dot_general | solution.py:59
  159.2 4.6 %fusion.11 = f32[16,16,192]{2,1,0:T(8,128)S(1)} fusion(bf16[32,192,192,1]{2,1,0,3:T(8,128)(2,1)S(1)} %copy-done.3, bf16[16,32,16,192]{3,1,2,0:T(8,128)(2,1)S(1)} %fusion.4), kind=kOutput, calls=%fused_computation.17 | convolution fusion | flops 603979776 | bytes 5701632 | tf_op jit(solution)/shard_map/dot_general | solution.py:62
  163.8 3.5 %fusion.15 = bf16[16,16,192]{2,1,0:T(8,128)(2,1)S(1)} fusion(f32[16,16,192]{2,1,0:T(8,128)S(1)} %fusion.11, bf16[16,32,192]{2,1,0:T(8,128)(2,1)S(1)} %reshape.75, bf16[16,32,16,32]{3,2,1,0:T(8,128)(2,1)S(1)} %copy-done.1, bf16[16,32,32,32]{3,2,1,0:T(8,128)(2,1)} %reshape.78), kind=kOutput, calls=%fused_computation.19 | convolution fusion | flops 20029440 | bytes 2064384 | tf_op jit(solution)/shard_map/ihp,ipc->ihc/dot_general | solution.py:77
  (45 shorter events, 6.7 us)
Async XLA Ops:
  0.6 72.1 %collective-permute-start = (bf16[16,3072]{1,0:T(8,128)(2,1)}, bf16[16,3072]{1,0:T(8,128)(2,1)S(1)}, u32[]{:S(2)}, u32[]{:S(2)}) collective-permute-start(bf16[16,3072]{1,0:T(8,128)(2,1)} %param.12), channel_id=1, source_target_pairs={{0,16},{16,32},{32,48},{48,64},{64,80},{80,96},{96,112},{112,128},... | collective-permute-start | bytes 294920 | tf_op jit(solution)/shard_map/ppermute | solution.py:18
  0.7 72.1 %collective-permute-start.1 = (bf16[16,3072]{1,0:T(8,128)(2,1)}, bf16[16,3072]{1,0:T(8,128)(2,1)S(1)}, u32[]{:S(2)}, u32[]{:S(2)}) collective-permute-start(bf16[16,3072]{1,0:T(8,128)(2,1)} %param.12), channel_id=1, source_target_pairs={{16,0},{32,16},{48,32},{64,48},{80,64},{96,80},{112,96},{128,112},... | collective-permute-start | bytes 294920 | tf_op jit(solution)/shard_map/ppermute | solution.py:19
  57.2 4.5 %copy-start.8 = (s32[16,20]{1,0:T(8,128)S(1)}, s32[16,20]{1,0:T(8,128)}, u32[]{:S(2)}) copy-start(s32[16,20]{1,0:T(8,128)} %param.14) | copy-start | bytes 3844
  57.2 4.6 %copy-start.9 = (s32[16]{0:T(128)S(1)}, s32[16]{0:T(128)}, u32[]{:S(2)}) copy-start(s32[16]{0:T(128)} %param.16) | copy-start | bytes 196
  57.3 4.7 %copy-start.4 = (bf16[32,36864]{1,0:T(8,128)(2,1)S(1)}, bf16[32,36864]{1,0:T(8,128)(2,1)}, u32[]{:S(2)}) copy-start(bf16[32,36864]{1,0:T(8,128)(2,1)} %param.13) | copy-start | bytes 7077892
  66.5 6.3 %copy-start.5 = (bf16[16,3072]{1,0:T(8,128)(2,1)S(1)}, bf16[16,3072]{1,0:T(8,128)(2,1)}, u32[]{:S(2)}) copy-start(bf16[16,3072]{1,0:T(8,128)(2,1)} %param.12) | copy-start | bytes 294916
  81.2 4.7 %copy-start.7 = (s32[16,20]{1,0:T(8,128)S(1)}, s32[16,20]{1,0:T(8,128)}, u32[]{:S(2)}) copy-start(s32[16,20]{1,0:T(8,128)} %param.15) | copy-start | bytes 3844
  86.0 1.9 %copy-start.2 = (bf16[32,192,192,1]{2,1,0,3:T(8,128)(2,1)S(1)}, bf16[32,192,192,1]{2,1,0,3:T(8,128)(2,1)}, u32[]{:S(2)}) copy-start(bf16[32,192,192,1]{2,1,0,3:T(8,128)(2,1)} %reshape.141) | copy-start | bytes 7077892
  87.8 4.6 %copy-start = (bf16[16,32,16,32]{3,2,1,0:T(8,128)(2,1)S(1)}, bf16[16,32,16,32]{3,2,1,0:T(8,128)(2,1)}, u32[]{:S(2)}) copy-start(bf16[16,32,16,32]{3,2,1,0:T(8,128)(2,1)} %reshape.77) | copy-start | bytes 1572868
  96.2 48.2 %copy-start.6 = (bf16[16,3072]{1,0:T(8,128)(2,1)}, bf16[16,3072]{1,0:T(8,128)(2,1)S(1)}, u32[]{:S(2)}) copy-start(bf16[16,3072]{1,0:T(8,128)(2,1)S(1)} %reshape.79) | copy-start | bytes 294916
  96.2 48.1 %collective-permute-start.2 = (bf16[16,3072]{1,0:T(8,128)(2,1)S(1)}, bf16[16,3072]{1,0:T(8,128)(2,1)S(1)}, u32[]{:S(2)}, u32[]{:S(2)}) collective-permute-start(bf16[16,3072]{1,0:T(8,128)(2,1)S(1)} %reshape.79), channel_id=1, source_target_pairs={{0,16},{16,32},{32,48},{48,64},{64,80},{80,96},{96,112},{112,128},... | collective-permute-start | bytes 294920 | tf_op jit(solution)/shard_map/ppermute | solution.py:18
  96.3 48.1 %collective-permute-start.3 = (bf16[16,3072]{1,0:T(8,128)(2,1)S(1)}, bf16[16,3072]{1,0:T(8,128)(2,1)S(1)}, u32[]{:S(2)}, u32[]{:S(2)}) collective-permute-start(bf16[16,3072]{1,0:T(8,128)(2,1)S(1)} %reshape.79), channel_id=1, source_target_pairs={{16,0},{32,16},{48,32},{64,48},{80,64},{96,80},{112,96},{128,112},... | collective-permute-start | bytes 294920 | tf_op jit(solution)/shard_map/ppermute | solution.py:19
  157.3 1.9 %copy-start.3 = (bf16[32,192,192,1]{2,1,0,3:T(8,128)(2,1)S(1)}, bf16[32,192,192,1]{2,1,0,3:T(8,128)(2,1)}, u32[]{:S(2)}) copy-start(bf16[32,192,192,1]{2,1,0,3:T(8,128)(2,1)} %reshape.141) | copy-start | bytes 7077892
  159.2 4.6 %copy-start.1 = (bf16[16,32,16,32]{3,2,1,0:T(8,128)(2,1)S(1)}, bf16[16,32,16,32]{3,2,1,0:T(8,128)(2,1)}, u32[]{:S(2)}) copy-start(bf16[16,32,16,32]{3,2,1,0:T(8,128)(2,1)} %reshape.82) | copy-start | bytes 1572868
where the time goes:
time: 169 us; the launch traced here: 168 us
  blocking collectives  86.8 us (51%)
  local copies, waits for them, and re-layouts  43.8 us (26%)
  matrix products  20 us (12%)
  other arithmetic  8.75 us (5%)
  starting transfers between devices  7.85 us (5%)
    all_gather x2, blocking collectives, apply_operator(): every_coef = lax.all_gather(coefficients, 'grp', axis=0, tiled=True)  86.8 us
    gather x4, local copies, waits for them, and re-layouts, apply_operator(): jnp.take(extended, positions, axis=0)  9.99 us
    dot_general x2, matrix products, apply_operator(): lax.dot_general(placed, table, (((1, 3), (0, 2)), ((), ())), preferred_el...  9.22 us
    reshape x2, local copies, waits for them, and re-layouts, apply_operator(): jnp.take(extended, positions, axis=0)  9.18 us
    ppermute x2, starting transfers between devices, padded(): after = lax.ppermute(initial, axis, down)  7.68 us
    dot_general x2, matrix products, apply_operator(): jnp.einsum('ihp,ipc->ihc', far_mix.astype(jnp.bfloat16), basis, preferred...  7.01 us
    select_n x2, other arithmetic, apply_operator(): jnp.take(extended, positions, axis=0)  6.82 us
    reshape x1, local copies, waits for them, and re-layouts, per_device(): coupling.reshape(block_count, partner_count, rank_width, rank_width)  6.26 us
  transfers between devices with their start and end apart: 4, of which 0 were waited for; matrix products, arithmetic and copies ran while one was open for 15% of the time, Pallas kernels for 0%

commit v1 on v0

v1 whole, which is shorter than its diff:
```python
import functools

import jax
import jax.numpy as jnp
from jax import lax
from jax.experimental import pallas as pl
from jax.experimental.pallas import tpu as pltpu
from jax.sharding import PartitionSpec as P

TILE = 192
RHS = 16
RANK = 32
RIM = 8
LANES = 128
WIDE = 256
GROUP = 8

VMEM = pl.BlockSpec(memory_space=pltpu.VMEM)
SMEM = pl.BlockSpec(memory_space=pltpu.SMEM)
F32 = jnp.float32
BF16 = jnp.bfloat16
NT = (((1,), (1,)), ((), ()))
NN = (((1,), (0,)), ((), ()))


def params():
    return pltpu.CompilerParams(vmem_limit_bytes=40 * 1024 * 1024)


def project(field, basis_ref, blocks):
    rows, cols = GROUP * RHS, GROUP * RANK
    lane = lax.broadcasted_iota(jnp.int32, (RHS, LANES), 1) // RANK
    packed = []
    for g in range(blocks // GROUP):
        cross = lax.dot_general(
            field[g * rows : (g + 1) * rows, :],
            basis_ref[g * cols : (g + 1) * cols, :],
            NT,
            preferred_element_type=F32,
        )
        for half in range(GROUP // 4):
            out = None
            for j in range(4):
                at = (half * 4 + j) * RHS
                part = cross[at : at + RHS, half * LANES : (half + 1) * LANES]
                out = part if out is None else jnp.where(lane == j, part, out)
            packed.append(out)
    return jnp.concatenate(packed, axis=0).astype(BF16)


def halves(pair):
    low = lax.broadcasted_iota(jnp.int32, (pair.shape[0], LANES), 1) < LANES // 2
    one, two, three = (pair[:, j * LANES : (j + 1) * LANES] for j in range(3))
    two_turned, three_turned = (pltpu.roll(x, LANES // 2, 1) for x in (two, three))
    return (
        (one, jnp.where(low, two, 0.0)),
        (jnp.where(low, two_turned, three_turned), jnp.where(low, three_turned, 0.0)),
    )


def spread(source_ref, scratch, rows, count, stride):
    size = rows * stride
    for j in range(0, count, 2):
        pair = source_ref[:, j * TILE : (j + 2) * TILE].astype(F32)
        for k, parts in enumerate(halves(pair)):
            for side, part in enumerate(parts):
                scratch[pl.ds(side * size + j + k, rows, stride=stride), :] = part


def join(scratch, start, count, size):
    return jnp.concatenate(
        [scratch[side * size + start : side * size + start + count, :].astype(BF16) for side in range(2)],
        axis=1,
    )


def opening_kernel(v_ref, b_ref, lo_ref, hi_ref, basis_ref, coef_ref, f_s, b_s):
    blocks = v_ref.shape[0]
    rows, ranks = blocks * RHS, blocks * RANK
    spread(v_ref, f_s, blocks, RHS, RHS)
    spread(b_ref, b_s, blocks, RANK, RANK)
    field = join(f_s, 0, rows, rows)
    rim = RIM * RHS
    lo_ref[...] = field[:rim]
    hi_ref[...] = field[rim:]
    basis_ref[...] = join(b_s, 0, ranks, ranks)
    packed = project(field, basis_ref, blocks)
    for j in range(coef_ref.shape[0]):
        coef_ref[j] = packed


def layout_kernel(
    slab_blocks, tiles_ref, coup_ref, far_ref, table_ref, mat_ref, idx_ref, t_s, c_s, m_s
):
    types = tiles_ref.shape[0]
    blocks, partners, _ = coup_ref.shape
    spread(tiles_ref, t_s, types, TILE, TILE)
    for t in range(types):
        table_ref[t] = join(t_s, t * TILE, TILE, types * TILE)

    deep = partners // 4
    rows = blocks * RANK
    lane = lax.broadcasted_iota(jnp.int32, (deep, LANES), 1) // RANK

    def one_block(i, _):
        for big in range(RANK // 4):
            at = big * partners
            c_s[at : at + partners, :] = coup_ref[i, :, big * LANES : (big + 1) * LANES].astype(F32)
        for big in range(RANK // 4):
            parts = [
                c_s[pl.ds(big * partners + j, deep, stride=4), :] for j in range(4)
            ]
            turned = [
                [parts[j] if r == 0 else pltpu.roll(parts[j], r * RANK, 1) for r in range(4)]
                for j in range(4)
            ]
            for small in range(4):
                out = turned[0][(0 - small) % 4]
                for j in range(1, 4):
                    out = jnp.where(lane == j, turned[j][(j - small) % 4], out)
                m_s[pl.ds(i * RANK + big * 4 + small, deep, stride=rows), :] = out
        return 0

    lax.fori_loop(0, blocks, one_block, 0)
    for k in range(deep):
        mat_ref[:, k * LANES : (k + 1) * LANES] = m_s[k * rows : (k + 1) * rows, :].astype(BF16)

    source = far_ref[...] % slab_blocks
    slot = lax.broadcasted_iota(jnp.int32, source.shape, 1)
    idx_ref[...] = ((slot - source) & 3) * (slab_blocks // 4) + source // 4


def near_kernel(
    slabs, slab_blocks,
    me_ref, src_ref, type_ref, count_ref, lo_ref, hi_ref, prev_ref, next_ref, table_ref,
    out_ref, e_s, p_s,
):
    blocks, slots = src_ref.shape
    types = table_ref.shape[0]
    rim = RIM * RHS
    e_s[0:rim, :] = lo_ref[...]
    e_s[rim : 2 * rim, :] = hi_ref[...]
    e_s[2 * rim : 3 * rim, :] = prev_ref[...]
    e_s[3 * rim : 4 * rim, :] = next_ref[...]
    p_s[0:types] = jnp.zeros((types,) + p_s.shape[1:], BF16)
    me = me_ref[0]

    def one_block(i, _):
        count = count_ref[i]
        for k in range(slots):
            source = src_ref[i, k]
            step = lax.rem(source // slab_blocks - me + slabs, slabs)
            local = lax.rem(source, blocks)
            at = local + jnp.where(step == 0, 0, jnp.where(step == 1, 3 * RIM, RIM))
            kind = jnp.where(k < count, type_ref[i, k], types)
            slab = e_s[pl.ds(pl.multiple_of(at * RHS, RHS), RHS), :]
            p_s[kind, pl.ds(pl.multiple_of(i * RHS, RHS), RHS), :] = slab
        return 0

    lax.fori_loop(0, blocks, one_block, 0)
    half = blocks * RHS // 2
    for a in range(2):
        total = None
        for t in range(types):
            term = lax.dot_general(
                p_s[t, a * half : (a + 1) * half, :], table_ref[t], NT, preferred_element_type=F32
            )
            total = term if total is None else total + term
        out_ref[a * half : (a + 1) * half, LANES:] = jnp.zeros((half, LANES), F32)
        out_ref[a * half : (a + 1) * half, :TILE] = total


def far_kernel(last, idx_ref, got_ref, mat_ref, basis_ref, near_ref, *rest):
    if last:
        y_ref, turn_s, pick_s, sum_s = rest
    else:
        y_ref, lo_ref, hi_ref, coef_ref, turn_s, pick_s, sum_s = rest
    blocks, partners = idx_ref.shape
    peers, packed_rows, _ = got_ref.shape
    quarter = peers * packed_rows
    for j in range(peers):
        got = got_ref[j].astype(F32)
        for r in range(4):
            turned = got if r == 0 else pltpu.roll(got, r * RANK, 1)
            at = r * quarter + j * packed_rows
            turn_s[at : at + packed_rows, :] = turned.astype(BF16)
    lane = lax.broadcasted_iota(jnp.int32, (RHS, LANES), 1) // RANK

    def one_block(i, _):
        for k in range(partners // 4):
            out = None
            for j in range(4):
                at = pl.multiple_of(idx_ref[i, k * 4 + j] * RHS, RHS)
                part = turn_s[pl.ds(at, RHS), :]
                out = part if out is None else jnp.where(lane == j, part, out)
            pick_s[pl.ds(pl.multiple_of(i * RHS, RHS), RHS), k * LANES : (k + 1) * LANES] = out
        return 0

    lax.fori_loop(0, blocks, one_block, 0)
    size = blocks * RHS
    rows, cols = GROUP * RHS, GROUP * RANK
    own = (
        lax.broadcasted_iota(jnp.int32, (rows, cols), 0) // RHS
        == lax.broadcasted_iota(jnp.int32, (rows, cols), 1) // RANK
    )
    for g in range(blocks // GROUP):
        cross = lax.dot_general(
            pick_s[g * rows : (g + 1) * rows, :],
            mat_ref[g * cols : (g + 1) * cols, :],
            NT,
            preferred_element_type=F32,
        )
        mix = jnp.where(own, cross, 0.0).astype(BF16)
        far = lax.dot_general(
            mix, basis_ref[g * cols : (g + 1) * cols, :], NN, preferred_element_type=F32
        )
        total = near_ref[g * rows : (g + 1) * rows, :] + far
        sum_s[g * rows : (g + 1) * rows, :] = total[:, :LANES]
        sum_s[size + g * rows : size + (g + 1) * rows, :] = total[:, LANES:]
    if not last:
        field = join(sum_s, 0, size, size)
        rim = RIM * RHS
        lo_ref[...] = field[:rim]
        hi_ref[...] = field[rim:]
        packed = project(field, basis_ref, blocks)
        for j in range(coef_ref.shape[0]):
            coef_ref[j] = packed
    low = lax.broadcasted_iota(jnp.int32, (blocks, LANES), 1) < LANES // 2
    for h in range(0, RHS, 2):
        one, two, three, four = (
            sum_s[pl.ds(side * size + h + k, blocks, stride=RHS), :]
            for k in range(2)
            for side in range(2)
        )
        three, four = (pltpu.roll(x, LANES // 2, 1) for x in (three, four))
        pair = (one, jnp.where(low, two, three), jnp.where(low, three, four))
        for j in range(3):
            at = h * TILE + j * LANES
            y_ref[:, at : at + LANES] = pair[j].astype(BF16)


def per_device(vectors, tiles, near_src, near_type, near_count, bases, far_src, coupling):
    blocks = vectors.shape[0]
    types = tiles.shape[0]
    partners = far_src.shape[1]
    slabs, peers = lax.axis_size("slab"), lax.axis_size("grp")
    slab_blocks = blocks * peers
    rows = blocks * RHS
    rim = RIM * RHS
    ranks = blocks * RANK
    packed = rows // 4
    shape = jax.ShapeDtypeStruct
    up = [(i, (i + 1) % slabs) for i in range(slabs)]
    down = [(j, i) for i, j in up]
    me = lax.axis_index("slab").astype(jnp.int32).reshape(1)

    lo, hi, basis, coef = pl.pallas_call(
        opening_kernel,
        out_shape=(
            shape((rim, WIDE), BF16),
            shape((rim, WIDE), BF16),
            shape((ranks, WIDE), BF16),
            shape((peers, packed, LANES), BF16),
        ),
        in_specs=[VMEM] * 2,
        out_specs=(VMEM,) * 4,
        scratch_shapes=[pltpu.VMEM((2 * rows, LANES), F32), pltpu.VMEM((2 * ranks, LANES), F32)],
        compiler_params=params(),
        name="opening",
    )(vectors, bases)

    table, mat, idx = pl.pallas_call(
        functools.partial(layout_kernel, slab_blocks),
        out_shape=(
            shape((types, TILE, WIDE), BF16),
            shape((ranks, partners * RANK), BF16),
            shape(far_src.shape, jnp.int32),
        ),
        in_specs=[VMEM] * 3,
        out_specs=(VMEM,) * 3,
        scratch_shapes=[
            pltpu.VMEM((2 * types * TILE, LANES), F32),
            pltpu.VMEM((partners * RANK // 4, LANES), F32),
            pltpu.VMEM((partners // 4 * ranks, LANES), F32),
        ],
        compiler_params=params(),
        cost_estimate=pl.CostEstimate(flops=0, bytes_accessed=12_000_000, transcendentals=0),
        name="layout",
    )(tiles, coupling, far_src)

    def near(lo, hi):
        prev = lax.ppermute(hi, "slab", up)
        succ = lax.ppermute(lo, "slab", down)
        return pl.pallas_call(
            functools.partial(near_kernel, slabs, slab_blocks),
            out_shape=shape((rows, WIDE), F32),
            in_specs=[SMEM] * 4 + [VMEM] * 5,
            out_specs=VMEM,
            scratch_shapes=[
                pltpu.VMEM((4 * rim, WIDE), BF16),
                pltpu.VMEM((types + 1, rows, WIDE), BF16),
            ],
            compiler_params=params(),
            cost_estimate=pl.CostEstimate(flops=0, bytes_accessed=12_000_000, transcendentals=0),
            name="near",
        )(me, near_src, near_type, near_count, lo, hi, prev, succ, table)

    def far(last, got, near_term):
        field = [shape((blocks, RHS * TILE), BF16)]
        if not last:
            field += [
                shape((rim, WIDE), BF16),
                shape((rim, WIDE), BF16),
                shape((peers, packed, LANES), BF16),
            ]
        return pl.pallas_call(
            functools.partial(far_kernel, last),
            out_shape=tuple(field),
            in_specs=[SMEM] + [VMEM] * 4,
            out_specs=(VMEM,) * len(field),
            scratch_shapes=[
                pltpu.VMEM((4 * peers * packed, LANES), BF16),
                pltpu.VMEM((rows, partners * RANK), BF16),
                pltpu.VMEM((2 * rows, LANES), F32),
            ],
            compiler_params=params(),
            name="far_last" if last else "far_first",
        )(idx, got, mat, basis, near_term)

    got = lax.all_to_all(coef, "grp", 0, 0, tiled=True)
    near_term = near(lo, hi)
    first, lo, hi, coef = far(False, got, near_term)
    got = lax.all_to_all(coef, "grp", 0, 0, tiled=True)
    near_term = near(lo, hi)
    (second,) = far(True, got, near_term)
    return (first, second)


def solution(mesh):
    in_specs = (
        P(("slab", "grp"), None),
        P(),
        P(("slab", "grp"), None),
        P(("slab", "grp"), None),
        P(("slab", "grp")),
        P(("slab", "grp"), None),
        P(("slab", "grp"), None),
        P(("slab", "grp"), None, None),
    )
    out_specs = (P(("slab", "grp"), None), P(("slab", "grp"), None))
    return jax.shard_map(
        per_device, mesh=mesh, in_specs=in_specs, out_specs=out_specs, check_vma=False
    )
```

time: 169 us -> 84.2 us (0.50)
  the two profiles are of different devices: /device:TPU:32 before, /device:TPU:8 now
where the time goes in v1:
time: 84.2 us; the launch traced here: 83.5 us
  Pallas kernels  32.4 us (38%)
  starting transfers between devices  26.7 us (32%)
  local copies, waits for them, and re-layouts  17.2 us (20%)
  waiting for transfers between devices  6.45 us (8%)
    all_to_all x2, starting transfers between devices, per_device(): got = lax.all_to_all(coef, 'grp', 0, 0, tiled=True)  21.3 us
    unnamed x46, local copies, waits for them, and re-layouts  17.2 us
    pallas_call x2, Pallas kernels, near(): pl.pallas_call(functools.partial(near_kernel, slabs, slab_blocks), out_sh...  14.3 us
    pallas_call x1, Pallas kernels, per_device(): pl.pallas_call(functools.partial(layout_kernel, slab_blocks), out_shape=(...  9.19 us
    pallas_call x2, Pallas kernels, far(): pl.pallas_call(functools.partial(far_kernel, last), out_shape=tuple(field...  7.38 us
    ppermute x2, starting transfers between devices, near(): succ = lax.ppermute(lo, 'slab', down)  5.39 us
    ppermute x2, waiting for transfers between devices, near(): prev = lax.ppermute(hi, 'slab', up)  4.36 us
    ppermute x2, waiting for transfers between devices, near(): succ = lax.ppermute(lo, 'slab', down)  2.09 us
  transfers between devices with their start and end apart: 6, of which 2 were waited for; matrix products, arithmetic and copies ran while one was open for 0% of the time, Pallas kernels for 28%

profile of v1, /device:TPU:8, one launch (start us, length us, event | category | flops | bytes accessed | tf_op | source)
XLA Modules:
  0.0 83.5 jit_solution(7221861964785418731)
XLA Ops:
  0.6 0.9 %copy-done.13 = bf16[16,6144]{1,0:T(8,128)(2,1)S(1)} copy-done((bf16[16,6144]{1,0:T(8,128)(2,1)S(1)}, bf16[16,6144]{1,0:T(8,128)(2,1)}, u32[]{:S(2)}) %copy-start.13) | copy-done | bytes 196632
  1.6 0.9 %copy-done.14 = bf16[16,3072]{1,0:T(8,128)(2,1)S(1)} copy-done((bf16[16,3072]{1,0:T(8,128)(2,1)S(1)}, bf16[16,3072]{1,0:T(8,128)(2,1)}, u32[]{:S(2)}) %copy-start.14) | copy-done | bytes 98328
  2.5 1.6 %opening.1 = (bf16[128,256]{1,0:T(8,128)(2,1)S(1)}, bf16[128,256]{1,0:T(8,128)(2,1)S(1)}, bf16[512,256]{1,0:T(8,128)(2,1)S(1)}, bf16[16,64,128]{2,1,0:T(8,128)(2,1)}) custom-call(bf16[16,3072]{1,0:T(8,128)(2,1)S(1)} %copy-done.14, bf16[16,6144]{1,0:T(8,128)(2,1)S(1)} %copy-done.13), custom_call_target="tpu_custom_call" | custom-call | tf_op jit(solution)/shard_map/opening/pallas_call | solution.py:257
  4.7 11.6 %all-to-all-start = ((bf16[16,64,128]{2,1,0:T(8,128)(2,1)}), bf16[16,64,128]{2,1,0:T(8,128)(2,1)S(1)}, u32[]{:S(2)}, u32[]{:S(2)}) async-start(bf16[16,64,128]{2,1,0:T(8,128)(2,1)} %get-tuple-element.14), calls=%async_computation | async-start | bytes 524288 | tf_op jit(solution)/shard_map/all_to_all | solution.py:330
  16.3 2.1 %collective-permute-start.1 = (bf16[128,256]{1,0:T(8,128)(2,1)S(1)}, bf16[128,256]{1,0:T(8,128)(2,1)}, u32[]{:S(2)}, u32[]{:S(2)}) collective-permute-start(bf16[128,256]{1,0:T(8,128)(2,1)S(1)} %get-tuple-element.17.lo_ref), channel_id=1, source_target_pairs={{16,0},{32,16},{48,32},{64,48},{80,64},{96,80},{112,96},{128,112},... | collective-permute-start | bytes 196616 | tf_op jit(solution)/shard_map/ppermute | solution.py:293
  18.4 1.7 %copy-done.3 = bf16[32,36864]{1,0:T(8,128)(2,1)S(1)} copy-done((bf16[32,36864]{1,0:T(8,128)(2,1)S(1)}, bf16[32,36864]{1,0:T(8,128)(2,1)}, u32[]{:S(2)}) %copy-start.3) | copy-done | bytes 2359320
  20.0 1.2 %copy-done.4 = bf16[16,32,1024]{2,1,0:T(8,128)(2,1)S(1)} copy-done((bf16[16,32,1024]{2,1,0:T(8,128)(2,1)S(1)}, bf16[16,32,1024]{2,1,0:T(8,128)(2,1)}, u32[]{:S(2)}) %copy-start.4) | copy-done | bytes 1048600
  22.0 9.2 %layout.1 = (bf16[32,192,256]{2,1,0:T(8,128)(2,1)S(1)}, bf16[512,1024]{1,0:T(8,128)(2,1)S(1)}, s32[16,32]{1,0:T(8,128)S(1)}) custom-call(bf16[32,36864]{1,0:T(8,128)(2,1)S(1)} %copy-done.3, bf16[16,32,1024]{2,1,0:T(8,128)(2,1)S(1)} %copy-done.4, s32[16,32]{1,0:T(8,128)S(1)} %copy-done.20), custom_call_target="tpu_custom_call" | custom-call | bytes 12000000 | tf_op jit(solution)/shard_map/layout/pallas_call | solution.py:272
  31.2 1.0 %copy-done = bf16[512,1024]{1,0:T(8,128)(2,1)} copy-done((bf16[512,1024]{1,0:T(8,128)(2,1)}, bf16[512,1024]{1,0:T(8,128)(2,1)S(1)}, u32[]{:S(2)}) %copy-start) | copy-done | bytes 1048600
  32.8 7.2 %near.2.near_ref = f32[256,256]{1,0:T(8,128)S(1)} custom-call(s32[1]{0:T(128)} %bitcast.me_ref, s32[16,20]{1,0:T(8,128)S(1)} %copy-done.15, s32[16,20]{1,0:T(8,128)S(1)} %copy-done.16, s32[16]{0:T(128)S(1)} %copy-done.21, bf16[128,256]{1,0:T(8,128)(2,1)S(1)} %get-tuple-element.17.lo_ref, bf16[128,256]{1,0:T(8,128)(2,1)S(1)} %get-tuple-element.18.hi_ref, ...), custom_call_target="tpu_custom_call" | custom-call | bytes 12000000 | tf_op jit(solution)/shard_map/near/pallas_call | solution.py:294
  40.0 0.7 copy-done.8
  40.7 1.2 %copy-done.1 = bf16[512,1024]{1,0:T(8,128)(2,1)S(1)} copy-done((bf16[512,1024]{1,0:T(8,128)(2,1)S(1)}, bf16[512,1024]{1,0:T(8,128)(2,1)}, u32[]{:S(2)}) %copy-start.1) | copy-done | bytes 1048600
  41.9 0.9 %copy-done.6 = bf16[512,256]{1,0:T(8,128)(2,1)S(1)} copy-done((bf16[512,256]{1,0:T(8,128)(2,1)S(1)}, bf16[512,256]{1,0:T(8,128)(2,1)}, u32[]{:S(2)}) %copy-start.6) | copy-done | bytes 262168
  42.9 0.9 %copy-done.9 = f32[256,256]{1,0:T(8,128)S(1)} copy-done((f32[256,256]{1,0:T(8,128)S(1)}, f32[256,256]{1,0:T(8,128)}, u32[]{:S(2)}) %copy-start.9) | copy-done | bytes 262168
  44.5 3.5 %far_first.1 = (bf16[16,3072]{1,0:T(8,128)(2,1)}, bf16[128,256]{1,0:T(8,128)(2,1)S(1)}, bf16[128,256]{1,0:T(8,128)(2,1)S(1)}, bf16[16,64,128]{2,1,0:T(8,128)(2,1)S(1)}) custom-call(s32[16,32]{1,0:T(8,128)S(1)} %copy-done.18, bf16[16,64,128]{2,1,0:T(8,128)(2,1)S(1)} %all-to-all-done.got_ref, bf16[512,1024]{1,0:T(8,128)(2,1)S(1)} %copy-done.1, ...), custom_call_target="tpu_custom_call" | custom-call | tf_op jit(solution)/shard_map/far_first/pallas_call | solution.py:316
  48.0 0.7 copy-done.12
  48.8 9.8 %all-to-all-start.1 = ((bf16[16,64,128]{2,1,0:T(8,128)(2,1)}), bf16[16,64,128]{2,1,0:T(8,128)(2,1)}, u32[]{:S(2)}, u32[]{:S(2)}) async-start(bf16[16,64,128]{2,1,0:T(8,128)(2,1)} %copy-done.12), calls=%async_computation.1 | async-start | bytes 524288 | tf_op jit(solution)/shard_map/all_to_all | solution.py:333
  58.5 3.3 %collective-permute-start.3 = (bf16[128,256]{1,0:T(8,128)(2,1)S(1)}, bf16[128,256]{1,0:T(8,128)(2,1)S(1)}, u32[]{:S(2)}, u32[]{:S(2)}) collective-permute-start(bf16[128,256]{1,0:T(8,128)(2,1)S(1)} %get-tuple-element.22.lo_ref), channel_id=1, source_target_pairs={{16,0},{32,16},{48,32},{64,48},{80,64},{96,80},{112,96},{128,112},... | collective-permute-start | bytes 196616 | tf_op jit(solution)/shard_map/ppermute | solution.py:293
  61.8 2.1 %collective-permute-done.3.next_ref = bf16[128,256]{1,0:T(8,128)(2,1)S(1)} collective-permute-done((bf16[128,256]{1,0:T(8,128)(2,1)S(1)}, bf16[128,256]{1,0:T(8,128)(2,1)S(1)}, u32[]{:S(2)}, u32[]{:S(2)}) %collective-permute-start.3) | collective-permute-done | bytes 65568 | tf_op jit(solution)/shard_map/ppermute | solution.py:293
  63.9 4.4 %collective-permute-done.2.prev_ref = bf16[128,256]{1,0:T(8,128)(2,1)S(1)} collective-permute-done((bf16[128,256]{1,0:T(8,128)(2,1)S(1)}, bf16[128,256]{1,0:T(8,128)(2,1)S(1)}, u32[]{:S(2)}, u32[]{:S(2)}) %collective-permute-start.2) | collective-permute-done | bytes 65568 | tf_op jit(solution)/shard_map/ppermute | solution.py:292
  68.9 7.1 %near.3.near_ref = f32[256,256]{1,0:T(8,128)S(1)} custom-call(s32[1]{0:T(128)} %bitcast.me_ref, s32[16,20]{1,0:T(8,128)S(1)} %copy-done.15, s32[16,20]{1,0:T(8,128)S(1)} %copy-done.16, s32[16]{0:T(128)S(1)} %copy-done.22, bf16[128,256]{1,0:T(8,128)(2,1)S(1)} %get-tuple-element.22.lo_ref, bf16[128,256]{1,0:T(8,128)(2,1)S(1)} %get-tuple-element.23.hi_ref, ...), custom_call_target="tpu_custom_call" | custom-call | bytes 12000000 | tf_op jit(solution)/shard_map/near/pallas_call | solution.py:294
  76.7 1.2 %copy-done.2 = bf16[512,1024]{1,0:T(8,128)(2,1)S(1)} copy-done((bf16[512,1024]{1,0:T(8,128)(2,1)S(1)}, bf16[512,1024]{1,0:T(8,128)(2,1)}, u32[]{:S(2)}) %copy-start.2) | copy-done | bytes 1048600
  78.0 0.9 %copy-done.11 = f32[256,256]{1,0:T(8,128)S(1)} copy-done((f32[256,256]{1,0:T(8,128)S(1)}, f32[256,256]{1,0:T(8,128)}, u32[]{:S(2)}) %copy-start.11) | copy-done | bytes 262168
  79.6 3.8 %far_last.1 = bf16[16,3072]{1,0:T(8,128)(2,1)} custom-call(s32[16,32]{1,0:T(8,128)S(1)} %copy-done.19, bf16[16,64,128]{2,1,0:T(8,128)(2,1)} %all-to-all-done.1.got_ref, bf16[512,1024]{1,0:T(8,128)(2,1)S(1)} %copy-done.2, bf16[512,256]{1,0:T(8,128)(2,1)S(1)} %copy-done.7, f32[256,256]{1,0:T(8,128)S(1)} %copy-done.11), custom_call_target="tpu_custom_call" | custom-call | tf_op jit(solution)/shard_map/far_last/pallas_call | solution.py:316
  (40 shorter events, 4.8 us)
Async XLA Ops:
  0.6 0.9 %copy-start.13 = (bf16[16,6144]{1,0:T(8,128)(2,1)S(1)}, bf16[16,6144]{1,0:T(8,128)(2,1)}, u32[]{:S(2)}) copy-start(bf16[16,6144]{1,0:T(8,128)(2,1)} %b_ref.1) | copy-start | bytes 589828
  1.6 0.9 %copy-start.14 = (bf16[16,3072]{1,0:T(8,128)(2,1)S(1)}, bf16[16,3072]{1,0:T(8,128)(2,1)}, u32[]{:S(2)}) copy-start(bf16[16,3072]{1,0:T(8,128)(2,1)} %v_ref.1) | copy-start | bytes 294916
  2.5 30.3 %copy-start.15 = (s32[16,20]{1,0:T(8,128)S(1)}, s32[16,20]{1,0:T(8,128)}, u32[]{:S(2)}) copy-start(s32[16,20]{1,0:T(8,128)} %src_ref.3) | copy-start | bytes 3844
  2.5 30.3 %copy-start.16 = (s32[16,20]{1,0:T(8,128)S(1)}, s32[16,20]{1,0:T(8,128)}, u32[]{:S(2)}) copy-start(s32[16,20]{1,0:T(8,128)} %type_ref.3) | copy-start | bytes 3844
  4.0 0.7 copy-start.5
  4.7 36.0 %all-to-all-start = ((bf16[16,64,128]{2,1,0:T(8,128)(2,1)}), bf16[16,64,128]{2,1,0:T(8,128)(2,1)S(1)}, u32[]{:S(2)}, u32[]{:S(2)}) async-start(bf16[16,64,128]{2,1,0:T(8,128)(2,1)} %get-tuple-element.14), calls=%async_computation | async-start | bytes 524288 | tf_op jit(solution)/shard_map/all_to_all | solution.py:330
  16.3 16.5 %collective-permute-start.1 = (bf16[128,256]{1,0:T(8,128)(2,1)S(1)}, bf16[128,256]{1,0:T(8,128)(2,1)}, u32[]{:S(2)}, u32[]{:S(2)}) collective-permute-start(bf16[128,256]{1,0:T(8,128)(2,1)S(1)} %get-tuple-element.17.lo_ref), channel_id=1, source_target_pairs={{16,0},{32,16},{48,32},{64,48},{80,64},{96,80},{112,96},{128,112},... | collective-permute-start | bytes 196616 | tf_op jit(solution)/shard_map/ppermute | solution.py:293
  18.4 14.4 %collective-permute-start = (bf16[128,256]{1,0:T(8,128)(2,1)S(1)}, bf16[128,256]{1,0:T(8,128)(2,1)}, u32[]{:S(2)}, u32[]{:S(2)}) collective-permute-start(bf16[128,256]{1,0:T(8,128)(2,1)S(1)} %get-tuple-element.18.hi_ref), channel_id=1, source_target_pairs={{0,16},{16,32},{32,48},{48,64},{64,80},{80,96},{96,112},{112,128},... | collective-permute-start | bytes 196616 | tf_op jit(solution)/shard_map/ppermute | solution.py:292
  18.4 1.7 %copy-start.3 = (bf16[32,36864]{1,0:T(8,128)(2,1)S(1)}, bf16[32,36864]{1,0:T(8,128)(2,1)}, u32[]{:S(2)}) copy-start(bf16[32,36864]{1,0:T(8,128)(2,1)} %tiles_ref.1) | copy-start | bytes 7077892
  20.0 1.2 %copy-start.4 = (bf16[16,32,1024]{2,1,0:T(8,128)(2,1)S(1)}, bf16[16,32,1024]{2,1,0:T(8,128)(2,1)}, u32[]{:S(2)}) copy-start(bf16[16,32,1024]{2,1,0:T(8,128)(2,1)} %coup_ref.1) | copy-start | bytes 3145732
  22.0 10.8 %copy-start.21 = (s32[16]{0:T(128)S(1)}, s32[16]{0:T(128)}, u32[]{:S(2)}) copy-start(s32[16]{0:T(128)} %count_ref.3) | copy-start | bytes 196
  31.2 1.0 %copy-start = (bf16[512,1024]{1,0:T(8,128)(2,1)}, bf16[512,1024]{1,0:T(8,128)(2,1)S(1)}, u32[]{:S(2)}) copy-start(bf16[512,1024]{1,0:T(8,128)(2,1)S(1)} %get-tuple-element.15.mat_ref) | copy-start | bytes 3145732
  39.9 0.7 copy-start.8
  40.7 1.2 %copy-start.1 = (bf16[512,1024]{1,0:T(8,128)(2,1)S(1)}, bf16[512,1024]{1,0:T(8,128)(2,1)}, u32[]{:S(2)}) copy-start(bf16[512,1024]{1,0:T(8,128)(2,1)} %copy-done) | copy-start | bytes 3145732
  41.9 0.9 %copy-start.6 = (bf16[512,256]{1,0:T(8,128)(2,1)S(1)}, bf16[512,256]{1,0:T(8,128)(2,1)}, u32[]{:S(2)}) copy-start(bf16[512,256]{1,0:T(8,128)(2,1)} %copy-done.5) | copy-start | bytes 786436
  42.9 0.9 %copy-start.9 = (f32[256,256]{1,0:T(8,128)S(1)}, f32[256,256]{1,0:T(8,128)}, u32[]{:S(2)}) copy-start(f32[256,256]{1,0:T(8,128)} %copy-done.8) | copy-start | bytes 786436
  48.0 0.7 copy-start.12
  48.8 28.0 %copy-start.7 = (bf16[512,256]{1,0:T(8,128)(2,1)S(1)}, bf16[512,256]{1,0:T(8,128)(2,1)}, u32[]{:S(2)}) copy-start(bf16[512,256]{1,0:T(8,128)(2,1)} %copy-done.5) | copy-start | bytes 786436
  48.8 28.0 %all-to-all-start.1 = ((bf16[16,64,128]{2,1,0:T(8,128)(2,1)}), bf16[16,64,128]{2,1,0:T(8,128)(2,1)}, u32[]{:S(2)}, u32[]{:S(2)}) async-start(bf16[16,64,128]{2,1,0:T(8,128)(2,1)} %copy-done.12), calls=%async_computation.1 | async-start | bytes 524288 | tf_op jit(solution)/shard_map/all_to_all | solution.py:333
  58.5 5.4 %collective-permute-start.3 = (bf16[128,256]{1,0:T(8,128)(2,1)S(1)}, bf16[128,256]{1,0:T(8,128)(2,1)S(1)}, u32[]{:S(2)}, u32[]{:S(2)}) collective-permute-start(bf16[128,256]{1,0:T(8,128)(2,1)S(1)} %get-tuple-element.22.lo_ref), channel_id=1, source_target_pairs={{16,0},{32,16},{48,32},{64,48},{80,64},{96,80},{112,96},{128,112},... | collective-permute-start | bytes 196616 | tf_op jit(solution)/shard_map/ppermute | solution.py:293
  61.8 6.4 %collective-permute-start.2 = (bf16[128,256]{1,0:T(8,128)(2,1)S(1)}, bf16[128,256]{1,0:T(8,128)(2,1)S(1)}, u32[]{:S(2)}, u32[]{:S(2)}) collective-permute-start(bf16[128,256]{1,0:T(8,128)(2,1)S(1)} %get-tuple-element.23.hi_ref), channel_id=1, source_target_pairs={{0,16},{16,32},{32,48},{48,64},{64,80},{80,96},{96,112},{112,128},... | collective-permute-start | bytes 196616 | tf_op jit(solution)/shard_map/ppermute | solution.py:292
  76.0 0.7 copy-start.10
  76.7 1.2 %copy-start.2 = (bf16[512,1024]{1,0:T(8,128)(2,1)S(1)}, bf16[512,1024]{1,0:T(8,128)(2,1)}, u32[]{:S(2)}) copy-start(bf16[512,1024]{1,0:T(8,128)(2,1)} %copy-done) | copy-start | bytes 3145732
  78.0 0.9 %copy-start.11 = (f32[256,256]{1,0:T(8,128)S(1)}, f32[256,256]{1,0:T(8,128)}, u32[]{:S(2)}) copy-start(f32[256,256]{1,0:T(8,128)} %copy-done.10) | copy-start | bytes 786436
  (5 other events, 3.3 us)

commit v2 on v0

v2 whole, which is shorter than its diff:
```python
import functools

import jax
import jax.numpy as jnp
from jax import lax
from jax.experimental import pallas as pl
from jax.experimental.pallas import tpu as pltpu
from jax.sharding import PartitionSpec as P

TILE = 192
RHS = 16
RANK = 32
RIM = 8
LANES = 128
WIDE = 256
GROUP = 8
SIDE = LANES // RANK

VMEM = pl.BlockSpec(memory_space=pltpu.VMEM)
SMEM = pl.BlockSpec(memory_space=pltpu.SMEM)
HBM = pl.BlockSpec(memory_space=pltpu.HBM)
F32 = jnp.float32
BF16 = jnp.bfloat16
NT = (((1,), (1,)), ((), ()))
NN = (((1,), (0,)), ((), ()))
shape = jax.ShapeDtypeStruct


def call(kernel, name, args, ins, outs, scratch, mib, moved=0):
    args = [
        pltpu.with_memory_space_constraint(a, pltpu.HBM) if s is HBM else a
        for a, s in zip(args, ins)
    ]
    return pl.pallas_call(
        kernel,
        out_shape=tuple(o for o, _ in outs),
        in_specs=ins,
        out_specs=tuple(s for _, s in outs),
        scratch_shapes=scratch,
        compiler_params=pltpu.CompilerParams(vmem_limit_bytes=mib * 1024 * 1024),
        cost_estimate=pl.CostEstimate(flops=0, bytes_accessed=moved, transcendentals=0),
        name=name,
    )(*args)


def iota(shape, axis):
    return lax.broadcasted_iota(jnp.int32, shape, axis)


def swap(rows, outer):
    at = iota((rows, rows), 0)
    source = (at % outer) * (rows // outer) + at // outer
    return (iota((rows, rows), 1) == source).astype(BF16)


def turn(x):
    return pltpu.roll(x, LANES // 2, 1)


def halves(pair):
    low = iota((pair.shape[0], LANES), 1) < LANES // 2
    one, two, three = (pair[:, j * LANES : (j + 1) * LANES] for j in range(3))
    two_turned, three_turned = turn(two), turn(three)
    zero = jnp.zeros_like(two)
    return (
        (one, jnp.where(low, two, zero)),
        (jnp.where(low, two_turned, three_turned), jnp.where(low, three_turned, zero)),
    )


def spread(source_ref, scratch, rows, count):
    size = rows * count
    for j in range(0, count, 2):
        pair = source_ref[:, j * TILE : (j + 2) * TILE].astype(F32)
        for k, parts in enumerate(halves(pair)):
            for side, part in enumerate(parts):
                scratch[pl.ds(side * size + j + k, rows, stride=count), :] = part


def gather_sides(scratch, y_ref, blocks):
    size = blocks * RHS
    low = iota((blocks, LANES), 1) < LANES // 2
    for h in range(0, RHS, 2):
        one, two, three, four = (
            scratch[pl.ds(side * size + h + k, blocks, stride=RHS), :]
            for k in range(2)
            for side in range(2)
        )
        three, four = turn(three), turn(four)
        pair = (one, jnp.where(low, two, three), jnp.where(low, three, four))
        for j in range(3):
            at = h * TILE + j * LANES
            y_ref[:, at : at + LANES] = pair[j].astype(BF16)


def join(scratch, size):
    return jnp.concatenate(
        [scratch[side * size : (side + 1) * size, :].astype(BF16) for side in range(2)], axis=1
    )


def opening_kernel(v_hbm, b_hbm, lo_ref, hi_ref, basis_ref, v_s, b_s, f_s, g_s, sems):
    blocks = v_s.shape[0]
    rows, ranks = blocks * RHS, blocks * RANK
    get_v = pltpu.make_async_copy(v_hbm, v_s, sems.at[0])
    get_b = pltpu.make_async_copy(b_hbm, b_s, sems.at[1])
    get_v.start()
    get_b.start()
    get_v.wait()
    spread(v_s, f_s, blocks, RHS)
    field = join(f_s, rows)
    rim = RIM * RHS
    lo_ref[...] = field[:rim]
    hi_ref[...] = field[rim:]
    get_b.wait()
    spread(b_s, g_s, blocks, RANK)
    basis_ref[...] = join(g_s, ranks)


def project_kernel(lo_ref, hi_ref, basis_ref, coef_hbm, coef_s, sem):
    rows, cols = GROUP * RHS, GROUP * RANK
    lane = iota((RHS, LANES), 1) // RANK
    for g, field_ref in enumerate((lo_ref, hi_ref)):
        cross = lax.dot_general(
            field_ref[...],
            basis_ref[g * cols : (g + 1) * cols, :],
            NT,
            preferred_element_type=F32,
        )
        for half in range(GROUP // SIDE):
            out = None
            for j in range(SIDE):
                at = (half * SIDE + j) * RHS
                part = cross[at : at + RHS, half * LANES : (half + 1) * LANES]
                out = part if out is None else jnp.where(lane == j, part, out)
            at = (g * (GROUP // SIDE) + half) * RHS
            for j in range(coef_s.shape[0]):
                coef_s[j, at : at + RHS, :] = out.astype(BF16)
    put = pltpu.make_async_copy(coef_s, coef_hbm, sem)
    put.start()
    put.wait()


def layout_kernel(
    slabs, slab_blocks,
    me_ref, count_ref, src_hbm, type_hbm, far_hbm, tiles_hbm, coup_hbm,
    table_ref, mat_ref, far_idx_ref, at_ref, kind_ref,
    src_s, type_s, far_s, tiles_s, coup_s, sems,
):
    gets = [
        pltpu.make_async_copy(source, to, sems.at[j])
        for j, (source, to) in enumerate(
            (
                (coup_hbm, coup_s),
                (src_hbm, src_s),
                (type_hbm, type_s),
                (far_hbm, far_s),
                (tiles_hbm, tiles_s),
            )
        )
    ]
    for get in gets:
        get.start()
    types = tiles_s.shape[0]
    blocks, partners, _ = coup_s.shape
    deep = partners // SIDE

    lane = iota((deep, LANES), 1) // RANK
    order = swap(RANK * deep, RANK)
    gets[0].wait()

    def two_blocks(n, _):
        stacks = []
        for b in range(2):
            i = 2 * n + b
            stack = []
            for big in range(RANK // SIDE):
                x = coup_s[i, :, big * LANES : (big + 1) * LANES].astype(F32)
                parts = [x[j * deep : (j + 1) * deep] for j in range(SIDE)]
                turned = [
                    [p if r == 0 else pltpu.roll(p, r * RANK, 1) for r in range(SIDE)]
                    for p in parts
                ]
                for small in range(SIDE):
                    out = turned[0][-small % SIDE]
                    for j in range(1, SIDE):
                        out = jnp.where(lane == j, turned[j][(j - small) % SIDE], out)
                    stack.append(out)
            stacks.append(jnp.concatenate(stack, axis=0).astype(BF16))
        both = jnp.concatenate(stacks, axis=1)
        both = lax.dot_general(order, both, NN, preferred_element_type=F32).astype(BF16)
        for b in range(2):
            at = pl.multiple_of((2 * n + b) * RANK, RANK)
            for k in range(deep):
                part = both[k * RANK : (k + 1) * RANK, b * LANES : (b + 1) * LANES]
                mat_ref[pl.ds(at, RANK), k * LANES : (k + 1) * LANES] = part
        return 0

    lax.fori_loop(0, blocks // 2, two_blocks, 0, unroll=True)

    many = 16
    order = swap(many * many, many)
    for get in gets[1:4]:
        get.wait()
    source = far_s[...] % slab_blocks
    group = iota(source.shape, 1) // deep
    turned = (group - source) & (SIDE - 1)
    far_idx_ref[...] = (turned * (slab_blocks // SIDE) + source // SIDE) * RHS

    source = src_s[...]
    step = (source // slab_blocks - me_ref[0] + slabs) % slabs
    offset = jnp.where(step == 0, 0, jnp.where(step == 1, 3 * RIM, RIM))
    at_ref[...] = (source % blocks + offset) * RHS
    row = iota(source.shape, 0)
    count = jnp.zeros(source.shape, jnp.int32)
    for i in range(blocks):
        count = jnp.where(row == i, count_ref[i], count)
    kind_ref[...] = jnp.where(iota(source.shape, 1) < count, type_s[...], types) * WIDE

    gets[4].wait()

    def some_rows(n, _):
        at = pl.multiple_of(n * many * TILE, many * TILE)
        for a in range(types // many):
            stack = []
            for d in range(0, many, 2):
                pair = tiles_s[a * many : (a + 1) * many, pl.ds(at + d * TILE, 2 * TILE)]
                stack += [jnp.concatenate(parts, axis=1) for parts in halves(pair)]
            out = jnp.concatenate(stack, axis=0)
            out = lax.dot_general(order, out, NN, preferred_element_type=F32).astype(BF16)
            for t in range(many):
                to = (a * many + t) * WIDE
                table_ref[pl.ds(pl.multiple_of(n * many, many), many), to : to + WIDE] = out[
                    t * many : (t + 1) * many
                ]
        return 0

    lax.fori_loop(0, TILE // many, some_rows, 0, unroll=True)


def near_kernel(
    give, at_ref, kind_ref, lo_ref, hi_ref, prev_ref, next_ref, table_ref, out_ref, *rest
):
    if give:
        y_ref, e_s, p_s, f_s = rest
    else:
        e_s, p_s = rest
    blocks, slots = at_ref.shape
    size = blocks * RHS
    rim = RIM * RHS
    for j, ref in enumerate((lo_ref, hi_ref, prev_ref, next_ref)):
        e_s[j * rim : (j + 1) * rim, :] = ref[...]
    columns = table_ref.shape[1]
    p_s[:, :columns] = jnp.zeros((size, columns), BF16)

    def one_block(i, _):
        row = pl.multiple_of(i * RHS, RHS)
        for k in range(slots):
            source = pl.multiple_of(at_ref[i, k], RHS)
            column = pl.multiple_of(kind_ref[i, k], WIDE)
            p_s[pl.ds(row, RHS), pl.ds(column, WIDE)] = e_s[pl.ds(source, RHS), :]
        return 0

    lax.fori_loop(0, blocks, one_block, 0, unroll=True)
    if give:
        for j in range(2):
            f_s[j * size : (j + 1) * size, :] = e_s[:size, j * LANES : (j + 1) * LANES].astype(F32)
        gather_sides(f_s, y_ref, blocks)
    out_ref[:, LANES:] = jnp.zeros((size, LANES), F32)
    out_ref[:, :TILE] = lax.dot_general(
        p_s[:, :columns], table_ref[...], NT, preferred_element_type=F32
    )


def far_kernel(last, idx_ref, got_ref, mat_ref, basis_ref, near_ref, *rest):
    if last:
        y_ref, turn_s, pick_s, sum_s = rest
    else:
        lo_ref, hi_ref, turn_s, pick_s = rest
    blocks, partners = idx_ref.shape
    deep = partners // SIDE
    peers, packed_rows, _ = got_ref.shape
    quarter = peers * packed_rows
    for j in range(peers):
        got = got_ref[j]
        for r in range(SIDE):
            at = r * quarter + j * packed_rows
            turn_s[at : at + packed_rows, :] = got if r == 0 else pltpu.roll(got, r * RANK, 1)
    lane = iota((RHS, LANES), 1) // RANK

    def one_block(i, _):
        row = pl.multiple_of(i * RHS, RHS)
        for k in range(deep):
            out = None
            for j in range(SIDE):
                at = pl.multiple_of(idx_ref[i, j * deep + k], RHS)
                part = turn_s[pl.ds(at, RHS), :]
                out = part if out is None else jnp.where(lane == j, part, out)
            pick_s[pl.ds(row, RHS), k * LANES : (k + 1) * LANES] = out
        return 0

    lax.fori_loop(0, blocks, one_block, 0, unroll=True)
    size = blocks * RHS
    rows, cols = GROUP * RHS, GROUP * RANK
    own = iota((rows, cols), 0) // RHS == iota((rows, cols), 1) // RANK
    for g in range(blocks // GROUP):
        cross = lax.dot_general(
            pick_s[g * rows : (g + 1) * rows, :],
            mat_ref[g * cols : (g + 1) * cols, :],
            NT,
            preferred_element_type=F32,
        )
        mix = jnp.where(own, cross, 0.0).astype(BF16)
        far = lax.dot_general(
            mix, basis_ref[g * cols : (g + 1) * cols, :], NN, preferred_element_type=F32
        )
        total = near_ref[g * rows : (g + 1) * rows, :] + far
        if last:
            for j in range(2):
                at = j * size + g * rows
                sum_s[at : at + rows, :] = total[:, j * LANES : (j + 1) * LANES]
        else:
            (lo_ref, hi_ref)[g][...] = total.astype(BF16)
    if last:
        gather_sides(sum_s, y_ref, blocks)


def opening(vectors, bases):
    blocks = vectors.shape[0]
    rows, ranks, rim = blocks * RHS, blocks * RANK, RIM * RHS
    field = (shape((rim, WIDE), BF16), VMEM)
    return call(
        opening_kernel, "opening", (vectors, bases), [HBM] * 2,
        [field, field, (shape((ranks, WIDE), BF16), VMEM)],
        [
            pltpu.VMEM(vectors.shape, BF16),
            pltpu.VMEM(bases.shape, BF16),
            pltpu.VMEM((2 * rows, LANES), F32),
            pltpu.VMEM((2 * ranks, LANES), F32),
            pltpu.SemaphoreType.DMA((2,)),
        ],
        8,
    )


def project(peers, lo, hi, basis):
    packed = lo.shape[0] * 2 // SIDE
    coef = (peers, packed, LANES)
    return call(
        project_kernel, "project", (lo, hi, basis), [VMEM] * 3,
        [(shape(coef, BF16), HBM)],
        [pltpu.VMEM(coef, BF16), pltpu.SemaphoreType.DMA],
        4,
    )[0]


def layout(slabs, peers, me, near_count, near_src, near_type, far_src, tiles, coupling):
    blocks, partners, _ = coupling.shape
    types = tiles.shape[0]
    table = (TILE, types * WIDE)
    slots = shape(near_src.shape, jnp.int32)
    return call(
        functools.partial(layout_kernel, slabs, blocks * peers), "layout",
        (me, near_count, near_src, near_type, far_src, tiles, coupling),
        [SMEM] * 2 + [HBM] * 5,
        [
            (shape(table, BF16), VMEM),
            (shape((blocks * RANK, partners * RANK), BF16), VMEM),
            (shape(far_src.shape, jnp.int32), VMEM),
            (slots, VMEM),
            (slots, VMEM),
        ],
        [
            pltpu.VMEM(near_src.shape, jnp.int32),
            pltpu.VMEM(near_src.shape, jnp.int32),
            pltpu.VMEM(far_src.shape, jnp.int32),
            pltpu.VMEM(tiles.shape, BF16),
            pltpu.VMEM(coupling.shape, BF16),
            pltpu.SemaphoreType.DMA((5,)),
        ],
        16, 12_000_000,
    )


def near(give, at, kind, lo, hi, prev, succ, table):
    rim = lo.shape[0]
    rows = 2 * rim
    outs = [(shape((rows, WIDE), F32), VMEM)]
    scratch = [
        pltpu.VMEM((2 * rows, WIDE), BF16),
        pltpu.VMEM((rows, table.shape[1] + WIDE), BF16),
    ]
    if give:
        outs.append((shape((rows // RHS, RHS * TILE), BF16), VMEM))
        scratch.append(pltpu.VMEM((2 * rows, LANES), F32))
    return call(
        functools.partial(near_kernel, give), "near_give" if give else "near",
        (at, kind, lo, hi, prev, succ, table),
        [SMEM] * 2 + [VMEM] * 5, outs, scratch, 16, 12_000_000,
    )


def far(last, idx, got, mat, basis, near_term):
    rows = near_term.shape[0]
    peers, packed, _ = got.shape
    scratch = [
        pltpu.VMEM((SIDE * peers * packed, LANES), BF16),
        pltpu.VMEM((rows, mat.shape[1]), BF16),
    ]
    if last:
        outs = [(shape((rows // RHS, RHS * TILE), BF16), VMEM)]
        scratch.append(pltpu.VMEM((2 * rows, LANES), F32))
    else:
        outs = [(shape((rows // 2, WIDE), BF16), VMEM)] * 2
    return call(
        functools.partial(far_kernel, last), "far_last" if last else "far",
        (idx, got, mat, basis, near_term), [SMEM] + [VMEM] * 4, outs, scratch, 8,
    )


def per_device(vectors, tiles, near_src, near_type, near_count, bases, far_src, coupling):
    slabs, peers = lax.axis_size("slab"), lax.axis_size("grp")
    up = [(i, (i + 1) % slabs) for i in range(slabs)]
    down = [(j, i) for i, j in up]
    me = lax.axis_index("slab").astype(jnp.int32).reshape(1)

    def halo(lo, hi):
        return lax.ppermute(hi, "slab", up), lax.ppermute(lo, "slab", down)

    def exchange(lo, hi, basis):
        return lax.all_to_all(project(peers, lo, hi, basis), "grp", 0, 0, tiled=True)

    lo, hi, basis = opening(vectors, bases)
    prev, succ = halo(lo, hi)
    got = exchange(lo, hi, basis)
    table, mat, idx, at, kind = layout(
        slabs, peers, me, near_count, near_src, near_type, far_src, tiles, coupling
    )
    (near_term,) = near(False, at, kind, lo, hi, prev, succ, table)
    lo, hi = far(False, idx, got, mat, basis, near_term)
    prev, succ = halo(lo, hi)
    got = exchange(lo, hi, basis)
    near_term, first = near(True, at, kind, lo, hi, prev, succ, table)
    (second,) = far(True, idx, got, mat, basis, near_term)
    return (first, second)


def solution(mesh):
    in_specs = (
        P(("slab", "grp"), None),
        P(),
        P(("slab", "grp"), None),
        P(("slab", "grp"), None),
        P(("slab", "grp")),
        P(("slab", "grp"), None),
        P(("slab", "grp"), None),
        P(("slab", "grp"), None, None),
    )
    out_specs = (P(("slab", "grp"), None), P(("slab", "grp"), None))
    return jax.shard_map(
        per_device, mesh=mesh, in_specs=in_specs, out_specs=out_specs, check_vma=False
    )
```

time: 169 us -> 62.3 us (0.37)
  the two profiles are of different devices: /device:TPU:32 before, /device:TPU:8 now
where the time goes in v2:
time: 62.3 us; the launch traced here: 61.7 us
  starting transfers between devices  24.5 us (39%)
  Pallas kernels  18.5 us (30%)
  local copies, waits for them, and re-layouts  9.38 us (15%)
  waiting for transfers between devices  8.55 us (14%)
  between operations  0.72 us (1%)
    all_to_all x2, starting transfers between devices, exchange(): lax.all_to_all(project(peers, lo, hi, basis), 'grp', 0, 0, tiled=True)  20.5 us
    pallas_call x8, Pallas kernels, call(): pl.pallas_call(kernel, out_shape=tuple((o for o, _ in outs)), in_specs=in...  18.5 us
    unnamed x22, local copies, waits for them, and re-layouts  9.38 us
    ppermute x4, waiting for transfers between devices, halo(): return (lax.ppermute(hi, 'slab', up), lax.ppermute(lo, 'slab', down))  8.55 us
    ppermute x4, starting transfers between devices, halo(): return (lax.ppermute(hi, 'slab', up), lax.ppermute(lo, 'slab', down))  3.97 us
  transfers between devices with their start and end apart: 6, of which 3 were waited for; matrix products, arithmetic and copies ran while one was open for 0% of the time, Pallas kernels for 17%

profile of v2, /device:TPU:8, one launch (start us, length us, event | category | flops | bytes accessed | tf_op | source)
XLA Modules:
  0.0 61.7 jit_solution(7272097263623693492)
XLA Ops:
  0.6 1.6 %opening.1 = (bf16[128,256]{1,0:T(8,128)(2,1)S(1)}, bf16[128,256]{1,0:T(8,128)(2,1)S(1)}, bf16[512,256]{1,0:T(8,128)(2,1)S(1)}) custom-call(bf16[16,3072]{1,0:T(8,128)(2,1)} %v_hbm.1, bf16[16,6144]{1,0:T(8,128)(2,1)} %b_hbm.1), custom_call_target="tpu_custom_call" | custom-call | tf_op jit(solution)/shard_map/opening/pallas_call | solution.py:34
  2.2 0.9 %project.2 = bf16[16,64,128]{2,1,0:T(8,128)(2,1)} custom-call(bf16[128,256]{1,0:T(8,128)(2,1)S(1)} %get-tuple-element.17.lo_ref, bf16[128,256]{1,0:T(8,128)(2,1)S(1)} %get-tuple-element.18.hi_ref, bf16[512,256]{1,0:T(8,128)(2,1)S(1)} %get-tuple-element.19.basis_ref), custom_call_target="tpu_custom_call" | custom-call | tf_op jit(solution)/shard_map/project/pallas_call | solution.py:34
  3.2 11.6 %all-to-all-start = ((bf16[16,64,128]{2,1,0:T(8,128)(2,1)}), bf16[16,64,128]{2,1,0:T(8,128)(2,1)}, u32[]{:S(2)}, u32[]{:S(2)}) async-start(bf16[16,64,128]{2,1,0:T(8,128)(2,1)} %project.2), calls=%async_computation | async-start | bytes 524288 | tf_op jit(solution)/shard_map/all_to_all | solution.py:431
  14.7 2.1 %collective-permute-start.1 = (bf16[128,256]{1,0:T(8,128)(2,1)S(1)}, bf16[128,256]{1,0:T(8,128)(2,1)}, u32[]{:S(2)}, u32[]{:S(2)}) collective-permute-start(bf16[128,256]{1,0:T(8,128)(2,1)S(1)} %get-tuple-element.17.lo_ref), channel_id=1, source_target_pairs={{16,0},{32,16},{48,32},{64,48},{80,64},{96,80},{112,96},{128,112},... | collective-permute-start | bytes 196616 | tf_op jit(solution)/shard_map/ppermute | solution.py:428
  16.8 0.7 %copy-done.10 = s32[16]{0:T(128)S(1)} copy-done((s32[16]{0:T(128)S(1)}, s32[16]{0:T(128)}, u32[]{:S(2)}) %copy-start.10) | copy-done | bytes 88
  17.5 4.1 %layout.1 = (bf16[192,8192]{1,0:T(8,128)(2,1)S(1)}, bf16[512,1024]{1,0:T(8,128)(2,1)S(1)}, s32[16,32]{1,0:T(8,128)S(1)}, s32[16,20]{1,0:T(8,128)S(1)}, s32[16,20]{1,0:T(8,128)S(1)}) custom-call(s32[1]{0:T(128)} %bitcast.me_ref, s32[16]{0:T(128)S(1)} %copy-done.10, s32[16,20]{1,0:T(8,128)} %src_hbm.1, s32[16,20]{1,0:T(8,128)} %type_hbm.1, s32[16,32]{1,0:T(8,128)} %far_hbm.1, ...), custom_call_target="tpu_custom_call" | custom-call | bytes 12000000 | tf_op jit(solution)/shard_map/layout/pallas_call | solution.py:34
  21.7 1.0 %copy-done = bf16[512,1024]{1,0:T(8,128)(2,1)} copy-done((bf16[512,1024]{1,0:T(8,128)(2,1)}, bf16[512,1024]{1,0:T(8,128)(2,1)S(1)}, u32[]{:S(2)}) %copy-start) | copy-done | bytes 1048600
  22.6 2.1 %collective-permute-done.prev_ref = bf16[128,256]{1,0:T(8,128)(2,1)} collective-permute-done((bf16[128,256]{1,0:T(8,128)(2,1)S(1)}, bf16[128,256]{1,0:T(8,128)(2,1)}, u32[]{:S(2)}, u32[]{:S(2)}) %collective-permute-start) | collective-permute-done | bytes 65568 | tf_op jit(solution)/shard_map/ppermute | solution.py:428
  24.8 3.0 %near.1.near_ref = f32[256,256]{1,0:T(8,128)S(1)} custom-call(s32[16,20]{1,0:T(8,128)S(1)} %get-tuple-element.14.at_ref, s32[16,20]{1,0:T(8,128)S(1)} %get-tuple-element.15.kind_ref, bf16[128,256]{1,0:T(8,128)(2,1)S(1)} %get-tuple-element.17.lo_ref, bf16[128,256]{1,0:T(8,128)(2,1)S(1)} %get-tuple-element.18.hi_ref, ...), custom_call_target="tpu_custom_call" | custom-call | bytes 12000000 | tf_op jit(solution)/shard_map/near/pallas_call | solution.py:34
  27.8 0.7 %copy-done.3 = f32[256,256]{1,0:T(8,128)} copy-done((f32[256,256]{1,0:T(8,128)}, f32[256,256]{1,0:T(8,128)S(1)}, u32[]{:S(2)}) %copy-start.3) | copy-done | bytes 262168
  29.1 1.2 %copy-done.1 = bf16[512,1024]{1,0:T(8,128)(2,1)S(1)} copy-done((bf16[512,1024]{1,0:T(8,128)(2,1)S(1)}, bf16[512,1024]{1,0:T(8,128)(2,1)}, u32[]{:S(2)}) %copy-start.1) | copy-done | bytes 1048600
  30.3 0.9 %copy-done.4 = f32[256,256]{1,0:T(8,128)S(1)} copy-done((f32[256,256]{1,0:T(8,128)S(1)}, f32[256,256]{1,0:T(8,128)}, u32[]{:S(2)}) %copy-start.4) | copy-done | bytes 262168
  31.3 2.1 %far.1 = (bf16[128,256]{1,0:T(8,128)(2,1)S(1)}, bf16[128,256]{1,0:T(8,128)(2,1)S(1)}) custom-call(s32[16,32]{1,0:T(8,128)S(1)} %get-tuple-element.16.idx_ref, bf16[16,64,128]{2,1,0:T(8,128)(2,1)} %all-to-all-done.got_ref, bf16[512,1024]{1,0:T(8,128)(2,1)S(1)} %copy-done.1, bf16[512,256]{1,0:T(8,128)(2,1)S(1)} %get-tuple-element.19.basis_ref, ...), custom_call_target="tpu_custom_call" | custom-call | tf_op jit(solution)/shard_map/far/pallas_call | solution.py:34
  33.7 0.7 %copy-done.5 = bf16[16,64,128]{2,1,0:T(8,128)(2,1)} copy-done((bf16[16,64,128]{2,1,0:T(8,128)(2,1)}, bf16[16,64,128]{2,1,0:T(8,128)(2,1)S(1)}, u32[]{:S(2)}) %copy-start.5) | copy-done | bytes 262168
  34.4 8.9 %all-to-all-start.1 = ((bf16[16,64,128]{2,1,0:T(8,128)(2,1)}), bf16[16,64,128]{2,1,0:T(8,128)(2,1)}, u32[]{:S(2)}, u32[]{:S(2)}) async-start(bf16[16,64,128]{2,1,0:T(8,128)(2,1)} %copy-done.5), calls=%async_computation.1 | async-start | bytes 524288 | tf_op jit(solution)/shard_map/all_to_all | solution.py:431
  43.3 1.9 %collective-permute-start.3 = (bf16[128,256]{1,0:T(8,128)(2,1)S(1)}, bf16[128,256]{1,0:T(8,128)(2,1)S(1)}, u32[]{:S(2)}, u32[]{:S(2)}) collective-permute-start(bf16[128,256]{1,0:T(8,128)(2,1)S(1)} %get-tuple-element.22.lo_ref), channel_id=1, source_target_pairs={{16,0},{32,16},{48,32},{64,48},{80,64},{96,80},{112,96},{128,112},... | collective-permute-start | bytes 196616 | tf_op jit(solution)/shard_map/ppermute | solution.py:428
  45.2 3.7 %collective-permute-done.3.next_ref = bf16[128,256]{1,0:T(8,128)(2,1)S(1)} collective-permute-done((bf16[128,256]{1,0:T(8,128)(2,1)S(1)}, bf16[128,256]{1,0:T(8,128)(2,1)S(1)}, u32[]{:S(2)}, u32[]{:S(2)}) %collective-permute-start.3) | collective-permute-done | bytes 65568 | tf_op jit(solution)/shard_map/ppermute | solution.py:428
  48.9 2.8 %collective-permute-done.2.prev_ref = bf16[128,256]{1,0:T(8,128)(2,1)S(1)} collective-permute-done((bf16[128,256]{1,0:T(8,128)(2,1)S(1)}, bf16[128,256]{1,0:T(8,128)(2,1)S(1)}, u32[]{:S(2)}, u32[]{:S(2)}) %collective-permute-start.2) | collective-permute-done | bytes 65568 | tf_op jit(solution)/shard_map/ppermute | solution.py:428
  51.7 0.7 %copy-done.9 = s32[16,20]{1,0:T(8,128)S(1)} copy-done((s32[16,20]{1,0:T(8,128)S(1)}, s32[16,20]{1,0:T(8,128)}, u32[]{:S(2)}) %copy-start.9) | copy-done | bytes 1304
  52.4 3.5 %near_give.1 = (f32[256,256]{1,0:T(8,128)S(1)}, bf16[16,3072]{1,0:T(8,128)(2,1)}) custom-call(s32[16,20]{1,0:T(8,128)S(1)} %get-tuple-element.14.at_ref, s32[16,20]{1,0:T(8,128)S(1)} %copy-done.9, bf16[128,256]{1,0:T(8,128)(2,1)S(1)} %get-tuple-element.22.lo_ref, bf16[128,256]{1,0:T(8,128)(2,1)S(1)} %get-tuple-element.23.hi_ref, ...), custom_call_target="tpu_custom_call" | custom-call | bytes 12000000 | tf_op jit(solution)/shard_map/near_give/pallas_call | solution.py:34
  55.9 0.7 %copy-done.6 = f32[256,256]{1,0:T(8,128)} copy-done((f32[256,256]{1,0:T(8,128)}, f32[256,256]{1,0:T(8,128)S(1)}, u32[]{:S(2)}) %copy-start.6) | copy-done | bytes 262168
  56.6 1.2 %copy-done.2 = bf16[512,1024]{1,0:T(8,128)(2,1)S(1)} copy-done((bf16[512,1024]{1,0:T(8,128)(2,1)S(1)}, bf16[512,1024]{1,0:T(8,128)(2,1)}, u32[]{:S(2)}) %copy-start.2) | copy-done | bytes 1048600
  57.8 0.9 %copy-done.7 = f32[256,256]{1,0:T(8,128)S(1)} copy-done((f32[256,256]{1,0:T(8,128)S(1)}, f32[256,256]{1,0:T(8,128)}, u32[]{:S(2)}) %copy-start.7) | copy-done | bytes 262168
  58.8 2.9 %far_last.1 = bf16[16,3072]{1,0:T(8,128)(2,1)} custom-call(s32[16,32]{1,0:T(8,128)S(1)} %get-tuple-element.16.idx_ref, bf16[16,64,128]{2,1,0:T(8,128)(2,1)} %all-to-all-done.1.got_ref, bf16[512,1024]{1,0:T(8,128)(2,1)S(1)} %copy-done.2, bf16[512,256]{1,0:T(8,128)(2,1)S(1)} %get-tuple-element.19.basis_ref, f32[256,256]{1,0:T(8,128)S(1)} %copy-done.7), custom_call_target="tpu_custom_call" | custom-call | tf_op jit(solution)/shard_map/far_last/pallas_call | solution.py:34
  (18 shorter events, 0.9 us)
Async XLA Ops:
  3.2 25.9 %all-to-all-start = ((bf16[16,64,128]{2,1,0:T(8,128)(2,1)}), bf16[16,64,128]{2,1,0:T(8,128)(2,1)}, u32[]{:S(2)}, u32[]{:S(2)}) async-start(bf16[16,64,128]{2,1,0:T(8,128)(2,1)} %project.2), calls=%async_computation | async-start | bytes 524288 | tf_op jit(solution)/shard_map/all_to_all | solution.py:431
  14.7 7.9 %collective-permute-start.1 = (bf16[128,256]{1,0:T(8,128)(2,1)S(1)}, bf16[128,256]{1,0:T(8,128)(2,1)}, u32[]{:S(2)}, u32[]{:S(2)}) collective-permute-start(bf16[128,256]{1,0:T(8,128)(2,1)S(1)} %get-tuple-element.17.lo_ref), channel_id=1, source_target_pairs={{16,0},{32,16},{48,32},{64,48},{80,64},{96,80},{112,96},{128,112},... | collective-permute-start | bytes 196616 | tf_op jit(solution)/shard_map/ppermute | solution.py:428
  16.8 7.9 %collective-permute-start = (bf16[128,256]{1,0:T(8,128)(2,1)S(1)}, bf16[128,256]{1,0:T(8,128)(2,1)}, u32[]{:S(2)}, u32[]{:S(2)}) collective-permute-start(bf16[128,256]{1,0:T(8,128)(2,1)S(1)} %get-tuple-element.18.hi_ref), channel_id=1, source_target_pairs={{0,16},{16,32},{32,48},{48,64},{64,80},{80,96},{96,112},{112,128},... | collective-permute-start | bytes 196616 | tf_op jit(solution)/shard_map/ppermute | solution.py:428
  16.8 0.7 %copy-start.10 = (s32[16]{0:T(128)S(1)}, s32[16]{0:T(128)}, u32[]{:S(2)}) copy-start(s32[16]{0:T(128)} %count_ref.1) | copy-start | bytes 196
  21.6 1.0 %copy-start = (bf16[512,1024]{1,0:T(8,128)(2,1)}, bf16[512,1024]{1,0:T(8,128)(2,1)S(1)}, u32[]{:S(2)}) copy-start(bf16[512,1024]{1,0:T(8,128)(2,1)S(1)} %get-tuple-element.20.mat_ref) | copy-start | bytes 3145732
  27.8 0.7 %copy-start.3 = (f32[256,256]{1,0:T(8,128)}, f32[256,256]{1,0:T(8,128)S(1)}, u32[]{:S(2)}) copy-start(f32[256,256]{1,0:T(8,128)S(1)} %near.1.near_ref) | copy-start | bytes 786436
  28.5 0.6 copy-start.8
  29.1 1.2 %copy-start.1 = (bf16[512,1024]{1,0:T(8,128)(2,1)S(1)}, bf16[512,1024]{1,0:T(8,128)(2,1)}, u32[]{:S(2)}) copy-start(bf16[512,1024]{1,0:T(8,128)(2,1)} %copy-done) | copy-start | bytes 3145732
  30.3 0.9 %copy-start.4 = (f32[256,256]{1,0:T(8,128)S(1)}, f32[256,256]{1,0:T(8,128)}, u32[]{:S(2)}) copy-start(f32[256,256]{1,0:T(8,128)} %copy-done.3) | copy-start | bytes 786436
  33.7 0.7 %copy-start.5 = (bf16[16,64,128]{2,1,0:T(8,128)(2,1)}, bf16[16,64,128]{2,1,0:T(8,128)(2,1)S(1)}, u32[]{:S(2)}) copy-start(bf16[16,64,128]{2,1,0:T(8,128)(2,1)S(1)} %project.3) | copy-start | bytes 786436
  34.4 22.2 %all-to-all-start.1 = ((bf16[16,64,128]{2,1,0:T(8,128)(2,1)}), bf16[16,64,128]{2,1,0:T(8,128)(2,1)}, u32[]{:S(2)}, u32[]{:S(2)}) async-start(bf16[16,64,128]{2,1,0:T(8,128)(2,1)} %copy-done.5), calls=%async_computation.1 | async-start | bytes 524288 | tf_op jit(solution)/shard_map/all_to_all | solution.py:431
  43.3 5.6 %collective-permute-start.3 = (bf16[128,256]{1,0:T(8,128)(2,1)S(1)}, bf16[128,256]{1,0:T(8,128)(2,1)S(1)}, u32[]{:S(2)}, u32[]{:S(2)}) collective-permute-start(bf16[128,256]{1,0:T(8,128)(2,1)S(1)} %get-tuple-element.22.lo_ref), channel_id=1, source_target_pairs={{16,0},{32,16},{48,32},{64,48},{80,64},{96,80},{112,96},{128,112},... | collective-permute-start | bytes 196616 | tf_op jit(solution)/shard_map/ppermute | solution.py:428
  45.2 6.4 %collective-permute-start.2 = (bf16[128,256]{1,0:T(8,128)(2,1)S(1)}, bf16[128,256]{1,0:T(8,128)(2,1)S(1)}, u32[]{:S(2)}, u32[]{:S(2)}) collective-permute-start(bf16[128,256]{1,0:T(8,128)(2,1)S(1)} %get-tuple-element.23.hi_ref), channel_id=1, source_target_pairs={{0,16},{16,32},{32,48},{48,64},{64,80},{80,96},{96,112},{112,128},... | collective-permute-start | bytes 196616 | tf_op jit(solution)/shard_map/ppermute | solution.py:428
  51.7 0.7 %copy-start.9 = (s32[16,20]{1,0:T(8,128)S(1)}, s32[16,20]{1,0:T(8,128)}, u32[]{:S(2)}) copy-start(s32[16,20]{1,0:T(8,128)} %copy-done.8) | copy-start | bytes 3844
  55.9 0.7 %copy-start.6 = (f32[256,256]{1,0:T(8,128)}, f32[256,256]{1,0:T(8,128)S(1)}, u32[]{:S(2)}) copy-start(f32[256,256]{1,0:T(8,128)S(1)} %get-tuple-element.25.near_ref) | copy-start | bytes 786436
  56.6 1.2 %copy-start.2 = (bf16[512,1024]{1,0:T(8,128)(2,1)S(1)}, bf16[512,1024]{1,0:T(8,128)(2,1)}, u32[]{:S(2)}) copy-start(bf16[512,1024]{1,0:T(8,128)(2,1)} %copy-done) | copy-start | bytes 3145732
  57.8 0.9 %copy-start.7 = (f32[256,256]{1,0:T(8,128)S(1)}, f32[256,256]{1,0:T(8,128)}, u32[]{:S(2)}) copy-start(f32[256,256]{1,0:T(8,128)} %copy-done.6) | copy-start | bytes 786436

commit v3 on v2

v3 whole, which is shorter than its diff:
```python
import functools

import jax
import jax.numpy as jnp
from jax import lax
from jax.experimental import pallas as pl
from jax.experimental.pallas import tpu as pltpu
from jax.sharding import PartitionSpec as P

TILE = 192
RHS = 16
RANK = 32
RIM = 8
LANES = 128
WIDE = 256
GROUP = 8
LONG = 1_000_000_000_000
STEPS = 2
SIDE = LANES // RANK

VMEM = pl.BlockSpec(memory_space=pltpu.VMEM)
SMEM = pl.BlockSpec(memory_space=pltpu.SMEM)
HBM = pl.BlockSpec(memory_space=pltpu.HBM)
ANY = pl.BlockSpec(memory_space=pl.ANY)
F32 = jnp.float32
BF16 = jnp.bfloat16
NT = (((1,), (1,)), ((), ()))
NN = (((1,), (0,)), ((), ()))
shape = jax.ShapeDtypeStruct


def call(kernel, name, args, ins, outs, scratch, mib, moved=0):
    args = [
        pltpu.with_memory_space_constraint(a, pltpu.HBM) if s is HBM else a
        for a, s in zip(args, ins)
    ]
    return pl.pallas_call(
        kernel,
        out_shape=tuple(pltpu.HBM(o.shape, o.dtype) if s is HBM else o for o, s in outs),
        in_specs=ins,
        out_specs=tuple(s for _, s in outs),
        scratch_shapes=scratch,
        compiler_params=pltpu.CompilerParams(vmem_limit_bytes=mib * 1024 * 1024),
        cost_estimate=pl.CostEstimate(flops=100 * moved, bytes_accessed=moved, transcendentals=0),
        name=name,
    )(*args)


def copies(pairs, sems, first=0):
    return [
        pltpu.make_async_copy(source, to, sems.at[first + j]) for j, (source, to) in enumerate(pairs)
    ]


def start(group):
    for copy in group:
        copy.start()


def wait(group):
    for copy in group:
        copy.wait()


def iota(shape, axis):
    return lax.broadcasted_iota(jnp.int32, shape, axis)


def swap(rows, outer):
    at = iota((rows, rows), 0)
    source = (at % outer) * (rows // outer) + at // outer
    return (iota((rows, rows), 1) == source).astype(BF16)


def turn(x):
    return pltpu.roll(x, LANES // 2, 1)


def halves(pair):
    low = iota((pair.shape[0], LANES), 1) < LANES // 2
    one, two, three = (pair[:, j * LANES : (j + 1) * LANES] for j in range(3))
    two_turned, three_turned = turn(two), turn(three)
    zero = jnp.zeros_like(two)
    return (
        (one, jnp.where(low, two, zero)),
        (jnp.where(low, two_turned, three_turned), jnp.where(low, three_turned, zero)),
    )


def spread(source_ref, scratch, rows, count, late=None):
    size = rows * count
    for j in range(0, count, 2):
        pair = source_ref[:, j * TILE : (j + 2) * TILE].astype(F32)
        if late is not None:
            pair = jnp.where(late, pair[rows:], pair[:rows])
        for k, parts in enumerate(halves(pair)):
            for side, part in enumerate(parts):
                scratch[pl.ds(side * size + j + k, rows, stride=count), :] = part


def gather_sides(scratch, y_ref, blocks):
    size = blocks * RHS
    low = iota((blocks, LANES), 1) < LANES // 2
    for h in range(0, RHS, 2):
        one, two, three, four = (
            scratch[pl.ds(side * size + h + k, blocks, stride=RHS), :]
            for k in range(2)
            for side in range(2)
        )
        three, four = turn(three), turn(four)
        pair = (one, jnp.where(low, two, three), jnp.where(low, three, four))
        for j in range(3):
            at = h * TILE + j * LANES
            y_ref[:, at : at + LANES] = pair[j].astype(BF16)


def join(scratch, size):
    return jnp.concatenate(
        [scratch[side * size : (side + 1) * size, :].astype(BF16) for side in range(2)], axis=1
    )


def project(fields, basis_ref, coef_s):
    cols = GROUP * RANK
    lane = iota((RHS, LANES), 1) // RANK
    for g, field in enumerate(fields):
        cross = lax.dot_general(
            field, basis_ref[g * cols : (g + 1) * cols, :], NT, preferred_element_type=F32
        )
        for half in range(GROUP // SIDE):
            out = None
            for j in range(SIDE):
                at = (half * SIDE + j) * RHS
                part = cross[at : at + RHS, half * LANES : (half + 1) * LANES]
                out = part if out is None else jnp.where(lane == j, part, out)
            at = (g * (GROUP // SIDE) + half) * RHS
            for j in range(coef_s.shape[0]):
                coef_s[j, at : at + RHS, :] = out.astype(BF16)


def opening_kernel(
    v_hbm, b_hbm, lo_ref, hi_ref, basis_ref, coef_hbm, v_s, b_s, f_s, g_s, coef_s, sems
):
    gets = copies(((v_hbm, v_s), (b_hbm, b_s)), sems)
    put = copies(((coef_s, coef_hbm),), sems, 2)
    start(gets)
    blocks = v_s.shape[0]
    rows, ranks = blocks * RHS, blocks * RANK
    gets[0].wait()
    spread(v_s, f_s, blocks, RHS)
    field = join(f_s, rows)
    rim = RIM * RHS
    lo_ref[...] = field[:rim]
    hi_ref[...] = field[rim:]
    gets[1].wait()
    spread(b_s, g_s, blocks, RANK)
    basis_ref[...] = join(g_s, ranks)
    project((field[:rim], field[rim:]), basis_ref, coef_s)
    start(put)
    wait(put)


def place(at_s, kind_s, e_s, p_s, unroll):
    blocks, slots = at_s.shape

    def one_block(i, _):
        row = pl.multiple_of(i * RHS, RHS)
        for k in range(slots):
            source = pl.multiple_of(at_s[i, k], RHS)
            column = pl.multiple_of(kind_s[i, k], WIDE)
            p_s[pl.ds(row, RHS), pl.ds(column, WIDE)] = e_s[pl.ds(source, RHS), :]
        return 0

    lax.fori_loop(0, blocks, one_block, 0, unroll=unroll)


def multiply(p_s, table_s, out_ref, chunk):
    size, columns = out_ref.shape[0], table_s.shape[1]
    out_ref[:, LANES:] = jnp.zeros((size, LANES), F32)

    def some_columns(n, total):
        at = pl.multiple_of(n * chunk, chunk)
        return total + lax.dot_general(
            p_s[:, pl.ds(at, chunk)], table_s[:, pl.ds(at, chunk)], NT, preferred_element_type=F32
        )

    total = jnp.zeros((size, TILE), F32)
    out_ref[:, :TILE] = lax.fori_loop(0, columns // chunk, some_columns, total)


def first_near_kernel(
    slabs, slab_blocks,
    count_hbm, src_hbm, type_hbm, far_hbm, tiles_hbm, coup_hbm, lo_ref, hi_ref, chip_ref, further_ref,
    near_ref, mat_ref, table_hbm, far_idx_hbm, at_hbm, kind_hbm,
    count_s, src_s, type_s, far_s, tiles_s, coup_s, far_idx_s, at_v, kind_v, at_s, kind_s,
    h_s, e_s, p_s, table_s, sems,
):
    gets = copies(
        (
            (count_hbm, count_s),
            (src_hbm, src_s),
            (type_hbm, type_s),
            (far_hbm, far_s),
            (coup_hbm, coup_s),
            (tiles_hbm, tiles_s),
        ),
        sems,
    )
    puts = copies(
        (
            (at_v, at_s),
            (kind_v, kind_s),
            (at_v, at_hbm),
            (kind_v, kind_hbm),
            (far_idx_s, far_idx_hbm),
        ),
        sems,
        len(gets),
    )
    start(gets)
    types = tiles_s.shape[0]
    blocks, partners, _ = coup_s.shape
    deep = partners // SIDE
    size, rim = blocks * RHS, RIM * RHS
    me = lax.axis_index("slab")
    odd = me % 2 == 1

    p_s[:, : types * WIDE] = jnp.zeros((size, types * WIDE), BF16)
    e_s[:rim, :] = lo_ref[...]
    e_s[rim : 2 * rim, :] = hi_ref[...]
    for j, (ref, late) in enumerate(((chip_ref, odd), (further_ref, ~odd))):
        spread(ref, h_s, RIM, RHS, late)
        e_s[(2 + j) * rim : (3 + j) * rim, :] = join(h_s, rim)

    wait(gets[:4])
    source = src_s[...]
    step = (source // slab_blocks - me + slabs) % slabs
    after = jnp.where(odd, 3 * RIM, 2 * RIM)
    before = jnp.where(odd, RIM, 2 * RIM)
    offset = jnp.where(step == 0, 0, jnp.where(step == 1, after, before))
    at_v[...] = (source % blocks + offset) * RHS
    row = iota(source.shape, 0)
    count = jnp.zeros(source.shape, jnp.int32)
    for i in range(blocks):
        count = jnp.where(row == i, count_s[i], count)
    kind_v[...] = jnp.where(iota(source.shape, 1) < count, type_s[...], types) * WIDE

    source = far_s[...] % slab_blocks
    group = iota(source.shape, 1) // deep
    turned = (group - source) & (SIDE - 1)
    far_idx_s[...] = (turned * (slab_blocks // SIDE) + source // SIDE) * RHS
    start(puts)

    lane = iota((deep, LANES), 1) // RANK
    order = swap(RANK * deep, RANK)
    gets[4].wait()

    def two_blocks(n, _):
        stacks = []
        for b in range(2):
            i = 2 * n + b
            stack = []
            for big in range(RANK // SIDE):
                x = coup_s[i, :, big * LANES : (big + 1) * LANES].astype(F32)
                parts = [x[j * deep : (j + 1) * deep] for j in range(SIDE)]
                turned = [
                    [p if r == 0 else pltpu.roll(p, r * RANK, 1) for r in range(SIDE)]
                    for p in parts
                ]
                for small in range(SIDE):
                    out = turned[0][-small % SIDE]
                    for j in range(1, SIDE):
                        out = jnp.where(lane == j, turned[j][(j - small) % SIDE], out)
                    stack.append(out)
            stacks.append(jnp.concatenate(stack, axis=0).astype(BF16))
        both = jnp.concatenate(stacks, axis=1)
        both = lax.dot_general(order, both, NN, preferred_element_type=F32).astype(BF16)
        for b in range(2):
            at = pl.multiple_of((2 * n + b) * RANK, RANK)
            for k in range(deep):
                part = both[k * RANK : (k + 1) * RANK, b * LANES : (b + 1) * LANES]
                mat_ref[pl.ds(at, RANK), k * LANES : (k + 1) * LANES] = part
        return 0

    lax.fori_loop(0, blocks // 2, two_blocks, 0, unroll=True)

    wait(puts[:2])
    place(at_s, kind_s, e_s, p_s, True)

    many = 16
    order = swap(many * many, many)
    gets[5].wait()

    low = iota((many, LANES), 1) < LANES // 2
    steps = STEPS
    each = TILE // steps
    put_table = [
        copies(((table_s.at[rows], table_hbm.at[rows]),), sems, 11 + n)
        for n, rows in enumerate(pl.ds(n * each, each) for n in range(steps))
    ]

    def some_rows(step, _):
        for n in range(each // many):
            at = pl.multiple_of(step * (each * TILE), LANES) + n * many * TILE
            for a in range(types // many):
                stack = []
                for d in range(0, many, 2):
                    one, two, three = (
                        tiles_s[a * many : (a + 1) * many, pl.ds(at + d * TILE + j * LANES, LANES)]
                        for j in range(3)
                    )
                    two_turned, three_turned = turn(two), turn(three)
                    stack.append(jnp.concatenate((one, two), axis=1))
                    mixed = jnp.where(low, two_turned, three_turned)
                    stack.append(jnp.concatenate((mixed, three_turned), axis=1))
                out = jnp.concatenate(stack, axis=0)
                out = lax.dot_general(order, out, NN, preferred_element_type=F32).astype(BF16)
                for t in range(many):
                    to = (a * many + t) * WIDE
                    row = pl.multiple_of(step * each + n * many, many)
                    table_s[pl.ds(row, many), to : to + WIDE] = out[t * many : (t + 1) * many]
        rows = pl.ds(pl.multiple_of(step * each, many), each)
        start(copies(((table_s.at[rows], table_hbm.at[rows]),), sems, 11 + step))
        return 0

    lax.fori_loop(0, steps, some_rows, 0)
    multiply(p_s, table_s, near_ref, table_s.shape[1] // 2)
    wait(puts[2:])
    for put in put_table:
        wait(put)


def second_near_kernel(
    at_hbm, kind_hbm, lo_ref, hi_ref, chip_ref, further_ref, table_hbm,
    near_ref, y_hbm,
    at_s, kind_s, e_s, p_s, table_s, f_s, y_s, sems,
):
    gets = copies(((at_hbm, at_s), (kind_hbm, kind_s), (table_hbm, table_s)), sems)
    put = copies(((y_s, y_hbm),), sems, len(gets))
    start(gets)
    blocks = at_s.shape[0]
    size, rim = blocks * RHS, RIM * RHS
    for j, ref in enumerate((lo_ref, hi_ref, chip_ref, further_ref)):
        e_s[j * rim : (j + 1) * rim, :] = ref[...]
    for j in range(2):
        f_s[j * size : (j + 1) * size, :] = e_s[:size, j * LANES : (j + 1) * LANES].astype(F32)
    gather_sides(f_s, y_s, blocks)
    start(put)
    columns = table_s.shape[1]
    p_s[:, :columns] = jnp.zeros((size, columns), BF16)
    wait(gets[:2])
    place(at_s, kind_s, e_s, p_s, True)
    gets[2].wait()
    multiply(p_s, table_s, near_ref, table_s.shape[1])
    wait(put)


def far_kernel(last, idx_hbm, got_any, mat_ref, basis_ref, near_ref, *rest):
    if last:
        y_ref, idx_s, got_ref, turn_s, pick_s, sem, sum_s = rest
    else:
        lo_ref, hi_ref, chip_ref, further_ref, coef_hbm, idx_s, got_ref, turn_s, pick_s, sem, coef_s = rest
        put = copies(((coef_s, coef_hbm),), sem, 2)
    gets = copies(((got_any, got_ref), (idx_hbm, idx_s)), sem)
    start(gets)
    gets[0].wait()
    blocks, partners = idx_s.shape
    deep = partners // SIDE
    peers, packed_rows, _ = got_ref.shape
    quarter = peers * packed_rows
    for j in range(peers):
        got = got_ref[j]
        for r in range(SIDE):
            at = r * quarter + j * packed_rows
            turn_s[at : at + packed_rows, :] = got if r == 0 else pltpu.roll(got, r * RANK, 1)
    lane = iota((RHS, LANES), 1) // RANK
    gets[1].wait()

    def one_block(i, _):
        row = pl.multiple_of(i * RHS, RHS)
        for k in range(deep):
            out = None
            for j in range(SIDE):
                at = pl.multiple_of(idx_s[i, j * deep + k], RHS)
                part = turn_s[pl.ds(at, RHS), :]
                out = part if out is None else jnp.where(lane == j, part, out)
            pick_s[pl.ds(row, RHS), k * LANES : (k + 1) * LANES] = out
        return 0

    lax.fori_loop(0, blocks, one_block, 0, unroll=True)
    size = blocks * RHS
    rows, cols = GROUP * RHS, GROUP * RANK
    own = iota((rows, cols), 0) // RHS == iota((rows, cols), 1) // RANK
    fields = []
    for g in range(blocks // GROUP):
        cross = lax.dot_general(
            pick_s[g * rows : (g + 1) * rows, :],
            mat_ref[g * cols : (g + 1) * cols, :],
            NT,
            preferred_element_type=F32,
        )
        mix = jnp.where(own, cross, 0.0).astype(BF16)
        far = lax.dot_general(
            mix, basis_ref[g * cols : (g + 1) * cols, :], NN, preferred_element_type=F32
        )
        total = near_ref[g * rows : (g + 1) * rows, :] + far
        if last:
            for j in range(2):
                at = j * size + g * rows
                sum_s[at : at + rows, :] = total[:, j * LANES : (j + 1) * LANES]
        else:
            fields.append(total.astype(BF16))
    if last:
        gather_sides(sum_s, y_ref, blocks)
    else:
        project(fields, basis_ref, coef_s)
        start(put)
        lo_ref[...], hi_ref[...] = lo, hi = fields
        odd = lax.axis_index("slab") % 2 == 1
        chip_ref[...] = jnp.where(odd, lo, hi)
        further_ref[...] = jnp.where(odd, hi, lo)
        wait(put)


def opening(peers, vectors, bases):
    blocks = vectors.shape[0]
    rows, ranks, rim = blocks * RHS, blocks * RANK, RIM * RHS
    field = (shape((rim, WIDE), BF16), VMEM)
    coef = (peers, rows // SIDE, LANES)
    return call(
        opening_kernel, "opening", (vectors, bases), [HBM] * 2,
        [field, field, (shape((ranks, WIDE), BF16), VMEM), (shape(coef, BF16), HBM)],
        [
            pltpu.VMEM(vectors.shape, BF16),
            pltpu.VMEM(bases.shape, BF16),
            pltpu.VMEM((2 * rows, LANES), F32),
            pltpu.VMEM((2 * ranks, LANES), F32),
            pltpu.VMEM(coef, BF16),
            pltpu.SemaphoreType.DMA((3,)),
        ],
        8,
    )


def first_near(
    slabs, peers, near_count, near_src, near_type, far_src, tiles, coupling, lo, hi, chip, further
):
    blocks, partners, _ = coupling.shape
    rows, rim = blocks * RHS, RIM * RHS
    types = tiles.shape[0]
    table = (TILE, types * WIDE)
    slots = (near_src.shape, jnp.int32)
    picks = (far_src.shape, jnp.int32)
    return call(
        functools.partial(first_near_kernel, slabs, blocks * peers), "first_near",
        (near_count, near_src, near_type, far_src, tiles, coupling, lo, hi, chip, further),
        [HBM] * 6 + [VMEM] * 4,
        [
            (shape((rows, WIDE), F32), VMEM),
            (shape((blocks * RANK, partners * RANK), BF16), VMEM),
            (shape(table, BF16), HBM),
            (shape(*picks), HBM),
            (shape(*slots), HBM),
            (shape(*slots), HBM),
        ],
        [
            pltpu.SMEM(near_count.shape, jnp.int32),
            pltpu.VMEM(*slots),
            pltpu.VMEM(*slots),
            pltpu.VMEM(*picks),
            pltpu.VMEM(tiles.shape, BF16),
            pltpu.VMEM(coupling.shape, BF16),
            pltpu.VMEM(*picks),
            pltpu.VMEM(*slots),
            pltpu.VMEM(*slots),
            pltpu.SMEM(*slots),
            pltpu.SMEM(*slots),
            pltpu.VMEM((2 * rim, LANES), F32),
            pltpu.VMEM((4 * rim, WIDE), BF16),
            pltpu.VMEM((rows, (types + 1) * WIDE), BF16),
            pltpu.VMEM(table, BF16),
            pltpu.SemaphoreType.DMA((11 + STEPS,)),
        ],
        20, LONG,
    )


def second_near(at, kind, lo, hi, chip, further, table):
    rim = lo.shape[0]
    rows = 2 * rim
    y = (rows // RHS, RHS * TILE)
    return call(
        second_near_kernel, "second_near", (at, kind, lo, hi, chip, further, table),
        [HBM] * 2 + [VMEM] * 4 + [HBM],
        [(shape((rows, WIDE), F32), VMEM), (shape(y, BF16), HBM)],
        [
            pltpu.SMEM(at.shape, jnp.int32),
            pltpu.SMEM(at.shape, jnp.int32),
            pltpu.VMEM((2 * rows, WIDE), BF16),
            pltpu.VMEM((rows, table.shape[1] + WIDE), BF16),
            pltpu.VMEM(table.shape, BF16),
            pltpu.VMEM((2 * rows, LANES), F32),
            pltpu.VMEM(y, BF16),
            pltpu.SemaphoreType.DMA((4,)),
        ],
        16, 12_000_000,
    )


def far(last, idx, got, mat, basis, near_term):
    rows = near_term.shape[0]
    peers, packed, _ = got.shape
    scratch = [
        pltpu.SMEM(idx.shape, jnp.int32),
        pltpu.VMEM(got.shape, BF16),
        pltpu.VMEM((SIDE * peers * packed, LANES), BF16),
        pltpu.VMEM((rows, mat.shape[1]), BF16),
        pltpu.SemaphoreType.DMA((3,)),
    ]
    if last:
        outs = [(shape((rows // RHS, RHS * TILE), BF16), VMEM)]
        scratch.append(pltpu.VMEM((2 * rows, LANES), F32))
    else:
        outs = [(shape((rows // 2, WIDE), BF16), VMEM)] * 4 + [(shape(got.shape, BF16), HBM)]
        scratch.append(pltpu.VMEM(got.shape, BF16))
    return call(
        functools.partial(far_kernel, last), "far_last" if last else "far",
        (idx, got, mat, basis, near_term), [HBM, ANY] + [VMEM] * 3, outs, scratch, 8,
    )


def per_device(vectors, tiles, near_src, near_type, near_count, bases, far_src, coupling):
    slabs, peers = lax.axis_size("slab"), lax.axis_size("grp")
    chips = [(i, i ^ 1) for i in range(slabs)]
    between = [(i, (i + 1 if i % 2 else i - 1) % slabs) for i in range(slabs)]

    def halo(chip, further):
        return lax.ppermute(chip, "slab", chips), lax.ppermute(further, "slab", between)

    def exchange(coef):
        return lax.all_to_all(coef, "grp", 0, 0, tiled=True)

    chip, further = halo(vectors, vectors)
    lo, hi, basis, coef = opening(peers, vectors, bases)
    got = exchange(coef)
    near_term, mat, table, idx, at, kind = first_near(
        slabs, peers, near_count, near_src, near_type, far_src, tiles, coupling, lo, hi, chip, further
    )
    lo, hi, chip, further, coef = far(False, idx, got, mat, basis, near_term)
    got = exchange(coef)
    chip, further = halo(chip, further)
    near_term, first = second_near(at, kind, lo, hi, chip, further, table)
    (second,) = far(True, idx, got, mat, basis, near_term)
    return (first, second)


def solution(mesh):
    in_specs = (
        P(("slab", "grp"), None),
        P(),
        P(("slab", "grp"), None),
        P(("slab", "grp"), None),
        P(("slab", "grp")),
        P(("slab", "grp"), None),
        P(("slab", "grp"), None),
        P(("slab", "grp"), None, None),
    )
    out_specs = (P(("slab", "grp"), None), P(("slab", "grp"), None))
    return jax.shard_map(
        per_device, mesh=mesh, in_specs=in_specs, out_specs=out_specs, check_vma=False
    )
```

time: 62.3 us -> 52.9 us (0.85)
  the two profiles are of different devices: /device:TPU:8 before, /device:TPU:32 now
where the time goes in v3:
time: 52.9 us; the launch traced here: 52.4 us
  starting transfers between devices  17.8 us (34%)
  Pallas kernels  17.8 us (34%)
  waiting for transfers between devices  16.1 us (30%)
  between operations  0.7 us (1%)
    pallas_call x5, Pallas kernels, call(): pl.pallas_call(kernel, out_shape=tuple((pltpu.HBM(o.shape, o.dtype) if s...  17.8 us
    all_to_all x2, starting transfers between devices, exchange(): return lax.all_to_all(coef, 'grp', 0, 0, tiled=True)  14.8 us
    all_to_all x2, waiting for transfers between devices, exchange(): return lax.all_to_all(coef, 'grp', 0, 0, tiled=True)  10.2 us
    ppermute x2, waiting for transfers between devices, halo(): lax.ppermute(further, 'slab', between)  5.78 us
    ppermute x2, starting transfers between devices, halo(): lax.ppermute(further, 'slab', between)  2.93 us
  transfers between devices with their start and end apart: 6, of which 4 were waited for; matrix products, arithmetic and copies ran while one was open for 0% of the time, Pallas kernels for 23%

profile of v3, /device:TPU:32, one launch (start us, length us, event | category | flops | bytes accessed | tf_op | source)
XLA Modules:
  0.0 52.4 jit_solution(3516496016790630931)
XLA Ops:
  0.6 1.8 %collective-permute-start.1 = (bf16[16,3072]{1,0:T(8,128)(2,1)}, bf16[16,3072]{1,0:T(8,128)(2,1)S(1)}, u32[]{:S(2)}, u32[]{:S(2)}) collective-permute-start(bf16[16,3072]{1,0:T(8,128)(2,1)} %v_hbm.1), channel_id=1, source_target_pairs={{0,240},{16,32},{32,16},{48,64},{64,48},{80,96},{96,80},{112,128},... | collective-permute-start | bytes 294920 | tf_op jit(solution)/shard_map/ppermute | solution.py:538
  2.5 0.0 collective-permute-start
  2.5 2.6 %opening.1 = (bf16[128,256]{1,0:T(8,128)(2,1)S(1)}, bf16[128,256]{1,0:T(8,128)(2,1)S(1)}, bf16[512,256]{1,0:T(8,128)(2,1)S(1)}, bf16[16,64,128]{2,1,0:T(8,128)(2,1)}) custom-call(bf16[16,3072]{1,0:T(8,128)(2,1)} %v_hbm.1, bf16[16,6144]{1,0:T(8,128)(2,1)} %b_hbm.1), custom_call_target="tpu_custom_call" | custom-call | tf_op jit(solution)/shard_map/opening/pallas_call | solution.py:37
  5.1 11.3 %all-to-all-start = ((bf16[16,64,128]{2,1,0:T(8,128)(2,1)}), bf16[16,64,128]{2,1,0:T(8,128)(2,1)}, u32[]{:S(2)}, u32[]{:S(2)}) async-start(bf16[16,64,128]{2,1,0:T(8,128)(2,1)} %get-tuple-element.24), calls=%async_computation | async-start | bytes 524288 | tf_op jit(solution)/shard_map/all_to_all | solution.py:541
  16.3 0.0 collective-permute-done.1.further_ref
  16.3 0.0 collective-permute-done.chip_ref
  16.4 6.2 %first_near.1 = (f32[256,256]{1,0:T(8,128)S(1)}, bf16[512,1024]{1,0:T(8,128)(2,1)S(1)}, bf16[192,8192]{1,0:T(8,128)(2,1)}, s32[16,32]{1,0:T(8,128)}, s32[16,20]{1,0:T(8,128)}, /*index=5*/s32[16,20]{1,0:T(8,128)}) custom-call(s32[16]{0:T(128)} %count_hbm.1, s32[16,20]{1,0:T(8,128)} %src_hbm.1, s32[16,20]{1,0:T(8,128)} %type_hbm.1, s32[16,32]{1,0:T(8,128)} %far_hbm.1, ...), custom_call_target="tpu_custom_call" | custom-call | flops 100000000376832 | bytes 999999995904 | tf_op jit(solution)/shard_map/first_near/pallas_call | solution.py:37
  22.5 7.9 %all-to-all-done.got_any = bf16[16,64,128]{2,1,0:T(8,128)(2,1)} async-done(((bf16[16,64,128]{2,1,0:T(8,128)(2,1)}), bf16[16,64,128]{2,1,0:T(8,128)(2,1)}, u32[]{:S(2)}, u32[]{:S(2)}) %all-to-all-start) | async-done | bytes 262176 | tf_op jit(solution)/shard_map/all_to_all | solution.py:541
  30.4 3.2 %far.1 = (bf16[128,256]{1,0:T(8,128)(2,1)S(1)}, bf16[128,256]{1,0:T(8,128)(2,1)S(1)}, bf16[128,256]{1,0:T(8,128)(2,1)S(1)}, bf16[128,256]{1,0:T(8,128)(2,1)S(1)}, bf16[16,64,128]{2,1,0:T(8,128)(2,1)}) custom-call(s32[16,32]{1,0:T(8,128)} %get-tuple-element.23.idx_hbm, bf16[16,64,128]{2,1,0:T(8,128)(2,1)} %all-to-all-done.got_any, ...), custom_call_target="tpu_custom_call" | custom-call | tf_op jit(solution)/shard_map/far/pallas_call | solution.py:37
  33.6 3.5 %all-to-all-start.1 = ((bf16[16,64,128]{2,1,0:T(8,128)(2,1)}), bf16[16,64,128]{2,1,0:T(8,128)(2,1)S(1)}, u32[]{:S(2)}, u32[]{:S(2)}) async-start(bf16[16,64,128]{2,1,0:T(8,128)(2,1)} %get-tuple-element.34), calls=%async_computation.1 | async-start | bytes 524288 | tf_op jit(solution)/shard_map/all_to_all | solution.py:541
  37.1 0.1 collective-permute-start.2
  37.2 1.1 %collective-permute-start.3 = (bf16[128,256]{1,0:T(8,128)(2,1)S(1)}, bf16[128,256]{1,0:T(8,128)(2,1)S(1)}, u32[]{:S(2)}, u32[]{:S(2)}) collective-permute-start(bf16[128,256]{1,0:T(8,128)(2,1)S(1)} %get-tuple-element.31), channel_id=1, source_target_pairs={{0,240},{16,32},{32,16},{48,64},{64,48},{80,96},{96,80},{112,128},... | collective-permute-start | bytes 196616 | tf_op jit(solution)/shard_map/ppermute | solution.py:538
  38.3 0.1 collective-permute-done.2.chip_ref
  38.5 5.8 %collective-permute-done.3.further_ref = bf16[128,256]{1,0:T(8,128)(2,1)S(1)} collective-permute-done((bf16[128,256]{1,0:T(8,128)(2,1)S(1)}, bf16[128,256]{1,0:T(8,128)(2,1)S(1)}, u32[]{:S(2)}, u32[]{:S(2)}) %collective-permute-start.3) | collective-permute-done | bytes 65568 | tf_op jit(solution)/shard_map/ppermute | solution.py:538
  44.3 3.2 %second_near.1 = (f32[256,256]{1,0:T(8,128)S(1)}, bf16[16,3072]{1,0:T(8,128)(2,1)}) custom-call(s32[16,20]{1,0:T(8,128)} %get-tuple-element.21.at_hbm, s32[16,20]{1,0:T(8,128)} %get-tuple-element.22.kind_hbm, bf16[128,256]{1,0:T(8,128)(2,1)S(1)} %get-tuple-element.28.lo_ref, bf16[128,256]{1,0:T(8,128)(2,1)S(1)} %get-tuple-element.29.hi_ref, ...), custom_call_target="tpu_custom_call" | custom-call | flops 1200000000 | bytes 12000000 | tf_op jit(solution)/shard_map/second_near/pallas_call | solution.py:37
  47.5 2.3 %all-to-all-done.1.got_any = bf16[16,64,128]{2,1,0:T(8,128)(2,1)S(1)} async-done(((bf16[16,64,128]{2,1,0:T(8,128)(2,1)}), bf16[16,64,128]{2,1,0:T(8,128)(2,1)S(1)}, u32[]{:S(2)}, u32[]{:S(2)}) %all-to-all-start.1) | async-done | bytes 262176 | tf_op jit(solution)/shard_map/all_to_all | solution.py:541
  49.8 2.6 %far_last.1 = bf16[16,3072]{1,0:T(8,128)(2,1)} custom-call(s32[16,32]{1,0:T(8,128)} %get-tuple-element.23.idx_hbm, bf16[16,64,128]{2,1,0:T(8,128)(2,1)S(1)} %all-to-all-done.1.got_any, bf16[512,1024]{1,0:T(8,128)(2,1)S(1)} %get-tuple-element.25.mat_ref, bf16[512,256]{1,0:T(8,128)(2,1)S(1)} %get-tuple-element.26.basis_ref, ...), custom_call_target="tpu_custom_call" | custom-call | tf_op jit(solution)/shard_map/far_last/pallas_call | solution.py:37
Async XLA Ops:
  0.6 15.7 %collective-permute-start.1 = (bf16[16,3072]{1,0:T(8,128)(2,1)}, bf16[16,3072]{1,0:T(8,128)(2,1)S(1)}, u32[]{:S(2)}, u32[]{:S(2)}) collective-permute-start(bf16[16,3072]{1,0:T(8,128)(2,1)} %v_hbm.1), channel_id=1, source_target_pairs={{0,240},{16,32},{32,16},{48,64},{64,48},{80,96},{96,80},{112,128},... | collective-permute-start | bytes 294920 | tf_op jit(solution)/shard_map/ppermute | solution.py:538
  2.5 13.9 %collective-permute-start = (bf16[16,3072]{1,0:T(8,128)(2,1)}, bf16[16,3072]{1,0:T(8,128)(2,1)S(1)}, u32[]{:S(2)}, u32[]{:S(2)}) collective-permute-start(bf16[16,3072]{1,0:T(8,128)(2,1)} %v_hbm.1), channel_id=1, source_target_pairs={{0,16},{16,0},{32,48},{48,32},{64,80},{80,64},{96,112},{112,96},{1... | collective-permute-start | bytes 294920 | tf_op jit(solution)/shard_map/ppermute | solution.py:538
  5.1 25.4 %all-to-all-start = ((bf16[16,64,128]{2,1,0:T(8,128)(2,1)}), bf16[16,64,128]{2,1,0:T(8,128)(2,1)}, u32[]{:S(2)}, u32[]{:S(2)}) async-start(bf16[16,64,128]{2,1,0:T(8,128)(2,1)} %get-tuple-element.24), calls=%async_computation | async-start | bytes 524288 | tf_op jit(solution)/shard_map/all_to_all | solution.py:541
  33.6 16.2 %all-to-all-start.1 = ((bf16[16,64,128]{2,1,0:T(8,128)(2,1)}), bf16[16,64,128]{2,1,0:T(8,128)(2,1)S(1)}, u32[]{:S(2)}, u32[]{:S(2)}) async-start(bf16[16,64,128]{2,1,0:T(8,128)(2,1)} %get-tuple-element.34), calls=%async_computation.1 | async-start | bytes 524288 | tf_op jit(solution)/shard_map/all_to_all | solution.py:541
  37.1 1.3 %collective-permute-start.2 = (bf16[128,256]{1,0:T(8,128)(2,1)S(1)}, bf16[128,256]{1,0:T(8,128)(2,1)S(1)}, u32[]{:S(2)}, u32[]{:S(2)}) collective-permute-start(bf16[128,256]{1,0:T(8,128)(2,1)S(1)} %get-tuple-element.30), channel_id=1, source_target_pairs={{0,16},{16,0},{32,48},{48,32},{64,80},{80,64},{96,112},{112,96},{1... | collective-permute-start | bytes 196616 | tf_op jit(solution)/shard_map/ppermute | solution.py:538
  37.2 7.0 %collective-permute-start.3 = (bf16[128,256]{1,0:T(8,128)(2,1)S(1)}, bf16[128,256]{1,0:T(8,128)(2,1)S(1)}, u32[]{:S(2)}, u32[]{:S(2)}) collective-permute-start(bf16[128,256]{1,0:T(8,128)(2,1)S(1)} %get-tuple-element.31), channel_id=1, source_target_pairs={{0,240},{16,32},{32,16},{48,64},{64,48},{80,96},{96,80},{112,128},... | collective-permute-start | bytes 196616 | tf_op jit(solution)/shard_map/ppermute | solution.py:538

commit v4 on v3

--- a/solution.py
+++ b/solution.py
@@ -14,7 +14,7 @@
 LANES = 128
 WIDE = 256
 GROUP = 8
-LONG = 1_000_000_000_000
+LONG = 100_000_000
 STEPS = 2
 SIDE = LANES // RANK
 
@@ -22,6 +22,8 @@
 SMEM = pl.BlockSpec(memory_space=pltpu.SMEM)
 HBM = pl.BlockSpec(memory_space=pltpu.HBM)
 ANY = pl.BlockSpec(memory_space=pl.ANY)
+KEPT = pl.BlockSpec(memory_space=pltpu.VMEM)
+BOUND = (HBM, SMEM, KEPT)
 F32 = jnp.float32
 BF16 = jnp.bfloat16
 NT = (((1,), (1,)), ((), ()))
@@ -31,12 +33,14 @@
 
 def call(kernel, name, args, ins, outs, scratch, mib, moved=0):
     args = [
-        pltpu.with_memory_space_constraint(a, pltpu.HBM) if s is HBM else a
+        pltpu.with_memory_space_constraint(a, s.memory_space) if any(s is b for b in BOUND) else a
         for a, s in zip(args, ins)
     ]
     return pl.pallas_call(
         kernel,
-        out_shape=tuple(pltpu.HBM(o.shape, o.dtype) if s is HBM else o for o, s in outs),
+        out_shape=tuple(
+            s.memory_space(o.shape, o.dtype) if any(s is b for b in BOUND) else o for o, s in outs
+        ),
         in_specs=ins,
         out_specs=tuple(s for _, s in outs),
         scratch_shapes=scratch,
@@ -123,10 +127,13 @@
 def project(fields, basis_ref, coef_s):
     cols = GROUP * RANK
     lane = iota((RHS, LANES), 1) // RANK
-    for g, field in enumerate(fields):
-        cross = lax.dot_general(
+    crosses = [
+        lax.dot_general(
             field, basis_ref[g * cols : (g + 1) * cols, :], NT, preferred_element_type=F32
         )
+        for g, field in enumerate(fields)
+    ]
+    for g, cross in enumerate(crosses):
         for half in range(GROUP // SIDE):
             out = None
             for j in range(SIDE):
@@ -191,8 +198,8 @@
 def first_near_kernel(
     slabs, slab_blocks,
     count_hbm, src_hbm, type_hbm, far_hbm, tiles_hbm, coup_hbm, lo_ref, hi_ref, chip_ref, further_ref,
-    near_ref, mat_ref, table_hbm, far_idx_hbm, at_hbm, kind_hbm,
-    count_s, src_s, type_s, far_s, tiles_s, coup_s, far_idx_s, at_v, kind_v, at_s, kind_s,
+    near_ref, mat_ref, table_hbm, far_idx_ref, at_s, kind_s,
+    count_s, src_s, type_s, far_s, tiles_s, coup_s, far_idx_s, at_v, kind_v,
     h_s, e_s, p_s, table_s, sems,
 ):
     gets = copies(
@@ -210,9 +217,7 @@
         (
             (at_v, at_s),
             (kind_v, kind_s),
-            (at_v, at_hbm),
-            (kind_v, kind_hbm),
-            (far_idx_s, far_idx_hbm),
+            (far_idx_s, far_idx_ref),
         ),
         sems,
         len(gets),
@@ -295,7 +300,7 @@
     steps = STEPS
     each = TILE // steps
     put_table = [
-        copies(((table_s.at[rows], table_hbm.at[rows]),), sems, 11 + n)
+        copies(((table_s.at[rows], table_hbm.at[rows]),), sems, 9 + n)
         for n, rows in enumerate(pl.ds(n * each, each) for n in range(steps))
     ]
 
@@ -320,7 +325,7 @@
                     row = pl.multiple_of(step * each + n * many, many)
                     table_s[pl.ds(row, many), to : to + WIDE] = out[t * many : (t + 1) * many]
         rows = pl.ds(pl.multiple_of(step * each, many), each)
-        start(copies(((table_s.at[rows], table_hbm.at[rows]),), sems, 11 + step))
+        start(copies(((table_s.at[rows], table_hbm.at[rows]),), sems, 9 + step))
         return 0
 
     lax.fori_loop(0, steps, some_rows, 0)
@@ -330,40 +335,40 @@
         wait(put)
 
 
+def give_kernel(lo_ref, hi_ref, table_hbm, y_hbm, table_ref, f_s, y_s, sems):
+    gets = copies(((table_hbm, table_ref),), sems)
+    put = copies(((y_s, y_hbm),), sems, 1)
+    start(gets)
+    rim = lo_ref.shape[0]
+    for k, ref in enumerate((lo_ref, hi_ref)):
+        for j in range(2):
+            at = (2 * j + k) * rim
+            f_s[at : at + rim, :] = ref[:, j * LANES : (j + 1) * LANES].astype(F32)
+    gather_sides(f_s, y_s, y_s.shape[0])
+    start(put)
+    wait(gets + put)
+
+
 def second_near_kernel(
-    at_hbm, kind_hbm, lo_ref, hi_ref, chip_ref, further_ref, table_hbm,
-    near_ref, y_hbm,
-    at_s, kind_s, e_s, p_s, table_s, f_s, y_s, sems,
+    at_s, kind_s, lo_ref, hi_ref, chip_ref, further_ref, table_ref, near_ref, e_s, p_s
 ):
-    gets = copies(((at_hbm, at_s), (kind_hbm, kind_s), (table_hbm, table_s)), sems)
-    put = copies(((y_s, y_hbm),), sems, len(gets))
-    start(gets)
-    blocks = at_s.shape[0]
-    size, rim = blocks * RHS, RIM * RHS
+    rim, columns = RIM * RHS, table_ref.shape[1]
     for j, ref in enumerate((lo_ref, hi_ref, chip_ref, further_ref)):
         e_s[j * rim : (j + 1) * rim, :] = ref[...]
-    for j in range(2):
-        f_s[j * size : (j + 1) * size, :] = e_s[:size, j * LANES : (j + 1) * LANES].astype(F32)
-    gather_sides(f_s, y_s, blocks)
-    start(put)
-    columns = table_s.shape[1]
-    p_s[:, :columns] = jnp.zeros((size, columns), BF16)
-    wait(gets[:2])
+    p_s[:, :columns] = jnp.zeros((p_s.shape[0], columns), BF16)
     place(at_s, kind_s, e_s, p_s, True)
-    gets[2].wait()
-    multiply(p_s, table_s, near_ref, table_s.shape[1])
-    wait(put)
-
-
-def far_kernel(last, idx_hbm, got_any, mat_ref, basis_ref, near_ref, *rest):
+    multiply(p_s, table_ref, near_ref, columns)
+
+
+def far_kernel(last, idx_s, got_any, mat_ref, basis_ref, near_ref, *rest):
     if last:
-        y_ref, idx_s, got_ref, turn_s, pick_s, sem, sum_s = rest
+        y_ref, got_ref, turn_s, pick_s, sem, sum_s = rest
     else:
-        lo_ref, hi_ref, chip_ref, further_ref, coef_hbm, idx_s, got_ref, turn_s, pick_s, sem, coef_s = rest
-        put = copies(((coef_s, coef_hbm),), sem, 2)
-    gets = copies(((got_any, got_ref), (idx_hbm, idx_s)), sem)
+        lo_ref, hi_ref, chip_ref, further_ref, coef_hbm, got_ref, turn_s, pick_s, sem, coef_s = rest
+        put = copies(((coef_s, coef_hbm),), sem, 1)
+    gets = copies(((got_any, got_ref),), sem)
     start(gets)
-    gets[0].wait()
+    wait(gets)
     blocks, partners = idx_s.shape
     deep = partners // SIDE
     peers, packed_rows, _ = got_ref.shape
@@ -374,7 +379,6 @@
             at = r * quarter + j * packed_rows
             turn_s[at : at + packed_rows, :] = got if r == 0 else pltpu.roll(got, r * RANK, 1)
     lane = iota((RHS, LANES), 1) // RANK
-    gets[1].wait()
 
     def one_block(i, _):
         row = pl.multiple_of(i * RHS, RHS)
@@ -391,25 +395,30 @@
     size = blocks * RHS
     rows, cols = GROUP * RHS, GROUP * RANK
     own = iota((rows, cols), 0) // RHS == iota((rows, cols), 1) // RANK
-    fields = []
-    for g in range(blocks // GROUP):
-        cross = lax.dot_general(
+    groups = range(blocks // GROUP)
+    crosses = [
+        lax.dot_general(
             pick_s[g * rows : (g + 1) * rows, :],
             mat_ref[g * cols : (g + 1) * cols, :],
             NT,
             preferred_element_type=F32,
         )
-        mix = jnp.where(own, cross, 0.0).astype(BF16)
-        far = lax.dot_general(
-            mix, basis_ref[g * cols : (g + 1) * cols, :], NN, preferred_element_type=F32
+        for g in groups
+    ]
+    mixes = [jnp.where(own, cross, 0.0).astype(BF16) for cross in crosses]
+    totals = [
+        near_ref[g * rows : (g + 1) * rows, :]
+        + lax.dot_general(
+            mixes[g], basis_ref[g * cols : (g + 1) * cols, :], NN, preferred_element_type=F32
         )
-        total = near_ref[g * rows : (g + 1) * rows, :] + far
-        if last:
+        for g in groups
+    ]
+    if last:
+        for g in groups:
             for j in range(2):
                 at = j * size + g * rows
-                sum_s[at : at + rows, :] = total[:, j * LANES : (j + 1) * LANES]
-        else:
-            fields.append(total.astype(BF16))
+                sum_s[at : at + rows, :] = totals[g][:, j * LANES : (j + 1) * LANES]
+    fields = [total.astype(BF16) for total in totals]
     if last:
         gather_sides(sum_s, y_ref, blocks)
     else:
@@ -459,9 +468,9 @@
             (shape((rows, WIDE), F32), VMEM),
             (shape((blocks * RANK, partners * RANK), BF16), VMEM),
             (shape(table, BF16), HBM),
-            (shape(*picks), HBM),
-            (shape(*slots), HBM),
-            (shape(*slots), HBM),
+            (shape(*picks), SMEM),
+            (shape(*slots), SMEM),
+            (shape(*slots), SMEM),
         ],
         [
             pltpu.SMEM(near_count.shape, jnp.int32),
@@ -473,49 +482,53 @@
             pltpu.VMEM(*picks),
             pltpu.VMEM(*slots),
             pltpu.VMEM(*slots),
-            pltpu.SMEM(*slots),
-            pltpu.SMEM(*slots),
             pltpu.VMEM((2 * rim, LANES), F32),
             pltpu.VMEM((4 * rim, WIDE), BF16),
             pltpu.VMEM((rows, (types + 1) * WIDE), BF16),
             pltpu.VMEM(table, BF16),
-            pltpu.SemaphoreType.DMA((11 + STEPS,)),
+            pltpu.SemaphoreType.DMA((9 + STEPS,)),
         ],
         20, LONG,
     )
 
 
-def second_near(at, kind, lo, hi, chip, further, table):
-    rim = lo.shape[0]
-    rows = 2 * rim
+def give(lo, hi, table):
+    rows = 2 * lo.shape[0]
     y = (rows // RHS, RHS * TILE)
     return call(
+        give_kernel, "give", (lo, hi, table), [VMEM] * 2 + [HBM],
+        [(shape(y, BF16), HBM), (shape(table.shape, BF16), KEPT)],
+        [
+            pltpu.VMEM((2 * rows, LANES), F32),
+            pltpu.VMEM(y, BF16),
+            pltpu.SemaphoreType.DMA((2,)),
+        ],
+        4, 12_000_000,
+    )
+
+
+def second_near(at, kind, lo, hi, chip, further, table):
+    rows = 2 * lo.shape[0]
+    return call(
         second_near_kernel, "second_near", (at, kind, lo, hi, chip, further, table),
-        [HBM] * 2 + [VMEM] * 4 + [HBM],
-        [(shape((rows, WIDE), F32), VMEM), (shape(y, BF16), HBM)],
+        [SMEM] * 2 + [VMEM] * 4 + [KEPT],
+        [(shape((rows, WIDE), F32), VMEM)],
         [
-            pltpu.SMEM(at.shape, jnp.int32),
-            pltpu.SMEM(at.shape, jnp.int32),
             pltpu.VMEM((2 * rows, WIDE), BF16),
             pltpu.VMEM((rows, table.shape[1] + WIDE), BF16),
-            pltpu.VMEM(table.shape, BF16),
-            pltpu.VMEM((2 * rows, LANES), F32),
-            pltpu.VMEM(y, BF16),
-            pltpu.SemaphoreType.DMA((4,)),
         ],
-        16, 12_000_000,
-    )
+        8, 12_000_000,
+    )[0]
 
 
 def far(last, idx, got, mat, basis, near_term):
     rows = near_term.shape[0]
     peers, packed, _ = got.shape
     scratch = [
-        pltpu.SMEM(idx.shape, jnp.int32),
         pltpu.VMEM(got.shape, BF16),
         pltpu.VMEM((SIDE * peers * packed, LANES), BF16),
         pltpu.VMEM((rows, mat.shape[1]), BF16),
-        pltpu.SemaphoreType.DMA((3,)),
+        pltpu.SemaphoreType.DMA((2,)),
     ]
     if last:
         outs = [(shape((rows // RHS, RHS * TILE), BF16), VMEM)]
@@ -525,7 +538,7 @@
         scratch.append(pltpu.VMEM(got.shape, BF16))
     return call(
         functools.partial(far_kernel, last), "far_last" if last else "far",
-        (idx, got, mat, basis, near_term), [HBM, ANY] + [VMEM] * 3, outs, scratch, 8,
+        (idx, got, mat, basis, near_term), [SMEM, ANY] + [VMEM] * 3, outs, scratch, 8,
     )
 
 
@@ -549,7 +562,8 @@
     lo, hi, chip, further, coef = far(False, idx, got, mat, basis, near_term)
     got = exchange(coef)
     chip, further = halo(chip, further)
-    near_term, first = second_near(at, kind, lo, hi, chip, further, table)
+    first, table = give(lo, hi, table)
+    near_term = second_near(at, kind, lo, hi, chip, further, table)
     (second,) = far(True, idx, got, mat, basis, near_term)
     return (first, second)
 

time: 52.9 us -> 51 us (0.964)
  waiting for transfers between devices: 16.1 us -> 14.9 us
  Pallas kernels: 17.8 us -> 17.2 us
    ppermute x2, waiting for transfers between devices: 5.78 us -> 3.94 us  [halo(): lax.ppermute(further, 'slab', between)]
    all_to_all x2, waiting for transfers between devices: 10.2 us -> 11 us  [exchange(): return lax.all_to_all(coef, 'grp', 0, 0, tiled=True)]
    pallas_call x5 -> x6, Pallas kernels: 17.8 us -> 17.2 us  [call(): pl.pallas_call(kernel, out_shape=tuple((s.memory_space(o.shape, o.dtype)...]
  transfers between devices with their start and end apart: 6 -> 6, of which waited for: 4 -> 3; matrix products, arithmetic and copies ran while one was open for 0% -> 0% of each run, Pallas kernels for 23% -> 26%
where the time goes in v4:
time: 51 us; the launch traced here: 50.6 us
  starting transfers between devices  17.8 us (35%)
  Pallas kernels  17.2 us (34%)
  waiting for transfers between devices  14.9 us (29%)
  between operations  0.72 us (1%)
    pallas_call x6, Pallas kernels, call(): pl.pallas_call(kernel, out_shape=tuple((s.memory_space(o.shape, o.dtype)...  17.2 us
    all_to_all x2, starting transfers between devices, exchange(): return lax.all_to_all(coef, 'grp', 0, 0, tiled=True)  14.8 us
    all_to_all x2, waiting for transfers between devices, exchange(): return lax.all_to_all(coef, 'grp', 0, 0, tiled=True)  11 us
    ppermute x2, waiting for transfers between devices, halo(): lax.ppermute(further, 'slab', between)  3.94 us
    ppermute x2, starting transfers between devices, halo(): lax.ppermute(further, 'slab', between)  2.94 us
  transfers between devices with their start and end apart: 6, of which 3 were waited for; matrix products, arithmetic and copies ran while one was open for 0% of the time, Pallas kernels for 26%

profile of v4, /device:TPU:32, one launch (start us, length us, event | category | flops | bytes accessed | tf_op | source)
XLA Modules:
  0.0 50.6 jit_solution(7586064927326035897)
XLA Ops:
  0.6 1.8 %collective-permute-start.1 = (bf16[16,3072]{1,0:T(8,128)(2,1)}, bf16[16,3072]{1,0:T(8,128)(2,1)S(1)}, u32[]{:S(2)}, u32[]{:S(2)}) collective-permute-start(bf16[16,3072]{1,0:T(8,128)(2,1)} %v_hbm.1), channel_id=1, source_target_pairs={{0,240},{16,32},{32,16},{48,64},{64,48},{80,96},{96,80},{112,128},... | collective-permute-start | bytes 294920 | tf_op jit(solution)/shard_map/ppermute | solution.py:551
  2.5 0.0 collective-permute-start
  2.5 2.6 %opening.1 = (bf16[128,256]{1,0:T(8,128)(2,1)S(1)}, bf16[128,256]{1,0:T(8,128)(2,1)S(1)}, bf16[512,256]{1,0:T(8,128)(2,1)S(1)}, bf16[16,64,128]{2,1,0:T(8,128)(2,1)}) custom-call(bf16[16,3072]{1,0:T(8,128)(2,1)} %v_hbm.1, bf16[16,6144]{1,0:T(8,128)(2,1)} %b_hbm.1), custom_call_target="tpu_custom_call" | custom-call | tf_op jit(solution)/shard_map/opening/pallas_call | solution.py:39
  5.0 11.2 %all-to-all-start = ((bf16[16,64,128]{2,1,0:T(8,128)(2,1)}), bf16[16,64,128]{2,1,0:T(8,128)(2,1)S(1)}, u32[]{:S(2)}, u32[]{:S(2)}) async-start(bf16[16,64,128]{2,1,0:T(8,128)(2,1)} %get-tuple-element.22), calls=%async_computation | async-start | bytes 524288 | tf_op jit(solution)/shard_map/all_to_all | solution.py:554
  16.3 0.0 collective-permute-done.1.further_ref
  16.3 0.0 collective-permute-done.chip_ref
  16.3 6.3 %first_near.1 = (f32[256,256]{1,0:T(8,128)S(1)}, bf16[512,1024]{1,0:T(8,128)(2,1)S(1)}, bf16[192,8192]{1,0:T(8,128)(2,1)}, s32[16,32]{1,0:T(8,128)S(4)}, s32[16,20]{1,0:T(8,128)S(4)}, /*index=5*/s32[16,20]{1,0:T(8,128)S(4)}) custom-call(s32[16]{0:T(128)} %count_hbm.1, s32[16,20]{1,0:T(8,128)} %src_hbm.1, s32[16,20]{1,0:T(8,128)} %type_hbm.1, ...), custom_call_target="tpu_custom_call" | custom-call | flops 10000000000 | bytes 100000000 | tf_op jit(solution)/shard_map/first_near/pallas_call | solution.py:39
  22.6 7.7 %all-to-all-done.got_any = bf16[16,64,128]{2,1,0:T(8,128)(2,1)S(1)} async-done(((bf16[16,64,128]{2,1,0:T(8,128)(2,1)}), bf16[16,64,128]{2,1,0:T(8,128)(2,1)S(1)}, u32[]{:S(2)}, u32[]{:S(2)}) %all-to-all-start) | async-done | bytes 262176 | tf_op jit(solution)/shard_map/all_to_all | solution.py:554
  30.3 2.1 %far.1 = (bf16[128,256]{1,0:T(8,128)(2,1)S(1)}, bf16[128,256]{1,0:T(8,128)(2,1)S(1)}, bf16[128,256]{1,0:T(8,128)(2,1)S(1)}, bf16[128,256]{1,0:T(8,128)(2,1)S(1)}, bf16[16,64,128]{2,1,0:T(8,128)(2,1)}) custom-call(s32[16,32]{1,0:T(8,128)S(4)} %get-tuple-element.21.idx_s, bf16[16,64,128]{2,1,0:T(8,128)(2,1)S(1)} %all-to-all-done.got_any, ...), custom_call_target="tpu_custom_call" | custom-call | tf_op jit(solution)/shard_map/far/pallas_call | solution.py:39
  32.4 3.5 %all-to-all-start.1 = ((bf16[16,64,128]{2,1,0:T(8,128)(2,1)}), bf16[16,64,128]{2,1,0:T(8,128)(2,1)S(1)}, u32[]{:S(2)}, u32[]{:S(2)}) async-start(bf16[16,64,128]{2,1,0:T(8,128)(2,1)} %get-tuple-element.30), calls=%async_computation.1 | async-start | bytes 524288 | tf_op jit(solution)/shard_map/all_to_all | solution.py:554
  36.0 0.1 collective-permute-start.2
  36.1 1.1 %collective-permute-start.3 = (bf16[128,256]{1,0:T(8,128)(2,1)S(1)}, bf16[128,256]{1,0:T(8,128)(2,1)S(1)}, u32[]{:S(2)}, u32[]{:S(2)}) collective-permute-start(bf16[128,256]{1,0:T(8,128)(2,1)S(1)} %get-tuple-element.34), channel_id=1, source_target_pairs={{0,240},{16,32},{32,16},{48,64},{64,48},{80,96},{96,80},{112,128},... | collective-permute-start | bytes 196616 | tf_op jit(solution)/shard_map/ppermute | solution.py:551
  37.2 1.9 %give.1 = (bf16[16,3072]{1,0:T(8,128)(2,1)}, bf16[192,8192]{1,0:T(8,128)(2,1)S(1)}) custom-call(bf16[128,256]{1,0:T(8,128)(2,1)S(1)} %get-tuple-element.26.lo_ref, bf16[128,256]{1,0:T(8,128)(2,1)S(1)} %get-tuple-element.27.hi_ref, bf16[192,8192]{1,0:T(8,128)(2,1)} %get-tuple-element.28.table_hbm), custom_call_target="tpu_custom_call" | custom-call | flops 1200000000 | bytes 12000000 | tf_op jit(solution)/shard_map/give/pallas_call | solution.py:39
  39.1 0.0 collective-permute-done.2.chip_ref
  39.2 3.9 %collective-permute-done.3.further_ref = bf16[128,256]{1,0:T(8,128)(2,1)S(1)} collective-permute-done((bf16[128,256]{1,0:T(8,128)(2,1)S(1)}, bf16[128,256]{1,0:T(8,128)(2,1)S(1)}, u32[]{:S(2)}, u32[]{:S(2)}) %collective-permute-start.3) | collective-permute-done | bytes 65568 | tf_op jit(solution)/shard_map/ppermute | solution.py:551
  43.1 2.3 %second_near.1.near_ref = f32[256,256]{1,0:T(8,128)S(1)} custom-call(s32[16,20]{1,0:T(8,128)S(4)} %get-tuple-element.31.at_s, s32[16,20]{1,0:T(8,128)S(4)} %get-tuple-element.32.kind_s, bf16[128,256]{1,0:T(8,128)(2,1)S(1)} %get-tuple-element.26.lo_ref, bf16[128,256]{1,0:T(8,128)(2,1)S(1)} %get-tuple-element.27.hi_ref, ...), custom_call_target="tpu_custom_call" | custom-call | flops 1200000000 | bytes 12000000 | tf_op jit(solution)/shard_map/second_near/pallas_call | solution.py:39
  45.4 3.2 %all-to-all-done.1.got_any = bf16[16,64,128]{2,1,0:T(8,128)(2,1)S(1)} async-done(((bf16[16,64,128]{2,1,0:T(8,128)(2,1)}), bf16[16,64,128]{2,1,0:T(8,128)(2,1)S(1)}, u32[]{:S(2)}, u32[]{:S(2)}) %all-to-all-start.1) | async-done | bytes 262176 | tf_op jit(solution)/shard_map/all_to_all | solution.py:554
  48.6 2.0 %far_last.1 = bf16[16,3072]{1,0:T(8,128)(2,1)} custom-call(s32[16,32]{1,0:T(8,128)S(4)} %get-tuple-element.21.idx_s, bf16[16,64,128]{2,1,0:T(8,128)(2,1)S(1)} %all-to-all-done.1.got_any, bf16[512,1024]{1,0:T(8,128)(2,1)S(1)} %get-tuple-element.23.mat_ref, bf16[512,256]{1,0:T(8,128)(2,1)S(1)} %get-tuple-element.24.basis_ref, f32[256,256]{1,0:T(8,128)S(1)} %second_near.1.near_ref), custom_call_target="tpu_custom_call" | custom-call | tf_op jit(solution)/shard_map/far_last/pallas_call | solution.py:39
Async XLA Ops:
  0.6 15.6 %collective-permute-start.1 = (bf16[16,3072]{1,0:T(8,128)(2,1)}, bf16[16,3072]{1,0:T(8,128)(2,1)S(1)}, u32[]{:S(2)}, u32[]{:S(2)}) collective-permute-start(bf16[16,3072]{1,0:T(8,128)(2,1)} %v_hbm.1), channel_id=1, source_target_pairs={{0,240},{16,32},{32,16},{48,64},{64,48},{80,96},{96,80},{112,128},... | collective-permute-start | bytes 294920 | tf_op jit(solution)/shard_map/ppermute | solution.py:551
  2.5 13.8 %collective-permute-start = (bf16[16,3072]{1,0:T(8,128)(2,1)}, bf16[16,3072]{1,0:T(8,128)(2,1)S(1)}, u32[]{:S(2)}, u32[]{:S(2)}) collective-permute-start(bf16[16,3072]{1,0:T(8,128)(2,1)} %v_hbm.1), channel_id=1, source_target_pairs={{0,16},{16,0},{32,48},{48,32},{64,80},{80,64},{96,112},{112,96},{1... | collective-permute-start | bytes 294920 | tf_op jit(solution)/shard_map/ppermute | solution.py:551
  5.0 25.3 %all-to-all-start = ((bf16[16,64,128]{2,1,0:T(8,128)(2,1)}), bf16[16,64,128]{2,1,0:T(8,128)(2,1)S(1)}, u32[]{:S(2)}, u32[]{:S(2)}) async-start(bf16[16,64,128]{2,1,0:T(8,128)(2,1)} %get-tuple-element.22), calls=%async_computation | async-start | bytes 524288 | tf_op jit(solution)/shard_map/all_to_all | solution.py:554
  32.4 16.2 %all-to-all-start.1 = ((bf16[16,64,128]{2,1,0:T(8,128)(2,1)}), bf16[16,64,128]{2,1,0:T(8,128)(2,1)S(1)}, u32[]{:S(2)}, u32[]{:S(2)}) async-start(bf16[16,64,128]{2,1,0:T(8,128)(2,1)} %get-tuple-element.30), calls=%async_computation.1 | async-start | bytes 524288 | tf_op jit(solution)/shard_map/all_to_all | solution.py:554
  36.0 3.2 %collective-permute-start.2 = (bf16[128,256]{1,0:T(8,128)(2,1)S(1)}, bf16[128,256]{1,0:T(8,128)(2,1)S(1)}, u32[]{:S(2)}, u32[]{:S(2)}) collective-permute-start(bf16[128,256]{1,0:T(8,128)(2,1)S(1)} %get-tuple-element.33), channel_id=1, source_target_pairs={{0,16},{16,0},{32,48},{48,32},{64,80},{80,64},{96,112},{112,96},{1... | collective-permute-start | bytes 196616 | tf_op jit(solution)/shard_map/ppermute | solution.py:551
  36.1 7.0 %collective-permute-start.3 = (bf16[128,256]{1,0:T(8,128)(2,1)S(1)}, bf16[128,256]{1,0:T(8,128)(2,1)S(1)}, u32[]{:S(2)}, u32[]{:S(2)}) collective-permute-start(bf16[128,256]{1,0:T(8,128)(2,1)S(1)} %get-tuple-element.34), channel_id=1, source_target_pairs={{0,240},{16,32},{32,16},{48,64},{64,48},{80,96},{96,80},{112,128},... | collective-permute-start | bytes 196616 | tf_op jit(solution)/shard_map/ppermute | solution.py:551

commit v5 on v4

--- a/solution.py
+++ b/solution.py
@@ -21,7 +21,6 @@
 VMEM = pl.BlockSpec(memory_space=pltpu.VMEM)
 SMEM = pl.BlockSpec(memory_space=pltpu.SMEM)
 HBM = pl.BlockSpec(memory_space=pltpu.HBM)
-ANY = pl.BlockSpec(memory_space=pl.ANY)
 KEPT = pl.BlockSpec(memory_space=pltpu.VMEM)
 BOUND = (HBM, SMEM, KEPT)
 F32 = jnp.float32
@@ -146,25 +145,30 @@
 
 
 def opening_kernel(
-    v_hbm, b_hbm, lo_ref, hi_ref, basis_ref, coef_hbm, v_s, b_s, f_s, g_s, coef_s, sems
+    v_hbm, b_hbm, lo_ref, hi_ref, basis_ref, coef_ref, v_s, b_s, f_s, sems
 ):
     gets = copies(((v_hbm, v_s), (b_hbm, b_s)), sems)
-    put = copies(((coef_s, coef_hbm),), sems, 2)
     start(gets)
     blocks = v_s.shape[0]
-    rows, ranks = blocks * RHS, blocks * RANK
+    rows = blocks * RHS
     gets[0].wait()
     spread(v_s, f_s, blocks, RHS)
     field = join(f_s, rows)
     rim = RIM * RHS
     lo_ref[...] = field[:rim]
     hi_ref[...] = field[rim:]
+    order = swap(blocks * blocks, blocks)
     gets[1].wait()
-    spread(b_s, g_s, blocks, RANK)
-    basis_ref[...] = join(g_s, ranks)
-    project((field[:rim], field[rim:]), basis_ref, coef_s)
-    start(put)
-    wait(put)
+    for a in range(0, RANK, blocks):
+        stack = []
+        for p in range(a, a + blocks, 2):
+            pair = b_s[:, p * TILE : (p + 2) * TILE]
+            stack += [jnp.concatenate(parts, axis=1) for parts in halves(pair)]
+        out = jnp.concatenate(stack, axis=0)
+        out = lax.dot_general(order, out, NN, preferred_element_type=F32).astype(BF16)
+        for i in range(blocks):
+            basis_ref[i * RANK + a : i * RANK + a + blocks, :] = out[i * blocks : (i + 1) * blocks]
+    project((field[:rim], field[rim:]), basis_ref, coef_ref)
 
 
 def place(at_s, kind_s, e_s, p_s, unroll):
@@ -360,15 +364,11 @@
     multiply(p_s, table_ref, near_ref, columns)
 
 
-def far_kernel(last, idx_s, got_any, mat_ref, basis_ref, near_ref, *rest):
+def far_kernel(last, idx_s, got_ref, mat_ref, basis_ref, near_ref, *rest):
     if last:
-        y_ref, got_ref, turn_s, pick_s, sem, sum_s = rest
+        y_ref, turn_s, pick_s, sum_s = rest
     else:
-        lo_ref, hi_ref, chip_ref, further_ref, coef_hbm, got_ref, turn_s, pick_s, sem, coef_s = rest
-        put = copies(((coef_s, coef_hbm),), sem, 1)
-    gets = copies(((got_any, got_ref),), sem)
-    start(gets)
-    wait(gets)
+        lo_ref, hi_ref, chip_ref, further_ref, coef_ref, turn_s, pick_s = rest
     blocks, partners = idx_s.shape
     deep = partners // SIDE
     peers, packed_rows, _ = got_ref.shape
@@ -422,13 +422,11 @@
     if last:
         gather_sides(sum_s, y_ref, blocks)
     else:
-        project(fields, basis_ref, coef_s)
-        start(put)
+        project(fields, basis_ref, coef_ref)
         lo_ref[...], hi_ref[...] = lo, hi = fields
         odd = lax.axis_index("slab") % 2 == 1
         chip_ref[...] = jnp.where(odd, lo, hi)
         further_ref[...] = jnp.where(odd, hi, lo)
-        wait(put)
 
 
 def opening(peers, vectors, bases):
@@ -438,14 +436,12 @@
     coef = (peers, rows // SIDE, LANES)
     return call(
         opening_kernel, "opening", (vectors, bases), [HBM] * 2,
-        [field, field, (shape((ranks, WIDE), BF16), VMEM), (shape(coef, BF16), HBM)],
+        [field, field, (shape((ranks, WIDE), BF16), VMEM), (shape(coef, BF16), VMEM)],
         [
             pltpu.VMEM(vectors.shape, BF16),
             pltpu.VMEM(bases.shape, BF16),
             pltpu.VMEM((2 * rows, LANES), F32),
-            pltpu.VMEM((2 * ranks, LANES), F32),
-            pltpu.VMEM(coef, BF16),
-            pltpu.SemaphoreType.DMA((3,)),
+            pltpu.SemaphoreType.DMA((2,)),
         ],
         8,
     )
@@ -525,20 +521,17 @@
     rows = near_term.shape[0]
     peers, packed, _ = got.shape
     scratch = [
-        pltpu.VMEM(got.shape, BF16),
         pltpu.VMEM((SIDE * peers * packed, LANES), BF16),
         pltpu.VMEM((rows, mat.shape[1]), BF16),
-        pltpu.SemaphoreType.DMA((2,)),
     ]
     if last:
         outs = [(shape((rows // RHS, RHS * TILE), BF16), VMEM)]
         scratch.append(pltpu.VMEM((2 * rows, LANES), F32))
     else:
-        outs = [(shape((rows // 2, WIDE), BF16), VMEM)] * 4 + [(shape(got.shape, BF16), HBM)]
-        scratch.append(pltpu.VMEM(got.shape, BF16))
+        outs = [(shape((rows // 2, WIDE), BF16), VMEM)] * 4 + [(shape(got.shape, BF16), VMEM)]
     return call(
         functools.partial(far_kernel, last), "far_last" if last else "far",
-        (idx, got, mat, basis, near_term), [SMEM, ANY] + [VMEM] * 3, outs, scratch, 8,
+        (idx, got, mat, basis, near_term), [SMEM] + [VMEM] * 4, outs, scratch, 8,
     )
 
 

time: 51 us -> 50.7 us (level)
  no operation moved by 1% of the time
where the time goes in v5:
time: 50.7 us; the launch traced here: 50.3 us
  starting transfers between devices  17.8 us (35%)
  Pallas kernels  16.9 us (33%)
  waiting for transfers between devices  14.9 us (29%)
  between operations  0.71 us (1%)
    pallas_call x6, Pallas kernels, call(): pl.pallas_call(kernel, out_shape=tuple((s.memory_space(o.shape, o.dtype)...  16.9 us
    all_to_all x2, starting transfers between devices, exchange(): return lax.all_to_all(coef, 'grp', 0, 0, tiled=True)  14.7 us
    all_to_all x2, waiting for transfers between devices, exchange(): return lax.all_to_all(coef, 'grp', 0, 0, tiled=True)  10.9 us
    ppermute x2, waiting for transfers between devices, halo(): lax.ppermute(further, 'slab', between)  3.97 us
    ppermute x2, starting transfers between devices, halo(): lax.ppermute(further, 'slab', between)  2.93 us
  transfers between devices with their start and end apart: 6, of which 3 were waited for; matrix products, arithmetic and copies ran while one was open for 0% of the time, Pallas kernels for 26%

profile of v5, /device:TPU:32, one launch (start us, length us, event | category | flops | bytes accessed | tf_op | source)
XLA Modules:
  0.0 50.3 jit_solution(13806630623679716577)
XLA Ops:
  0.6 1.8 %collective-permute-start.1 = (bf16[16,3072]{1,0:T(8,128)(2,1)}, bf16[16,3072]{1,0:T(8,128)(2,1)S(1)}, u32[]{:S(2)}, u32[]{:S(2)}) collective-permute-start(bf16[16,3072]{1,0:T(8,128)(2,1)} %v_hbm.1), channel_id=1, source_target_pairs={{0,240},{16,32},{32,16},{48,64},{64,48},{80,96},{96,80},{112,128},... | collective-permute-start | bytes 294920 | tf_op jit(solution)/shard_map/ppermute | solution.py:544
  2.5 0.0 collective-permute-start
  2.5 2.3 %opening.1 = (bf16[128,256]{1,0:T(8,128)(2,1)S(1)}, bf16[128,256]{1,0:T(8,128)(2,1)S(1)}, bf16[512,256]{1,0:T(8,128)(2,1)S(1)}, bf16[16,64,128]{2,1,0:T(8,128)(2,1)}) custom-call(bf16[16,3072]{1,0:T(8,128)(2,1)} %v_hbm.1, bf16[16,6144]{1,0:T(8,128)(2,1)} %b_hbm.1), custom_call_target="tpu_custom_call" | custom-call | tf_op jit(solution)/shard_map/opening/pallas_call | solution.py:38
  4.8 11.2 %all-to-all-start = ((bf16[16,64,128]{2,1,0:T(8,128)(2,1)}), bf16[16,64,128]{2,1,0:T(8,128)(2,1)S(1)}, u32[]{:S(2)}, u32[]{:S(2)}) async-start(bf16[16,64,128]{2,1,0:T(8,128)(2,1)} %get-tuple-element.22), calls=%async_computation | async-start | bytes 524288 | tf_op jit(solution)/shard_map/all_to_all | solution.py:547
  16.0 0.0 collective-permute-done.1.further_ref
  16.0 0.0 collective-permute-done.chip_ref
  16.1 6.3 %first_near.1 = (f32[256,256]{1,0:T(8,128)S(1)}, bf16[512,1024]{1,0:T(8,128)(2,1)S(1)}, bf16[192,8192]{1,0:T(8,128)(2,1)}, s32[16,32]{1,0:T(8,128)S(4)}, s32[16,20]{1,0:T(8,128)S(4)}, /*index=5*/s32[16,20]{1,0:T(8,128)S(4)}) custom-call(s32[16]{0:T(128)} %count_hbm.1, s32[16,20]{1,0:T(8,128)} %src_hbm.1, s32[16,20]{1,0:T(8,128)} %type_hbm.1, ...), custom_call_target="tpu_custom_call" | custom-call | flops 10000000000 | bytes 100000000 | tf_op jit(solution)/shard_map/first_near/pallas_call | solution.py:38
  22.4 7.7 %all-to-all-done.got_ref = bf16[16,64,128]{2,1,0:T(8,128)(2,1)S(1)} async-done(((bf16[16,64,128]{2,1,0:T(8,128)(2,1)}), bf16[16,64,128]{2,1,0:T(8,128)(2,1)S(1)}, u32[]{:S(2)}, u32[]{:S(2)}) %all-to-all-start) | async-done | bytes 262176 | tf_op jit(solution)/shard_map/all_to_all | solution.py:547
  30.1 2.1 %far.1 = (bf16[128,256]{1,0:T(8,128)(2,1)S(1)}, bf16[128,256]{1,0:T(8,128)(2,1)S(1)}, bf16[128,256]{1,0:T(8,128)(2,1)S(1)}, bf16[128,256]{1,0:T(8,128)(2,1)S(1)}, bf16[16,64,128]{2,1,0:T(8,128)(2,1)}) custom-call(s32[16,32]{1,0:T(8,128)S(4)} %get-tuple-element.21.idx_s, bf16[16,64,128]{2,1,0:T(8,128)(2,1)S(1)} %all-to-all-done.got_ref, ...), custom_call_target="tpu_custom_call" | custom-call | tf_op jit(solution)/shard_map/far/pallas_call | solution.py:38
  32.2 3.5 %all-to-all-start.1 = ((bf16[16,64,128]{2,1,0:T(8,128)(2,1)}), bf16[16,64,128]{2,1,0:T(8,128)(2,1)S(1)}, u32[]{:S(2)}, u32[]{:S(2)}) async-start(bf16[16,64,128]{2,1,0:T(8,128)(2,1)} %get-tuple-element.30), calls=%async_computation.1 | async-start | bytes 524288 | tf_op jit(solution)/shard_map/all_to_all | solution.py:547
  35.7 0.1 collective-permute-start.2
  35.8 1.1 %collective-permute-start.3 = (bf16[128,256]{1,0:T(8,128)(2,1)S(1)}, bf16[128,256]{1,0:T(8,128)(2,1)S(1)}, u32[]{:S(2)}, u32[]{:S(2)}) collective-permute-start(bf16[128,256]{1,0:T(8,128)(2,1)S(1)} %get-tuple-element.34), channel_id=1, source_target_pairs={{0,240},{16,32},{32,16},{48,64},{64,48},{80,96},{96,80},{112,128},... | collective-permute-start | bytes 196616 | tf_op jit(solution)/shard_map/ppermute | solution.py:544
  36.9 1.9 %give.1 = (bf16[16,3072]{1,0:T(8,128)(2,1)}, bf16[192,8192]{1,0:T(8,128)(2,1)S(1)}) custom-call(bf16[128,256]{1,0:T(8,128)(2,1)S(1)} %get-tuple-element.26.lo_ref, bf16[128,256]{1,0:T(8,128)(2,1)S(1)} %get-tuple-element.27.hi_ref, bf16[192,8192]{1,0:T(8,128)(2,1)} %get-tuple-element.28.table_hbm), custom_call_target="tpu_custom_call" | custom-call | flops 1200000000 | bytes 12000000 | tf_op jit(solution)/shard_map/give/pallas_call | solution.py:38
  38.9 0.0 collective-permute-done.2.chip_ref
  38.9 4.0 %collective-permute-done.3.further_ref = bf16[128,256]{1,0:T(8,128)(2,1)S(1)} collective-permute-done((bf16[128,256]{1,0:T(8,128)(2,1)S(1)}, bf16[128,256]{1,0:T(8,128)(2,1)S(1)}, u32[]{:S(2)}, u32[]{:S(2)}) %collective-permute-start.3) | collective-permute-done | bytes 65568 | tf_op jit(solution)/shard_map/ppermute | solution.py:544
  42.8 2.3 %second_near.1.near_ref = f32[256,256]{1,0:T(8,128)S(1)} custom-call(s32[16,20]{1,0:T(8,128)S(4)} %get-tuple-element.31.at_s, s32[16,20]{1,0:T(8,128)S(4)} %get-tuple-element.32.kind_s, bf16[128,256]{1,0:T(8,128)(2,1)S(1)} %get-tuple-element.26.lo_ref, bf16[128,256]{1,0:T(8,128)(2,1)S(1)} %get-tuple-element.27.hi_ref, ...), custom_call_target="tpu_custom_call" | custom-call | flops 1200000000 | bytes 12000000 | tf_op jit(solution)/shard_map/second_near/pallas_call | solution.py:38
  45.1 3.2 %all-to-all-done.1.got_ref = bf16[16,64,128]{2,1,0:T(8,128)(2,1)S(1)} async-done(((bf16[16,64,128]{2,1,0:T(8,128)(2,1)}), bf16[16,64,128]{2,1,0:T(8,128)(2,1)S(1)}, u32[]{:S(2)}, u32[]{:S(2)}) %all-to-all-start.1) | async-done | bytes 262176 | tf_op jit(solution)/shard_map/all_to_all | solution.py:547
  48.3 2.0 %far_last.1 = bf16[16,3072]{1,0:T(8,128)(2,1)} custom-call(s32[16,32]{1,0:T(8,128)S(4)} %get-tuple-element.21.idx_s, bf16[16,64,128]{2,1,0:T(8,128)(2,1)S(1)} %all-to-all-done.1.got_ref, bf16[512,1024]{1,0:T(8,128)(2,1)S(1)} %get-tuple-element.23.mat_ref, bf16[512,256]{1,0:T(8,128)(2,1)S(1)} %get-tuple-element.24.basis_ref, f32[256,256]{1,0:T(8,128)S(1)} %second_near.1.near_ref), custom_call_target="tpu_custom_call" | custom-call | tf_op jit(solution)/shard_map/far_last/pallas_call | solution.py:38
Async XLA Ops:
  0.6 15.4 %collective-permute-start.1 = (bf16[16,3072]{1,0:T(8,128)(2,1)}, bf16[16,3072]{1,0:T(8,128)(2,1)S(1)}, u32[]{:S(2)}, u32[]{:S(2)}) collective-permute-start(bf16[16,3072]{1,0:T(8,128)(2,1)} %v_hbm.1), channel_id=1, source_target_pairs={{0,240},{16,32},{32,16},{48,64},{64,48},{80,96},{96,80},{112,128},... | collective-permute-start | bytes 294920 | tf_op jit(solution)/shard_map/ppermute | solution.py:544
  2.5 13.6 %collective-permute-start = (bf16[16,3072]{1,0:T(8,128)(2,1)}, bf16[16,3072]{1,0:T(8,128)(2,1)S(1)}, u32[]{:S(2)}, u32[]{:S(2)}) collective-permute-start(bf16[16,3072]{1,0:T(8,128)(2,1)} %v_hbm.1), channel_id=1, source_target_pairs={{0,16},{16,0},{32,48},{48,32},{64,80},{80,64},{96,112},{112,96},{1... | collective-permute-start | bytes 294920 | tf_op jit(solution)/shard_map/ppermute | solution.py:544
  4.8 25.3 %all-to-all-start = ((bf16[16,64,128]{2,1,0:T(8,128)(2,1)}), bf16[16,64,128]{2,1,0:T(8,128)(2,1)S(1)}, u32[]{:S(2)}, u32[]{:S(2)}) async-start(bf16[16,64,128]{2,1,0:T(8,128)(2,1)} %get-tuple-element.22), calls=%async_computation | async-start | bytes 524288 | tf_op jit(solution)/shard_map/all_to_all | solution.py:547
  32.2 16.2 %all-to-all-start.1 = ((bf16[16,64,128]{2,1,0:T(8,128)(2,1)}), bf16[16,64,128]{2,1,0:T(8,128)(2,1)S(1)}, u32[]{:S(2)}, u32[]{:S(2)}) async-start(bf16[16,64,128]{2,1,0:T(8,128)(2,1)} %get-tuple-element.30), calls=%async_computation.1 | async-start | bytes 524288 | tf_op jit(solution)/shard_map/all_to_all | solution.py:547
  35.7 3.2 %collective-permute-start.2 = (bf16[128,256]{1,0:T(8,128)(2,1)S(1)}, bf16[128,256]{1,0:T(8,128)(2,1)S(1)}, u32[]{:S(2)}, u32[]{:S(2)}) collective-permute-start(bf16[128,256]{1,0:T(8,128)(2,1)S(1)} %get-tuple-element.33), channel_id=1, source_target_pairs={{0,16},{16,0},{32,48},{48,32},{64,80},{80,64},{96,112},{112,96},{1... | collective-permute-start | bytes 196616 | tf_op jit(solution)/shard_map/ppermute | solution.py:544
  35.8 7.0 %collective-permute-start.3 = (bf16[128,256]{1,0:T(8,128)(2,1)S(1)}, bf16[128,256]{1,0:T(8,128)(2,1)S(1)}, u32[]{:S(2)}, u32[]{:S(2)}) collective-permute-start(bf16[128,256]{1,0:T(8,128)(2,1)S(1)} %get-tuple-element.34), channel_id=1, source_target_pairs={{0,240},{16,32},{32,16},{48,64},{64,48},{80,96},{96,80},{112,128},... | collective-permute-start | bytes 196616 | tf_op jit(solution)/shard_map/ppermute | solution.py:544

commit v6 on v5

--- a/solution.py
+++ b/solution.py
@@ -354,7 +354,7 @@
 
 
 def second_near_kernel(
-    at_s, kind_s, lo_ref, hi_ref, chip_ref, further_ref, table_ref, near_ref, e_s, p_s
+    at_s, kind_s, lo_ref, hi_ref, further_ref, chip_ref, table_ref, near_ref, e_s, p_s
 ):
     rim, columns = RIM * RHS, table_ref.shape[1]
     for j, ref in enumerate((lo_ref, hi_ref, chip_ref, further_ref)):
@@ -506,7 +506,7 @@
 def second_near(at, kind, lo, hi, chip, further, table):
     rows = 2 * lo.shape[0]
     return call(
-        second_near_kernel, "second_near", (at, kind, lo, hi, chip, further, table),
+        second_near_kernel, "second_near", (at, kind, lo, hi, further, chip, table),
         [SMEM] * 2 + [VMEM] * 4 + [KEPT],
         [(shape((rows, WIDE), F32), VMEM)],
         [

time: 50.7 us -> 50.7 us (level)
  starting transfers between devices: 17.8 us -> 16.8 us
  waiting for transfers between devices: 14.9 us -> 15.9 us
    ppermute x2, starting transfers between devices: 2.93 us -> 1.92 us  [halo(): lax.ppermute(further, 'slab', between)]
    ppermute x2, waiting for transfers between devices: 3.97 us -> 4.86 us  [halo(): lax.ppermute(further, 'slab', between)]
where the time goes in v6:
time: 50.7 us; the launch traced here: 50.3 us
  Pallas kernels  16.9 us (33%)
  starting transfers between devices  16.8 us (33%)
  waiting for transfers between devices  15.9 us (31%)
  between operations  0.71 us (1%)
    pallas_call x6, Pallas kernels, call(): pl.pallas_call(kernel, out_shape=tuple((s.memory_space(o.shape, o.dtype)...  16.9 us
    all_to_all x2, starting transfers between devices, exchange(): return lax.all_to_all(coef, 'grp', 0, 0, tiled=True)  14.7 us
    all_to_all x2, waiting for transfers between devices, exchange(): return lax.all_to_all(coef, 'grp', 0, 0, tiled=True)  11 us
    ppermute x2, waiting for transfers between devices, halo(): lax.ppermute(further, 'slab', between)  4.86 us
    ppermute x2, starting transfers between devices, halo(): lax.ppermute(further, 'slab', between)  1.92 us
  transfers between devices with their start and end apart: 6, of which 3 were waited for; matrix products, arithmetic and copies ran while one was open for 0% of the time, Pallas kernels for 26%

profile of v6, /device:TPU:32, one launch (start us, length us, event | category | flops | bytes accessed | tf_op | source)
XLA Modules:
  0.0 50.3 jit_solution(2200508620434660215)
XLA Ops:
  0.6 1.8 %collective-permute-start.1 = (bf16[16,3072]{1,0:T(8,128)(2,1)}, bf16[16,3072]{1,0:T(8,128)(2,1)S(1)}, u32[]{:S(2)}, u32[]{:S(2)}) collective-permute-start(bf16[16,3072]{1,0:T(8,128)(2,1)} %v_hbm.1), channel_id=1, source_target_pairs={{0,240},{16,32},{32,16},{48,64},{64,48},{80,96},{96,80},{112,128},... | collective-permute-start | bytes 294920 | tf_op jit(solution)/shard_map/ppermute | solution.py:544
  2.5 0.0 collective-permute-start
  2.5 2.3 %opening.1 = (bf16[128,256]{1,0:T(8,128)(2,1)S(1)}, bf16[128,256]{1,0:T(8,128)(2,1)S(1)}, bf16[512,256]{1,0:T(8,128)(2,1)S(1)}, bf16[16,64,128]{2,1,0:T(8,128)(2,1)}) custom-call(bf16[16,3072]{1,0:T(8,128)(2,1)} %v_hbm.1, bf16[16,6144]{1,0:T(8,128)(2,1)} %b_hbm.1), custom_call_target="tpu_custom_call" | custom-call | tf_op jit(solution)/shard_map/opening/pallas_call | solution.py:38
  4.8 11.2 %all-to-all-start = ((bf16[16,64,128]{2,1,0:T(8,128)(2,1)}), bf16[16,64,128]{2,1,0:T(8,128)(2,1)S(1)}, u32[]{:S(2)}, u32[]{:S(2)}) async-start(bf16[16,64,128]{2,1,0:T(8,128)(2,1)} %get-tuple-element.22), calls=%async_computation | async-start | bytes 524288 | tf_op jit(solution)/shard_map/all_to_all | solution.py:547
  16.0 0.0 collective-permute-done.1.further_ref
  16.0 0.0 collective-permute-done.chip_ref
  16.1 6.3 %first_near.1 = (f32[256,256]{1,0:T(8,128)S(1)}, bf16[512,1024]{1,0:T(8,128)(2,1)S(1)}, bf16[192,8192]{1,0:T(8,128)(2,1)}, s32[16,32]{1,0:T(8,128)S(4)}, s32[16,20]{1,0:T(8,128)S(4)}, /*index=5*/s32[16,20]{1,0:T(8,128)S(4)}) custom-call(s32[16]{0:T(128)} %count_hbm.1, s32[16,20]{1,0:T(8,128)} %src_hbm.1, s32[16,20]{1,0:T(8,128)} %type_hbm.1, ...), custom_call_target="tpu_custom_call" | custom-call | flops 10000000000 | bytes 100000000 | tf_op jit(solution)/shard_map/first_near/pallas_call | solution.py:38
  22.4 7.7 %all-to-all-done.got_ref = bf16[16,64,128]{2,1,0:T(8,128)(2,1)S(1)} async-done(((bf16[16,64,128]{2,1,0:T(8,128)(2,1)}), bf16[16,64,128]{2,1,0:T(8,128)(2,1)S(1)}, u32[]{:S(2)}, u32[]{:S(2)}) %all-to-all-start) | async-done | bytes 262176 | tf_op jit(solution)/shard_map/all_to_all | solution.py:547
  30.1 2.1 %far.1 = (bf16[128,256]{1,0:T(8,128)(2,1)S(1)}, bf16[128,256]{1,0:T(8,128)(2,1)S(1)}, bf16[128,256]{1,0:T(8,128)(2,1)S(1)}, bf16[128,256]{1,0:T(8,128)(2,1)S(1)}, bf16[16,64,128]{2,1,0:T(8,128)(2,1)}) custom-call(s32[16,32]{1,0:T(8,128)S(4)} %get-tuple-element.21.idx_s, bf16[16,64,128]{2,1,0:T(8,128)(2,1)S(1)} %all-to-all-done.got_ref, ...), custom_call_target="tpu_custom_call" | custom-call | tf_op jit(solution)/shard_map/far/pallas_call | solution.py:38
  32.2 3.5 %all-to-all-start.1 = ((bf16[16,64,128]{2,1,0:T(8,128)(2,1)}), bf16[16,64,128]{2,1,0:T(8,128)(2,1)S(1)}, u32[]{:S(2)}, u32[]{:S(2)}) async-start(bf16[16,64,128]{2,1,0:T(8,128)(2,1)} %get-tuple-element.30), calls=%async_computation.1 | async-start | bytes 524288 | tf_op jit(solution)/shard_map/all_to_all | solution.py:547
  35.7 0.1 collective-permute-start.2
  35.8 0.1 collective-permute-start.3
  35.9 1.9 %give.1 = (bf16[16,3072]{1,0:T(8,128)(2,1)}, bf16[192,8192]{1,0:T(8,128)(2,1)S(1)}) custom-call(bf16[128,256]{1,0:T(8,128)(2,1)S(1)} %get-tuple-element.26.lo_ref, bf16[128,256]{1,0:T(8,128)(2,1)S(1)} %get-tuple-element.27.hi_ref, bf16[192,8192]{1,0:T(8,128)(2,1)} %get-tuple-element.28.table_hbm), custom_call_target="tpu_custom_call" | custom-call | flops 1200000000 | bytes 12000000 | tf_op jit(solution)/shard_map/give/pallas_call | solution.py:38
  37.9 4.9 %collective-permute-done.2.further_ref = bf16[128,256]{1,0:T(8,128)(2,1)S(1)} collective-permute-done((bf16[128,256]{1,0:T(8,128)(2,1)S(1)}, bf16[128,256]{1,0:T(8,128)(2,1)S(1)}, u32[]{:S(2)}, u32[]{:S(2)}) %collective-permute-start.2) | collective-permute-done | bytes 65568 | tf_op jit(solution)/shard_map/ppermute | solution.py:544
  42.7 0.0 collective-permute-done.3.chip_ref
  42.7 2.3 %second_near.1.near_ref = f32[256,256]{1,0:T(8,128)S(1)} custom-call(s32[16,20]{1,0:T(8,128)S(4)} %get-tuple-element.31.at_s, s32[16,20]{1,0:T(8,128)S(4)} %get-tuple-element.32.kind_s, bf16[128,256]{1,0:T(8,128)(2,1)S(1)} %get-tuple-element.26.lo_ref, bf16[128,256]{1,0:T(8,128)(2,1)S(1)} %get-tuple-element.27.hi_ref, ...), custom_call_target="tpu_custom_call" | custom-call | flops 1200000000 | bytes 12000000 | tf_op jit(solution)/shard_map/second_near/pallas_call | solution.py:38
  45.0 3.3 %all-to-all-done.1.got_ref = bf16[16,64,128]{2,1,0:T(8,128)(2,1)S(1)} async-done(((bf16[16,64,128]{2,1,0:T(8,128)(2,1)}), bf16[16,64,128]{2,1,0:T(8,128)(2,1)S(1)}, u32[]{:S(2)}, u32[]{:S(2)}) %all-to-all-start.1) | async-done | bytes 262176 | tf_op jit(solution)/shard_map/all_to_all | solution.py:547
  48.3 2.0 %far_last.1 = bf16[16,3072]{1,0:T(8,128)(2,1)} custom-call(s32[16,32]{1,0:T(8,128)S(4)} %get-tuple-element.21.idx_s, bf16[16,64,128]{2,1,0:T(8,128)(2,1)S(1)} %all-to-all-done.1.got_ref, bf16[512,1024]{1,0:T(8,128)(2,1)S(1)} %get-tuple-element.23.mat_ref, bf16[512,256]{1,0:T(8,128)(2,1)S(1)} %get-tuple-element.24.basis_ref, f32[256,256]{1,0:T(8,128)S(1)} %second_near.1.near_ref), custom_call_target="tpu_custom_call" | custom-call | tf_op jit(solution)/shard_map/far_last/pallas_call | solution.py:38
Async XLA Ops:
  0.6 15.4 %collective-permute-start.1 = (bf16[16,3072]{1,0:T(8,128)(2,1)}, bf16[16,3072]{1,0:T(8,128)(2,1)S(1)}, u32[]{:S(2)}, u32[]{:S(2)}) collective-permute-start(bf16[16,3072]{1,0:T(8,128)(2,1)} %v_hbm.1), channel_id=1, source_target_pairs={{0,240},{16,32},{32,16},{48,64},{64,48},{80,96},{96,80},{112,128},... | collective-permute-start | bytes 294920 | tf_op jit(solution)/shard_map/ppermute | solution.py:544
  2.5 13.6 %collective-permute-start = (bf16[16,3072]{1,0:T(8,128)(2,1)}, bf16[16,3072]{1,0:T(8,128)(2,1)S(1)}, u32[]{:S(2)}, u32[]{:S(2)}) collective-permute-start(bf16[16,3072]{1,0:T(8,128)(2,1)} %v_hbm.1), channel_id=1, source_target_pairs={{0,16},{16,0},{32,48},{48,32},{64,80},{80,64},{96,112},{112,96},{1... | collective-permute-start | bytes 294920 | tf_op jit(solution)/shard_map/ppermute | solution.py:544
  4.8 25.3 %all-to-all-start = ((bf16[16,64,128]{2,1,0:T(8,128)(2,1)}), bf16[16,64,128]{2,1,0:T(8,128)(2,1)S(1)}, u32[]{:S(2)}, u32[]{:S(2)}) async-start(bf16[16,64,128]{2,1,0:T(8,128)(2,1)} %get-tuple-element.22), calls=%async_computation | async-start | bytes 524288 | tf_op jit(solution)/shard_map/all_to_all | solution.py:547
  32.2 16.2 %all-to-all-start.1 = ((bf16[16,64,128]{2,1,0:T(8,128)(2,1)}), bf16[16,64,128]{2,1,0:T(8,128)(2,1)S(1)}, u32[]{:S(2)}, u32[]{:S(2)}) async-start(bf16[16,64,128]{2,1,0:T(8,128)(2,1)} %get-tuple-element.30), calls=%async_computation.1 | async-start | bytes 524288 | tf_op jit(solution)/shard_map/all_to_all | solution.py:547
  35.7 7.0 %collective-permute-start.2 = (bf16[128,256]{1,0:T(8,128)(2,1)S(1)}, bf16[128,256]{1,0:T(8,128)(2,1)S(1)}, u32[]{:S(2)}, u32[]{:S(2)}) collective-permute-start(bf16[128,256]{1,0:T(8,128)(2,1)S(1)} %get-tuple-element.33), channel_id=1, source_target_pairs={{0,240},{16,32},{32,16},{48,64},{64,48},{80,96},{96,80},{112,128},... | collective-permute-start | bytes 196616 | tf_op jit(solution)/shard_map/ppermute | solution.py:544
  35.8 6.9 %collective-permute-start.3 = (bf16[128,256]{1,0:T(8,128)(2,1)S(1)}, bf16[128,256]{1,0:T(8,128)(2,1)S(1)}, u32[]{:S(2)}, u32[]{:S(2)}) collective-permute-start(bf16[128,256]{1,0:T(8,128)(2,1)S(1)} %get-tuple-element.34), channel_id=1, source_target_pairs={{0,16},{16,0},{32,48},{48,32},{64,80},{80,64},{96,112},{112,96},{1... | collective-permute-start | bytes 196616 | tf_op jit(solution)/shard_map/ppermute | solution.py:544

commit v7 on v6

--- a/solution.py
+++ b/solution.py
@@ -15,7 +15,7 @@
 WIDE = 256
 GROUP = 8
 LONG = 100_000_000
-STEPS = 2
+STEPS = 1
 SIDE = LANES // RANK
 
 VMEM = pl.BlockSpec(memory_space=pltpu.VMEM)

time: 50.7 us -> 50.7 us (level)
  transfers between devices with their start and end apart: 6 -> 6, of which waited for: 3 -> 3; matrix products, arithmetic and copies ran while one was open for 0% -> 0% of each run, Pallas kernels for 26% -> 25%
where the time goes in v7:
time: 50.7 us; the launch traced here: 50.3 us
  starting transfers between devices  16.8 us (33%)
  Pallas kernels  16.8 us (33%)
  waiting for transfers between devices  16.1 us (32%)
  between operations  0.71 us (1%)
    pallas_call x6, Pallas kernels, call(): pl.pallas_call(kernel, out_shape=tuple((s.memory_space(o.shape, o.dtype)...  16.8 us
    all_to_all x2, starting transfers between devices, exchange(): return lax.all_to_all(coef, 'grp', 0, 0, tiled=True)  14.7 us
    all_to_all x2, waiting for transfers between devices, exchange(): return lax.all_to_all(coef, 'grp', 0, 0, tiled=True)  11.2 us
    ppermute x2, waiting for transfers between devices, halo(): lax.ppermute(further, 'slab', between)  4.86 us
    ppermute x2, starting transfers between devices, halo(): lax.ppermute(further, 'slab', between)  1.92 us
  transfers between devices with their start and end apart: 6, of which 3 were waited for; matrix products, arithmetic and copies ran while one was open for 0% of the time, Pallas kernels for 25%

profile of v7, /device:TPU:32, one launch (start us, length us, event | category | flops | bytes accessed | tf_op | source)
XLA Modules:
  0.0 50.3 jit_solution(8698903089417992386)
XLA Ops:
  0.6 1.8 %collective-permute-start.1 = (bf16[16,3072]{1,0:T(8,128)(2,1)}, bf16[16,3072]{1,0:T(8,128)(2,1)S(1)}, u32[]{:S(2)}, u32[]{:S(2)}) collective-permute-start(bf16[16,3072]{1,0:T(8,128)(2,1)} %v_hbm.1), channel_id=1, source_target_pairs={{0,240},{16,32},{32,16},{48,64},{64,48},{80,96},{96,80},{112,128},... | collective-permute-start | bytes 294920 | tf_op jit(solution)/shard_map/ppermute | solution.py:544
  2.5 0.0 collective-permute-start
  2.5 2.3 %opening.1 = (bf16[128,256]{1,0:T(8,128)(2,1)S(1)}, bf16[128,256]{1,0:T(8,128)(2,1)S(1)}, bf16[512,256]{1,0:T(8,128)(2,1)S(1)}, bf16[16,64,128]{2,1,0:T(8,128)(2,1)}) custom-call(bf16[16,3072]{1,0:T(8,128)(2,1)} %v_hbm.1, bf16[16,6144]{1,0:T(8,128)(2,1)} %b_hbm.1), custom_call_target="tpu_custom_call" | custom-call | tf_op jit(solution)/shard_map/opening/pallas_call | solution.py:38
  4.8 11.2 %all-to-all-start = ((bf16[16,64,128]{2,1,0:T(8,128)(2,1)}), bf16[16,64,128]{2,1,0:T(8,128)(2,1)S(1)}, u32[]{:S(2)}, u32[]{:S(2)}) async-start(bf16[16,64,128]{2,1,0:T(8,128)(2,1)} %get-tuple-element.22), calls=%async_computation | async-start | bytes 524288 | tf_op jit(solution)/shard_map/all_to_all | solution.py:547
  16.0 0.0 collective-permute-done.1.further_ref
  16.0 0.0 collective-permute-done.chip_ref
  16.1 6.1 %first_near.1 = (f32[256,256]{1,0:T(8,128)S(1)}, bf16[512,1024]{1,0:T(8,128)(2,1)S(1)}, bf16[192,8192]{1,0:T(8,128)(2,1)}, s32[16,32]{1,0:T(8,128)S(4)}, s32[16,20]{1,0:T(8,128)S(4)}, /*index=5*/s32[16,20]{1,0:T(8,128)S(4)}) custom-call(s32[16]{0:T(128)} %count_hbm.1, s32[16,20]{1,0:T(8,128)} %src_hbm.1, s32[16,20]{1,0:T(8,128)} %type_hbm.1, ...), custom_call_target="tpu_custom_call" | custom-call | flops 10000000000 | bytes 100000000 | tf_op jit(solution)/shard_map/first_near/pallas_call | solution.py:38
  22.2 7.9 %all-to-all-done.got_ref = bf16[16,64,128]{2,1,0:T(8,128)(2,1)S(1)} async-done(((bf16[16,64,128]{2,1,0:T(8,128)(2,1)}), bf16[16,64,128]{2,1,0:T(8,128)(2,1)S(1)}, u32[]{:S(2)}, u32[]{:S(2)}) %all-to-all-start) | async-done | bytes 262176 | tf_op jit(solution)/shard_map/all_to_all | solution.py:547
  30.1 2.1 %far.1 = (bf16[128,256]{1,0:T(8,128)(2,1)S(1)}, bf16[128,256]{1,0:T(8,128)(2,1)S(1)}, bf16[128,256]{1,0:T(8,128)(2,1)S(1)}, bf16[128,256]{1,0:T(8,128)(2,1)S(1)}, bf16[16,64,128]{2,1,0:T(8,128)(2,1)}) custom-call(s32[16,32]{1,0:T(8,128)S(4)} %get-tuple-element.21.idx_s, bf16[16,64,128]{2,1,0:T(8,128)(2,1)S(1)} %all-to-all-done.got_ref, ...), custom_call_target="tpu_custom_call" | custom-call | tf_op jit(solution)/shard_map/far/pallas_call | solution.py:38
  32.2 3.5 %all-to-all-start.1 = ((bf16[16,64,128]{2,1,0:T(8,128)(2,1)}), bf16[16,64,128]{2,1,0:T(8,128)(2,1)S(1)}, u32[]{:S(2)}, u32[]{:S(2)}) async-start(bf16[16,64,128]{2,1,0:T(8,128)(2,1)} %get-tuple-element.30), calls=%async_computation.1 | async-start | bytes 524288 | tf_op jit(solution)/shard_map/all_to_all | solution.py:547
  35.7 0.1 collective-permute-start.2
  35.8 0.1 collective-permute-start.3
  35.9 1.9 %give.1 = (bf16[16,3072]{1,0:T(8,128)(2,1)}, bf16[192,8192]{1,0:T(8,128)(2,1)S(1)}) custom-call(bf16[128,256]{1,0:T(8,128)(2,1)S(1)} %get-tuple-element.26.lo_ref, bf16[128,256]{1,0:T(8,128)(2,1)S(1)} %get-tuple-element.27.hi_ref, bf16[192,8192]{1,0:T(8,128)(2,1)} %get-tuple-element.28.table_hbm), custom_call_target="tpu_custom_call" | custom-call | flops 1200000000 | bytes 12000000 | tf_op jit(solution)/shard_map/give/pallas_call | solution.py:38
  37.9 4.9 %collective-permute-done.2.further_ref = bf16[128,256]{1,0:T(8,128)(2,1)S(1)} collective-permute-done((bf16[128,256]{1,0:T(8,128)(2,1)S(1)}, bf16[128,256]{1,0:T(8,128)(2,1)S(1)}, u32[]{:S(2)}, u32[]{:S(2)}) %collective-permute-start.2) | collective-permute-done | bytes 65568 | tf_op jit(solution)/shard_map/ppermute | solution.py:544
  42.7 0.0 collective-permute-done.3.chip_ref
  42.7 2.3 %second_near.1.near_ref = f32[256,256]{1,0:T(8,128)S(1)} custom-call(s32[16,20]{1,0:T(8,128)S(4)} %get-tuple-element.31.at_s, s32[16,20]{1,0:T(8,128)S(4)} %get-tuple-element.32.kind_s, bf16[128,256]{1,0:T(8,128)(2,1)S(1)} %get-tuple-element.26.lo_ref, bf16[128,256]{1,0:T(8,128)(2,1)S(1)} %get-tuple-element.27.hi_ref, ...), custom_call_target="tpu_custom_call" | custom-call | flops 1200000000 | bytes 12000000 | tf_op jit(solution)/shard_map/second_near/pallas_call | solution.py:38
  45.0 3.3 %all-to-all-done.1.got_ref = bf16[16,64,128]{2,1,0:T(8,128)(2,1)S(1)} async-done(((bf16[16,64,128]{2,1,0:T(8,128)(2,1)}), bf16[16,64,128]{2,1,0:T(8,128)(2,1)S(1)}, u32[]{:S(2)}, u32[]{:S(2)}) %all-to-all-start.1) | async-done | bytes 262176 | tf_op jit(solution)/shard_map/all_to_all | solution.py:547
  48.3 2.0 %far_last.1 = bf16[16,3072]{1,0:T(8,128)(2,1)} custom-call(s32[16,32]{1,0:T(8,128)S(4)} %get-tuple-element.21.idx_s, bf16[16,64,128]{2,1,0:T(8,128)(2,1)S(1)} %all-to-all-done.1.got_ref, bf16[512,1024]{1,0:T(8,128)(2,1)S(1)} %get-tuple-element.23.mat_ref, bf16[512,256]{1,0:T(8,128)(2,1)S(1)} %get-tuple-element.24.basis_ref, f32[256,256]{1,0:T(8,128)S(1)} %second_near.1.near_ref), custom_call_target="tpu_custom_call" | custom-call | tf_op jit(solution)/shard_map/far_last/pallas_call | solution.py:38
Async XLA Ops:
  0.6 15.4 %collective-permute-start.1 = (bf16[16,3072]{1,0:T(8,128)(2,1)}, bf16[16,3072]{1,0:T(8,128)(2,1)S(1)}, u32[]{:S(2)}, u32[]{:S(2)}) collective-permute-start(bf16[16,3072]{1,0:T(8,128)(2,1)} %v_hbm.1), channel_id=1, source_target_pairs={{0,240},{16,32},{32,16},{48,64},{64,48},{80,96},{96,80},{112,128},... | collective-permute-start | bytes 294920 | tf_op jit(solution)/shard_map/ppermute | solution.py:544
  2.5 13.6 %collective-permute-start = (bf16[16,3072]{1,0:T(8,128)(2,1)}, bf16[16,3072]{1,0:T(8,128)(2,1)S(1)}, u32[]{:S(2)}, u32[]{:S(2)}) collective-permute-start(bf16[16,3072]{1,0:T(8,128)(2,1)} %v_hbm.1), channel_id=1, source_target_pairs={{0,16},{16,0},{32,48},{48,32},{64,80},{80,64},{96,112},{112,96},{1... | collective-permute-start | bytes 294920 | tf_op jit(solution)/shard_map/ppermute | solution.py:544
  4.8 25.3 %all-to-all-start = ((bf16[16,64,128]{2,1,0:T(8,128)(2,1)}), bf16[16,64,128]{2,1,0:T(8,128)(2,1)S(1)}, u32[]{:S(2)}, u32[]{:S(2)}) async-start(bf16[16,64,128]{2,1,0:T(8,128)(2,1)} %get-tuple-element.22), calls=%async_computation | async-start | bytes 524288 | tf_op jit(solution)/shard_map/all_to_all | solution.py:547
  32.2 16.2 %all-to-all-start.1 = ((bf16[16,64,128]{2,1,0:T(8,128)(2,1)}), bf16[16,64,128]{2,1,0:T(8,128)(2,1)S(1)}, u32[]{:S(2)}, u32[]{:S(2)}) async-start(bf16[16,64,128]{2,1,0:T(8,128)(2,1)} %get-tuple-element.30), calls=%async_computation.1 | async-start | bytes 524288 | tf_op jit(solution)/shard_map/all_to_all | solution.py:547
  35.7 7.0 %collective-permute-start.2 = (bf16[128,256]{1,0:T(8,128)(2,1)S(1)}, bf16[128,256]{1,0:T(8,128)(2,1)S(1)}, u32[]{:S(2)}, u32[]{:S(2)}) collective-permute-start(bf16[128,256]{1,0:T(8,128)(2,1)S(1)} %get-tuple-element.33), channel_id=1, source_target_pairs={{0,240},{16,32},{32,16},{48,64},{64,48},{80,96},{96,80},{112,128},... | collective-permute-start | bytes 196616 | tf_op jit(solution)/shard_map/ppermute | solution.py:544
  35.8 6.9 %collective-permute-start.3 = (bf16[128,256]{1,0:T(8,128)(2,1)S(1)}, bf16[128,256]{1,0:T(8,128)(2,1)S(1)}, u32[]{:S(2)}, u32[]{:S(2)}) collective-permute-start(bf16[128,256]{1,0:T(8,128)(2,1)S(1)} %get-tuple-element.34), channel_id=1, source_target_pairs={{0,16},{16,0},{32,48},{48,32},{64,80},{80,64},{96,112},{112,96},{1... | collective-permute-start | bytes 196616 | tf_op jit(solution)/shard_map/ppermute | solution.py:544
